TPU v7x, 32 devices: a whole 2x2x4 slice. The times are simulated.
32 devices in a mesh: dp: 16 (over z, y, x), mp: 2 (over core).
Axes of the slice: x: 2, y: 2, z: 4, core: 2. Of those that a mesh axis runs over, the one named last changes fastest.
Arguments:
- spectrogram: bfloat16 [64, 1024, 128], P(('dp', 'mp')), may hold values from -6 to 6
- keep: int32 [64, 154], P(('dp', 'mp')), may hold values from 0 to 511, as said below
- counts: int32 [64], P(('dp', 'mp')), may hold values from 51 to 154, as said below
- enc_qkv: float32 [768, 2304], P('dp'), may hold values from -0.21875 to 0.21875
- enc_out: float32 [768, 768], P('dp'), may hold values from -1.75 to 1.75
- enc_up: float32 [768, 3072], P('dp'), may hold values from -0.21875 to 0.21875
- enc_down: float32 [3072, 768], P('dp'), may hold values from -0.109375 to 0.109375
- dec_qkv: float32 [512, 1536], P('dp'), may hold values from -0.25 to 0.25
- dec_out: float32 [512, 512], P('dp'), may hold values from -1 to 1
- dec_up: float32 [512, 2048], P('dp'), may hold values from -0.25 to 0.25
- dec_down: float32 [2048, 512], P('dp'), may hold values from -0.125 to 0.125
- mom_enc_qkv: float32 [768, 2304], P('dp'), may hold values from -4.7683716e-06 to 4.7683716e-06
- mom_enc_out: float32 [768, 768], P('dp'), may hold values from -4.7683716e-06 to 4.7683716e-06
- mom_enc_up: float32 [768, 3072], P('dp'), may hold values from -4.7683716e-06 to 4.7683716e-06
- mom_enc_down: float32 [3072, 768], P('dp'), may hold values from -4.7683716e-06 to 4.7683716e-06
- mom_dec_qkv: float32 [512, 1536], P('dp'), may hold values from -4.7683716e-06 to 4.7683716e-06
- mom_dec_out: float32 [512, 512], P('dp'), may hold values from -4.7683716e-06 to 4.7683716e-06
- mom_dec_up: float32 [512, 2048], P('dp'), may hold values from -4.7683716e-06 to 4.7683716e-06
- mom_dec_down: float32 [2048, 512], P('dp'), may hold values from -4.7683716e-06 to 4.7683716e-06
- patch_maps: float32 [256, 1280], P('dp'), may hold values from -0.375 to 0.375
- patch_first: float32 [256, 1280], P('dp'), may hold values from -4.7683716e-06 to 4.7683716e-06
- patch_second: float32 [256, 1280], P('dp'), may hold values from 4.5601797e-15 to 1.8240719e-14
- embed_map: float32 [768, 512], P('dp'), may hold values from -0.21875 to 0.21875
- embed_first: float32 [768, 512], P('dp'), may hold values from -4.7683716e-06 to 4.7683716e-06
- embed_second: float32 [768, 512], P('dp'), may hold values from 4.5601797e-15 to 1.8240719e-14
- vectors: float32 [19968], P('dp'), may hold values from -4 to 4
- vector_first: float32 [19968], P('dp'), may hold values from -2.2888184e-05 to 2.2888184e-05
- vector_second: float32 [19968], P('dp'), may hold values from 1.1856468e-13 to 4.56018e-13
Outputs:
- loss_sum: float32 [], replicated
- mask_count: float32 [], replicated
- grad_norm: float32 [], replicated
- new_enc_qkv: float32 [768, 2304], P('dp')
- new_enc_out: float32 [768, 768], P('dp')
- new_enc_up: float32 [768, 3072], P('dp')
- new_enc_down: float32 [3072, 768], P('dp')
- new_dec_qkv: float32 [512, 1536], P('dp')
- new_dec_out: float32 [512, 512], P('dp')
- new_dec_up: float32 [512, 2048], P('dp')
- new_dec_down: float32 [2048, 512], P('dp')
- new_mom_enc_qkv: float32 [768, 2304], P('dp')
- new_mom_enc_out: float32 [768, 768], P('dp')
- new_mom_enc_up: float32 [768, 3072], P('dp')
- new_mom_enc_down: float32 [3072, 768], P('dp')
- new_mom_dec_qkv: float32 [512, 1536], P('dp')
- new_mom_dec_out: float32 [512, 512], P('dp')
- new_mom_dec_up: float32 [512, 2048], P('dp')
- new_mom_dec_down: float32 [2048, 512], P('dp')
- new_patch_maps: float32 [256, 1280], P('dp')
- new_patch_first: float32 [256, 1280], P('dp')
- new_patch_second: float32 [256, 1280], P('dp')
- new_embed_map: float32 [768, 512], P('dp')
- new_embed_first: float32 [768, 512], P('dp')
- new_embed_second: float32 [768, 512], P('dp')
- new_vectors: float32 [19968], P('dp')
- new_vector_first: float32 [19968], P('dp')
- new_vector_second: float32 [19968], P('dp')
Inputs may be any that keep to these rules, and one draw needn't show every extreme that they name: `keep`: in each row the 154 entries are distinct patch numbers; only the first counts entries of a clip are visible. `counts`: some clip has exactly 154 visible patches in every draw.
All inputs are finite; a program needn't handle non-finite values.
Results may differ from a plain program's by a relative error of at most 0.011.
Values may be sent and summed in bfloat16 or wider, within the bound.
A program may use at most 256 MiB of HBM per device.

v0:
```python
from functools import partial
import functools
import math

import jax
import jax.numpy as jnp
from jax import lax
from jax.sharding import PartitionSpec as P

D = 768
HEADS = 12
HEAD = 64
MLP = 3072
DD = 512
DHEADS = 16
DHEAD = 32
DMLP = 2048
PS = 16
GT = 64
GF = 8
WIN = 4
VIS = 154
NS_ITERS = 5
STEP = 10
PATCH = 256
SHIFT = 2
NPATCH = 512


HIGH = lax.Precision.HIGHEST
CLIP_MAX = 0.001
LR_MUON = 0.1
LR_ADAM = 0.05
DECAY = 0.01
NS_A = 3.4445
NS_B = -4.775
NS_C = 2.0315
LONG_COLS = (True, True, True, False, True, True, True, False)


def shortened(x):
    return jax.tree.map(lambda a: a.astype(jnp.bfloat16) if a.dtype == jnp.float32 else a, x)


def narrow_core(value):
    return lax.optimization_barrier(value.astype(jnp.bfloat16)).astype(jnp.float32)


def narrow_keep(value):
    return (narrow_core(value), None)


def narrow_pass(kept, grad):
    return (grad,)


def same_core(value):
    return value


def same_keep(value):
    return (value, None)


def same_back(kept, grad):
    return (narrow_core(grad),)


def narrow(value):
    wrapped = jax.custom_vjp(narrow_core)
    wrapped.defvjp(narrow_keep, narrow_pass)
    return wrapped(value)


def narrow_grad(value):
    wrapped = jax.custom_vjp(same_core)
    wrapped.defvjp(same_keep, same_back)
    return wrapped(value)


def product(inputs, matrix):
    return narrow_grad(jnp.dot(narrow(inputs), narrow(matrix), preferred_element_type=jnp.float32))


def score_product(queries, key_rows):
    return narrow_grad(
        jnp.einsum(
            "bqhd,bkhd->bhqk", narrow(queries), narrow(key_rows), preferred_element_type=jnp.float32
        )
    )


def value_product(softmax_rows, values):
    return narrow_grad(
        jnp.einsum(
            "bhqk,bkhd->bqhd",
            narrow(softmax_rows),
            narrow(values),
            preferred_element_type=jnp.float32,
        )
    )


def unpack(vectors):
    extents = [D] * 7 + [MLP] + [D] * 4 + [DD] * 9 + [DMLP] + [DD] * 3 + [PATCH]
    pieces = []
    offset = 0
    for extent in extents:
        pieces.append(vectors[offset : offset + extent])
        offset += extent
    return pieces


def layer_norm(hidden, scaling, offset):
    centred = hidden - jnp.mean(hidden, axis=-1, keepdims=True)
    variance = jnp.mean(centred * centred, axis=-1, keepdims=True)
    return centred * lax.rsqrt(variance + 1e-06) * scaling + offset


def sinusoid(channels):
    quarter = channels // 4
    frequency = 1.0 / 10000.0 ** (jnp.arange(quarter, dtype=jnp.float32) / quarter)
    position = jnp.arange(GT * GF)
    time_rows = (position // GF).astype(jnp.float32)[:, None] * frequency
    freq_cols = (position % GF).astype(jnp.float32)[:, None] * frequency
    return jnp.concatenate(
        [jnp.sin(time_rows), jnp.cos(time_rows), jnp.sin(freq_cols), jnp.cos(freq_cols)], axis=1
    )


def patchify(spec):
    clip_total = spec.shape[0]
    arranged = spec.reshape(clip_total, GT, PS, GF, PS).transpose(0, 1, 3, 2, 4)
    return arranged.reshape(clip_total, GT * GF, PS * PS)


def window_mask():
    time_rows = jnp.arange(GT)
    freq_cols = jnp.arange(GF)
    time_part = (time_rows >= GT - WIN).astype(jnp.int32) + (time_rows >= GT - SHIFT).astype(
        jnp.int32
    )
    freq_part = (freq_cols >= GF - WIN).astype(jnp.int32) + (freq_cols >= GF - SHIFT).astype(
        jnp.int32
    )
    region = time_part[:, None] * 3 + freq_part[None, :]
    region = (
        region.reshape(GT // WIN, WIN, GF // WIN, WIN).transpose(0, 2, 1, 3).reshape(-1, WIN * WIN)
    )
    return region[:, :, None] == region[:, None, :]


def to_windows(grid_rows):
    clip_total = grid_rows.shape[0]
    channels = grid_rows.shape[2]
    arranged = jnp.roll(
        grid_rows.reshape(clip_total, GT, GF, channels), (-SHIFT, -SHIFT), axis=(1, 2)
    )
    arranged = arranged.reshape(clip_total, GT // WIN, WIN, GF // WIN, WIN, channels).transpose(
        0, 1, 3, 2, 4, 5
    )
    return arranged.reshape(-1, WIN * WIN, channels)


def from_windows(windows, clip_total):
    channels = windows.shape[-1]
    arranged = windows.reshape(clip_total, GT // WIN, GF // WIN, WIN, WIN, channels).transpose(
        0, 1, 3, 2, 4, 5
    )
    arranged = jnp.roll(arranged.reshape(clip_total, GT, GF, channels), (SHIFT, SHIFT), axis=(1, 2))
    return arranged.reshape(clip_total, GT * GF, channels)


def attend(queries, key_rows, values, allowed, scaling):
    scores = score_product(queries, key_rows) * scaling
    scores = jnp.where(allowed, scores, -1e30)
    scores = scores - jnp.max(scores, axis=-1, keepdims=True)
    exponent = jnp.exp(scores)
    softmax_rows = exponent / jnp.sum(exponent, axis=-1, keepdims=True)
    return value_product(softmax_rows, values)


def encode(weights, patches, keep, counts):
    pieces = unpack(weights[10])
    clip_total = patches.shape[0]
    picked = jnp.take_along_axis(patches, keep[:, :, None], axis=1)
    hidden = product(picked, weights[8][:, :D]) + pieces[11] + sinusoid(D)[keep]
    normed = layer_norm(hidden, pieces[0], pieces[1])
    joined = product(normed, weights[0])
    queries = (joined[..., :D] + pieces[2]).reshape(clip_total, VIS, HEADS, HEAD)
    key_rows = joined[..., D : 2 * D].reshape(clip_total, VIS, HEADS, HEAD)
    values = (joined[..., 2 * D :] + pieces[3]).reshape(clip_total, VIS, HEADS, HEAD)
    visible = (jnp.arange(VIS)[None, :] < counts[:, None])[:, None, None, :]
    attended = attend(queries, key_rows, values, visible, HEAD ** (-0.5)).reshape(
        clip_total, VIS, D
    )
    hidden = hidden + product(attended, weights[1]) + pieces[4]
    normed = layer_norm(hidden, pieces[5], pieces[6])
    inner = jax.nn.gelu(product(normed, weights[2]) + pieces[7], approximate=False)
    hidden = hidden + product(inner, weights[3]) + pieces[8]
    return layer_norm(hidden, pieces[9], pieces[10])


def decode(weights, latent, patches, keep, counts):
    pieces = unpack(weights[10])[12:]
    clip_total = latent.shape[0]
    placed = product(latent, weights[9]) + pieces[0]
    visible = jnp.arange(VIS)[None, :] < counts[:, None]
    target_rows = jnp.where(visible, keep, NPATCH)
    clip_rows = jnp.arange(clip_total)[:, None]
    filled = (
        jnp.zeros((clip_total, NPATCH + 1, DD), jnp.float32)
        .at[clip_rows, target_rows]
        .add(placed)[:, :NPATCH]
    )
    visible_cells = (
        jnp.zeros((clip_total, NPATCH + 1), jnp.float32)
        .at[clip_rows, target_rows]
        .add(1.0)[:, :NPATCH]
    )
    hidden = filled + (1.0 - visible_cells)[..., None] * pieces[1] + sinusoid(DD)
    normed = layer_norm(hidden, pieces[2], pieces[3])
    windows = to_windows(product(normed, weights[4]))
    queries = (windows[..., :DD] + pieces[4]).reshape(-1, WIN * WIN, DHEADS, DHEAD)
    key_rows = windows[..., DD : 2 * DD].reshape(-1, WIN * WIN, DHEADS, DHEAD)
    values = (windows[..., 2 * DD :] + pieces[5]).reshape(-1, WIN * WIN, DHEADS, DHEAD)
    allowed = jnp.tile(window_mask(), (clip_total, 1, 1))[:, None, :, :]
    attended = attend(queries, key_rows, values, allowed, DHEAD ** (-0.5)).reshape(
        -1, WIN * WIN, DD
    )
    hidden = hidden + product(from_windows(attended, clip_total), weights[5]) + pieces[6]
    normed = layer_norm(hidden, pieces[7], pieces[8])
    inner = jax.nn.gelu(product(normed, weights[6]) + pieces[9], approximate=False)
    hidden = hidden + product(inner, weights[7]) + pieces[10]
    normed = layer_norm(hidden, pieces[11], pieces[12])
    predicted = product(normed, weights[8][:, D:].T) + pieces[13]
    centred = patches - jnp.mean(patches, axis=-1, keepdims=True)
    target = centred * lax.rsqrt(jnp.mean(centred * centred, axis=-1, keepdims=True) + 1e-06)
    deviation = predicted - target
    patch_error = jnp.mean(deviation * deviation, axis=-1)
    return jnp.sum((1.0 - visible_cells) * patch_error)


def take_half(shard, number, core):
    if LONG_COLS[number]:
        extent = shard.shape[1] // 2
        return lax.dynamic_slice_in_dim(shard, core * extent, extent, 1)
    extent = shard.shape[0] // 2
    return lax.dynamic_slice_in_dim(shard, core * extent, extent, 0)


def arrange(gathered_half, number, long_max, short_max):
    upright = gathered_half.T if LONG_COLS[number] else gathered_half
    return jnp.pad(upright, ((0, long_max - upright.shape[0]), (0, short_max - upright.shape[1])))


def disperse(iterate, number, height, breadth, devices, flat_max):
    if LONG_COLS[number]:
        piece = iterate[: breadth // 2, :height].T.reshape(
            devices, height // devices * (breadth // 2)
        )
    else:
        piece = iterate[: height // 2, :breadth].reshape(devices, height // 2 // devices * breadth)
    return jnp.pad(piece, ((0, 0), (0, flat_max - piece.shape[1])))


def restore(row_piece, number, height, breadth, devices):
    if LONG_COLS[number]:
        return row_piece[: height // devices * (breadth // 2)].reshape(
            height // devices, breadth // 2
        )
    return row_piece[: height // 2 // devices * breadth].reshape(height // 2 // devices, breadth)


def adam_update(weight, first_moment, second_moment, gradient, decay):
    first_moment = 0.5 * first_moment + 0.5 * gradient
    second_moment = 0.95 * second_moment + 0.05 * gradient * gradient
    direction = (
        first_moment / (1.0 - 0.5**STEP) / (jnp.sqrt(second_moment / (1.0 - 0.95**STEP)) + 1e-08)
    )
    return (weight - LR_ADAM * (direction + decay * weight), first_moment, second_moment)


def body(
    spectrogram,
    keep,
    counts,
    enc_qkv,
    enc_out,
    enc_up,
    enc_down,
    dec_qkv,
    dec_out,
    dec_up,
    dec_down,
    mom_enc_qkv,
    mom_enc_out,
    mom_enc_up,
    mom_enc_down,
    mom_dec_qkv,
    mom_dec_out,
    mom_dec_up,
    mom_dec_down,
    patch_maps,
    patch_first,
    patch_second,
    embed_map,
    embed_first,
    embed_second,
    vectors,
    vector_first,
    vector_second,
):
    masters = (
        enc_qkv,
        enc_out,
        enc_up,
        enc_down,
        dec_qkv,
        dec_out,
        dec_up,
        dec_down,
        patch_maps,
        embed_map,
        vectors,
    )
    moments = (
        mom_enc_qkv,
        mom_enc_out,
        mom_enc_up,
        mom_enc_down,
        mom_dec_qkv,
        mom_dec_out,
        mom_dec_up,
        mom_dec_down,
    )
    sent = tuple((weight.astype(jnp.bfloat16) for weight in masters))
    gathered = (
        lax.all_gather(sent[0], "dp", axis=0, tiled=True),
        lax.all_gather(sent[1], "dp", axis=0, tiled=True),
        lax.all_gather(sent[2], "dp", axis=0, tiled=True),
        lax.all_gather(sent[3], "dp", axis=0, tiled=True),
        lax.all_gather(sent[4], "dp", axis=0, tiled=True),
        lax.all_gather(sent[5], "dp", axis=0, tiled=True),
        lax.all_gather(sent[6], "dp", axis=0, tiled=True),
        lax.all_gather(sent[7], "dp", axis=0, tiled=True),
        lax.all_gather(sent[8], "dp", axis=0, tiled=True),
        lax.all_gather(sent[9], "dp", axis=0, tiled=True),
        lax.all_gather(sent[10], "dp", axis=0, tiled=True),
    )
    widened = tuple((piece.astype(jnp.float32) for piece in gathered))
    patches = patchify(spectrogram.astype(jnp.float32))
    latent = encode(widened, patches, keep, counts)
    loss_part = decode(widened, latent, patches, keep, counts)
    count_part = jnp.sum(NPATCH - counts).astype(jnp.float32)
    loss_sum, mask_count = lax.psum((loss_part, count_part), ("dp", "mp"))
    regathered = (
        lax.all_gather(sent[0], "dp", axis=0, tiled=True),
        lax.all_gather(sent[1], "dp", axis=0, tiled=True),
        lax.all_gather(sent[2], "dp", axis=0, tiled=True),
        lax.all_gather(sent[3], "dp", axis=0, tiled=True),
        lax.all_gather(sent[4], "dp", axis=0, tiled=True),
        lax.all_gather(sent[5], "dp", axis=0, tiled=True),
        lax.all_gather(sent[6], "dp", axis=0, tiled=True),
        lax.all_gather(sent[7], "dp", axis=0, tiled=True),
        lax.all_gather(sent[8], "dp", axis=0, tiled=True),
        lax.all_gather(sent[9], "dp", axis=0, tiled=True),
        lax.all_gather(sent[10], "dp", axis=0, tiled=True),
    )
    widened = tuple((piece.astype(jnp.float32) for piece in regathered))
    cotangent = 1.0 / mask_count
    unused, pull_decode = jax.vjp(
        lambda params, hidden: decode(params, hidden, patches, keep, counts), widened, latent
    )
    decode_grads, latent_grad = pull_decode(cotangent)
    unused, pull_encode = jax.vjp(lambda params: encode(params, patches, keep, counts), widened)
    (encode_grads,) = pull_encode(latent_grad)
    grads = jax.tree.map(jnp.add, decode_grads, encode_grads)
    reduced = (
        lax.psum_scatter(grads[0], "dp", scatter_dimension=0, tiled=True),
        lax.psum_scatter(grads[1], "dp", scatter_dimension=0, tiled=True),
        lax.psum_scatter(grads[2], "dp", scatter_dimension=0, tiled=True),
        lax.psum_scatter(grads[3], "dp", scatter_dimension=0, tiled=True),
        lax.psum_scatter(grads[4], "dp", scatter_dimension=0, tiled=True),
        lax.psum_scatter(grads[5], "dp", scatter_dimension=0, tiled=True),
        lax.psum_scatter(grads[6], "dp", scatter_dimension=0, tiled=True),
        lax.psum_scatter(grads[7], "dp", scatter_dimension=0, tiled=True),
        lax.psum_scatter(grads[8], "dp", scatter_dimension=0, tiled=True),
        lax.psum_scatter(grads[9], "dp", scatter_dimension=0, tiled=True),
        lax.psum_scatter(grads[10], "dp", scatter_dimension=0, tiled=True),
    )
    reduced = lax.psum(
        (
            reduced[0],
            reduced[1],
            reduced[2],
            reduced[3],
            reduced[4],
            reduced[5],
            reduced[6],
            reduced[7],
            reduced[8],
            reduced[9],
            reduced[10],
        ),
        "mp",
    )
    local_squares = functools.reduce(
        jnp.add, [jnp.sum(gradient * gradient) for gradient in reduced]
    )
    grad_norm = jnp.sqrt(lax.psum(local_squares, "dp"))
    factor = jnp.minimum(1.0, CLIP_MAX / (grad_norm + 1e-06))
    clipped = [gradient * factor for gradient in reduced]
    devices = lax.axis_size("dp")
    renewed = [0.5 * moments[number] + clipped[number] for number in range(8)]
    core = lax.axis_index("mp")
    halves = [take_half(renewed[number], number, core) for number in range(8)]
    shapes = [(masters[number].shape[0] * devices, masters[number].shape[1]) for number in range(8)]
    long_max = max((max(shape_pair) // 2 for shape_pair in shapes))
    short_max = max((min(shape_pair) for shape_pair in shapes))
    flat_max = max((shape_pair[0] * shape_pair[1] // (2 * devices) for shape_pair in shapes))
    owner = lax.axis_index("dp") % 8
    collected = (
        lax.all_gather(halves[0], "dp", axis=0, tiled=True),
        lax.all_gather(halves[1], "dp", axis=0, tiled=True),
        lax.all_gather(halves[2], "dp", axis=0, tiled=True),
        lax.all_gather(halves[3], "dp", axis=0, tiled=True),
        lax.all_gather(halves[4], "dp", axis=0, tiled=True),
        lax.all_gather(halves[5], "dp", axis=0, tiled=True),
        lax.all_gather(halves[6], "dp", axis=0, tiled=True),
        lax.all_gather(halves[7], "dp", axis=0, tiled=True),
    )
    iterate = lax.switch(
        owner,
        [partial(arrange, collected[number], number, long_max, short_max) for number in range(8)],
    )
    for iteration in range(NS_ITERS):
        gram_sum = lax.psum(jnp.dot(iterate.T, iterate, precision=HIGH), "mp")
        if iteration == 0:
            norm_scale = 1.0 / (jnp.sqrt(jnp.trace(gram_sum)) + 1e-07)
            iterate = iterate * norm_scale
            gram_sum = gram_sum * (norm_scale * norm_scale)
        polynomial = NS_B * gram_sum + NS_C * jnp.dot(gram_sum, gram_sum, precision=HIGH)
        iterate = NS_A * iterate + jnp.dot(iterate, polynomial, precision=HIGH)
    outgoing = lax.switch(
        owner,
        [
            partial(
                disperse, iterate, number, shapes[number][0], shapes[number][1], devices, flat_max
            )
            for number in range(8)
        ],
    )
    arriving = jax.tree.map(
        lambda part, own: part.astype(own.dtype),
        lax.all_to_all(shortened(outgoing), "dp", split_axis=0, concat_axis=0, tiled=True),
        outgoing,
    )
    mine = [
        restore(arriving[number], number, shapes[number][0], shapes[number][1], devices)
        for number in range(8)
    ]
    whole = (
        lax.all_gather(shortened(mine[0]), "mp", axis=1, tiled=True),
        lax.all_gather(shortened(mine[1]), "mp", axis=1, tiled=True),
        lax.all_gather(shortened(mine[2]), "mp", axis=1, tiled=True),
        lax.all_gather(shortened(mine[3]), "mp", axis=0, tiled=True),
        lax.all_gather(shortened(mine[4]), "mp", axis=1, tiled=True),
        lax.all_gather(shortened(mine[5]), "mp", axis=1, tiled=True),
        lax.all_gather(shortened(mine[6]), "mp", axis=1, tiled=True),
        lax.all_gather(shortened(mine[7]), "mp", axis=0, tiled=True),
    )
    new_weights = []
    for number in range(8):
        step_rate = LR_MUON * 0.2 * math.sqrt(max(shapes[number]))
        new_weights.append(masters[number] * (1.0 - LR_MUON * DECAY) - step_rate * whole[number])
    patch_new = adam_update(patch_maps, patch_first, patch_second, clipped[8], DECAY)
    embed_new = adam_update(embed_map, embed_first, embed_second, clipped[9], DECAY)
    vector_new = adam_update(vectors, vector_first, vector_second, clipped[10], 0.0)
    return (
        loss_sum,
        mask_count,
        grad_norm,
        new_weights[0],
        new_weights[1],
        new_weights[2],
        new_weights[3],
        new_weights[4],
        new_weights[5],
        new_weights[6],
        new_weights[7],
        renewed[0],
        renewed[1],
        renewed[2],
        renewed[3],
        renewed[4],
        renewed[5],
        renewed[6],
        renewed[7],
        patch_new[0],
        patch_new[1],
        patch_new[2],
        embed_new[0],
        embed_new[1],
        embed_new[2],
        vector_new[0],
        vector_new[1],
        vector_new[2],
    )


def solution(mesh):
    placed = (
        P(("dp", "mp"), None, None),
        P(("dp", "mp"), None),
        P(("dp", "mp")),
        P("dp", None),
        P("dp", None),
        P("dp", None),
        P("dp", None),
        P("dp", None),
        P("dp", None),
        P("dp", None),
        P("dp", None),
        P("dp", None),
        P("dp", None),
        P("dp", None),
        P("dp", None),
        P("dp", None),
        P("dp", None),
        P("dp", None),
        P("dp", None),
        P("dp", None),
        P("dp", None),
        P("dp", None),
        P("dp", None),
        P("dp", None),
        P("dp", None),
        P("dp"),
        P("dp"),
        P("dp"),
    )
    return jax.shard_map(
        body,
        mesh=mesh,
        in_specs=placed,
        out_specs=(
            P(),
            P(),
            P(),
            P("dp", None),
            P("dp", None),
            P("dp", None),
            P("dp", None),
            P("dp", None),
            P("dp", None),
            P("dp", None),
            P("dp", None),
            P("dp", None),
            P("dp", None),
            P("dp", None),
            P("dp", None),
            P("dp", None),
            P("dp", None),
            P("dp", None),
            P("dp", None),
            P("dp", None),
            P("dp", None),
            P("dp", None),
            P("dp", None),
            P("dp", None),
            P("dp", None),
            P("dp"),
            P("dp"),
            P("dp"),
        ),
        check_vma=False,
    )
```

profile of v0, /device:TPU:15, one launch (start us, length us, event | category | flops | bytes accessed | tf_op | source)
XLA Modules:
  0.0 3303.1 jit_solution(10033038684563546109)
XLA Ops:
  21.6 49.7 %all-reduce.55 = bf16[19968]{0:T(1024)(128)(2,1)S(1)} all-reduce(bf16[19968]{0:T(1024)(128)(2,1)S(1)} %dynamic-update-slice), channel_id=1, replica_groups=mesh['dp'=16,'mp'=2] {'dp'}, use_global_device_ids=true, to_apply=%add.55 | all-reduce | flops 19968 | bytes 79872
  73.7 38.2 %all_gather.116 = bf16[256,1280]{1,0:T(8,128)(2,1)S(1)} all-gather(bf16[16,1280]{1,0:T(8,128)(2,1)S(1)} %convert_element_type.484), channel_id=1, replica_groups=mesh['dp'=16,'mp'=2] {'dp'}, dimensions={0}, use_global_device_ids=true | all-gather | bytes 696320 | tf_op jit(solution)/shard_map/all_gather | solution.py:347
  127.0 69.9 %psum.134 = f32[]{:T(128)} all-reduce(f32[]{:T(128)S(6)} %convert_element_type.527), channel_id=1, replica_groups=mesh['dp'=16,'mp'=2] {'dp','mp'}, use_global_device_ids=true, to_apply=%region_24.26 | all-reduce | flops 1 | bytes 8 | tf_op jit(solution)/shard_map/psum | solution.py:356
  226.6 39.2 %all_gather.122 = bf16[768,512]{1,0:T(8,128)(2,1)} all-gather(bf16[48,512]{1,0:T(8,128)(2,1)S(1)} %convert_element_type.506), channel_id=1, replica_groups=mesh['dp'=16,'mp'=2] {'dp'}, dimensions={0}, use_global_device_ids=true | all-gather | bytes 835584 | tf_op jit(solution)/shard_map/all_gather | solution.py:348
  348.9 66.6 %all-gather.19.cloned.1.call-done = bf16[768,3072]{1,0:T(8,128)(2,1)} async-done(((bf16[48,3072]{1,0:T(8,128)(2,1)}), bf16[768,3072]{1,0:T(8,128)(2,1)}) %all-gather.19.cloned.1.call-update) | async-done | bytes 4718608 | tf_op jit(solution)/shard_map/all_gather | solution.py:341
  430.0 68.0 %all-gather.21.cloned.1.call-done = bf16[3072,768]{1,0:T(8,128)(2,1)} async-done(((bf16[192,768]{1,0:T(8,128)(2,1)}), bf16[3072,768]{1,0:T(8,128)(2,1)}) %all-gather.21.cloned.1.call-update) | async-done | bytes 4718608 | tf_op jit(solution)/shard_map/all_gather | solution.py:342
  507.2 41.5 %scatter_fusion.1 = f32[2,513,512]{2,0,1:T(2,128)} fusion(f32[2,513,512]{2,0,1:T(2,128)} %broadcast.822, s32[308]{0:T(512)S(1)} %reshape.656, f32[308,512]{1,0:T(8,128)S(1)} %reshape.664), kind=kCustom, calls=%fused_computation.4 | custom fusion | flops 157696 | bytes 1894816 | tf_op jit(solution)/shard_map/scatter-add | solution.py:214
  983.8 72.6 %reduce-scatter.27.cloned.1.call-done = f32[16,1280]{1,0:T(8,128)} async-done(((f32[256,1280]{1,0:T(8,128)}), f32[16,1280]{1,0:T(8,128)}) %reduce-scatter.27.cloned.1.call-update) | async-done | bytes 81936 | tf_op jit(solution)/shard_map/reduce_scatter | solution.py:388
  1056.4 148.6 %reduce-scatter.29.cloned.1.call-done = f32[48,512]{1,0:T(8,128)} async-done(((f32[768,512]{1,0:T(8,128)}), f32[48,512]{1,0:T(8,128)}) %reduce-scatter.29.cloned.1.call-update) | async-done | bytes 98320 | tf_op jit(solution)/shard_map/reduce_scatter | solution.py:389
  1205.1 133.0 %reduce-scatter.13.cloned.1.call-done = f32[48,768]{1,0:T(8,128)} async-done(((f32[768,768]{1,0:T(8,128)}), f32[48,768]{1,0:T(8,128)}) %reduce-scatter.13.cloned.1.call-update) | async-done | bytes 147472 | tf_op jit(solution)/shard_map/reduce_scatter | solution.py:381
  1338.1 134.6 %reduce-scatter.19.cloned.1.call-done = f32[32,1536]{1,0:T(8,128)} async-done(((f32[512,1536]{1,0:T(8,128)}), f32[32,1536]{1,0:T(8,128)}) %reduce-scatter.19.cloned.1.call-update) | async-done | bytes 196624 | tf_op jit(solution)/shard_map/reduce_scatter | solution.py:384
  1472.6 96.0 %reduce-scatter.25.cloned.1.call-done = f32[128,512]{1,0:T(8,128)} async-done(((f32[2048,512]{1,0:T(8,128)}), f32[128,512]{1,0:T(8,128)}) %reduce-scatter.25.cloned.1.call-update) | async-done | bytes 262160 | tf_op jit(solution)/shard_map/reduce_scatter | solution.py:387
  1568.6 96.9 %reduce-scatter.23.cloned.1.call-done = f32[32,2048]{1,0:T(8,128)} async-done(((f32[512,2048]{1,0:T(8,128)}), f32[32,2048]{1,0:T(8,128)}) %reduce-scatter.23.cloned.1.call-update) | async-done | bytes 262160 | tf_op jit(solution)/shard_map/reduce_scatter | solution.py:386
  1665.5 156.1 %reduce-scatter.11.cloned.1.call-done = f32[48,2304]{1,0:T(8,128)} async-done(((f32[768,2304]{1,0:T(8,128)}), f32[48,2304]{1,0:T(8,128)}) %reduce-scatter.11.cloned.1.call-update) | async-done | bytes 442384 | tf_op jit(solution)/shard_map/reduce_scatter | solution.py:380
  1821.7 176.1 %reduce-scatter.15.cloned.1.call-done = f32[48,3072]{1,0:T(8,128)} async-done(((f32[768,3072]{1,0:T(8,128)}), f32[48,3072]{1,0:T(8,128)}) %reduce-scatter.15.cloned.1.call-update) | async-done | bytes 589840 | tf_op jit(solution)/shard_map/reduce_scatter | solution.py:382
  1997.7 176.5 %reduce-scatter.17.cloned.1.call-done = f32[192,768]{1,0:T(8,128)} async-done(((f32[3072,768]{1,0:T(8,128)}), f32[192,768]{1,0:T(8,128)}) %reduce-scatter.17.cloned.1.call-update) | async-done | bytes 589840 | tf_op jit(solution)/shard_map/reduce_scatter | solution.py:383
  2174.9 106.6 %all-reduce.76.cloned.1.call-done = f32[19968]{0:T(1024)} async-done(((f32[19968]{0:T(1024)}), f32[19968]{0:T(1024)}) %all-reduce.76.cloned.1.call-update) | async-done | bytes 79888
  2430.3 60.0 %all-gather.37.cloned.1.call-done = f32[512,768]{1,0:T(8,128)} async-done(((f32[32,768]{1,0:T(8,128)}), f32[512,768]{1,0:T(8,128)}) %all-gather.37.cloned.1.call-update) | async-done | bytes 1572880 | tf_op jit(solution)/shard_map/all_gather | solution.py:428
  2490.3 63.9 %all-gather.39.cloned.1.call-done = f32[512,1024]{1,0:T(8,128)} async-done(((f32[32,1024]{1,0:T(8,128)}), f32[512,1024]{1,0:T(8,128)}) %all-gather.39.cloned.1.call-update) | async-done | bytes 2097168 | tf_op jit(solution)/shard_map/all_gather | solution.py:430
  2554.2 62.7 %all-gather.41.cloned.1.call-done = f32[1024,512]{1,0:T(8,128)} async-done(((f32[64,512]{1,0:T(8,128)}), f32[1024,512]{1,0:T(8,128)}) %all-gather.41.cloned.1.call-update) | async-done | bytes 2097168 | tf_op jit(solution)/shard_map/all_gather | solution.py:431
  2617.0 72.7 %all-gather.29.cloned.1.call-done = f32[768,1152]{1,0:T(8,128)} async-done(((f32[48,1152]{1,0:T(8,128)}), f32[768,1152]{1,0:T(8,128)}) %all-gather.29.cloned.1.call-update) | async-done | bytes 3538960 | tf_op jit(solution)/shard_map/all_gather | solution.py:424
  2689.6 82.2 %all-gather.33.cloned.1.call-done = f32[768,1536]{1,0:T(8,128)} async-done(((f32[48,1536]{1,0:T(8,128)}), f32[768,1536]{1,0:T(8,128)}) %all-gather.33.cloned.1.call-update) | async-done | bytes 4718608 | tf_op jit(solution)/shard_map/all_gather | solution.py:426
  2771.8 82.3 %all-gather.35.cloned.1.call-done = f32[1536,768]{1,0:T(8,128)} async-done(((f32[96,768]{1,0:T(8,128)}), f32[1536,768]{1,0:T(8,128)}) %all-gather.35.cloned.1.call-update) | async-done | bytes 4718608 | tf_op jit(solution)/shard_map/all_gather | solution.py:427
  3180.1 72.2 %psum.133 = f32[]{:T(128)} all-reduce(f32[]{:T(128)} %multiply_reduce_fusion.34), channel_id=1, replica_groups=mesh['dp'=16,'mp'=2] {'dp','mp'}, use_global_device_ids=true, to_apply=%region_22.24 | all-reduce | flops 1 | bytes 8 | tf_op jit(solution)/shard_map/psum | solution.py:356
  (880 shorter events, 1113.3 us)
Async XLA Ops:
  7.3 310.4 %all-gather.17.cloned.1.call-start = ((), (), s32[]{:S(2)}) async-start(), calls=%async_computation.12 | async-start | bytes 1253376 | tf_op jit(solution)/shard_map/all_gather | solution.py:340
  9.0 308.7 %all-gather.23.cloned.1.call-start = ((), (), s32[]{:S(2)}) async-start(), calls=%async_computation.15 | async-start | bytes 1671168 | tf_op jit(solution)/shard_map/all_gather | solution.py:343
  10.6 307.1 %all-gather.25.cloned.1.call-start = ((), (), s32[]{:S(2)}) async-start(), calls=%async_computation.16 | async-start | bytes 2228224 | tf_op jit(solution)/shard_map/all_gather | solution.py:345
  12.3 305.4 %all-gather.27.cloned.1.call-start = ((), (), s32[]{:S(2)}) async-start(), calls=%async_computation.17 | async-start | bytes 2228224 | tf_op jit(solution)/shard_map/all_gather | solution.py:346
  14.0 319.4 %all-gather.15.cloned.1.call-start = ((), (), s32[]{:S(2)}) async-start(), calls=%async_computation.11 | async-start | bytes 3760128 | tf_op jit(solution)/shard_map/all_gather | solution.py:339
  15.8 399.6 %all-gather.19.cloned.1.call-start = ((), (), s32[]{:S(2)}) async-start(), calls=%async_computation.13 | async-start | bytes 5013504 | tf_op jit(solution)/shard_map/all_gather | solution.py:341
  17.7 480.2 %all-gather.21.cloned.1.call-start = ((), (), s32[]{:S(2)}) async-start(), calls=%async_computation.14 | async-start | bytes 5013504 | tf_op jit(solution)/shard_map/all_gather | solution.py:342
  18.6 965.3 %reduce-scatter.21.cloned.1.call-start = ((), (), s32[]{:S(2)}) async-start(), calls=%async_computation.23 | async-start | bytes 1114112 | tf_op jit(solution)/shard_map/reduce_scatter | solution.py:385
  936.6 268.5 %reduce-scatter.29.cloned.1.call-start = ((), (), s32[]{:S(2)}) async-start(), calls=%async_computation.27 | async-start | bytes 1671168 | tf_op jit(solution)/shard_map/reduce_scatter | solution.py:389
  939.4 398.6 %reduce-scatter.13.cloned.1.call-start = ((), (), s32[]{:S(2)}) async-start(), calls=%async_computation.19 | async-start | bytes 2506752 | tf_op jit(solution)/shard_map/reduce_scatter | solution.py:381
  941.7 530.9 %reduce-scatter.19.cloned.1.call-start = ((), (), s32[]{:S(2)}) async-start(), calls=%async_computation.22 | async-start | bytes 3342336 | tf_op jit(solution)/shard_map/reduce_scatter | solution.py:384
  947.6 621.0 %reduce-scatter.25.cloned.1.call-start = ((), (), s32[]{:S(2)}) async-start(), calls=%async_computation.25 | async-start | bytes 4456448 | tf_op jit(solution)/shard_map/reduce_scatter | solution.py:387
  954.3 711.2 %reduce-scatter.23.cloned.1.call-start = ((), (), s32[]{:S(2)}) async-start(), calls=%async_computation.24 | async-start | bytes 4456448 | tf_op jit(solution)/shard_map/reduce_scatter | solution.py:386
  962.1 859.6 %reduce-scatter.11.cloned.1.call-start = ((), (), s32[]{:S(2)}) async-start(), calls=%async_computation.18 | async-start | bytes 7520256 | tf_op jit(solution)/shard_map/reduce_scatter | solution.py:380
  968.1 1029.6 %reduce-scatter.15.cloned.1.call-start = ((), (), s32[]{:S(2)}) async-start(), calls=%async_computation.20 | async-start | bytes 10027008 | tf_op jit(solution)/shard_map/reduce_scatter | solution.py:382
  974.9 1199.3 %reduce-scatter.17.cloned.1.call-start = ((), (), s32[]{:S(2)}) async-start(), calls=%async_computation.21 | async-start | bytes 10027008 | tf_op jit(solution)/shard_map/reduce_scatter | solution.py:383
  981.9 1299.6 %all-reduce.76.cloned.1.call-start = ((), (), s32[]{:S(2)}) async-start(), calls=%async_computation.40 | async-start | bytes 163840
  983.7 1327.4 %all-reduce.78.cloned.1.call-start = ((), (), s32[]{:S(2)}) async-start(), calls=%async_computation.41 | async-start | bytes 5472256 | tf_op jit(solution)/shard_map/psum | solution.py:392
  2174.2 256.1 %all-gather.31.cloned.1.call-start = ((), (), s32[]{:S(2)}) async-start(), calls=%async_computation.29 | async-start | bytes 1253376 | tf_op jit(solution)/shard_map/all_gather | solution.py:425
  2365.3 251.7 %all-gather.41.cloned.1.call-start = ((), (), s32[]{:S(2)}) async-start(), calls=%async_computation.34 | async-start | bytes 2228224 | tf_op jit(solution)/shard_map/all_gather | solution.py:431
  2367.1 322.5 %all-gather.29.cloned.1.call-start = ((), (), s32[]{:S(2)}) async-start(), calls=%async_computation.28 | async-start | bytes 3760128 | tf_op jit(solution)/shard_map/all_gather | solution.py:424
  2369.7 402.1 %all-gather.33.cloned.1.call-start = ((), (), s32[]{:S(2)}) async-start(), calls=%async_computation.30 | async-start | bytes 5013504 | tf_op jit(solution)/shard_map/all_gather | solution.py:426
  2371.4 482.7 %all-gather.35.cloned.1.call-start = ((), (), s32[]{:S(2)}) async-start(), calls=%async_computation.31 | async-start | bytes 5013504 | tf_op jit(solution)/shard_map/all_gather | solution.py:427
  2373.1 527.0 %all-reduce.66.cloned.1.call-start = ((), (), s32[]{:S(2)}) async-start(), calls=%async_computation.35 | async-start | bytes 4718592 | tf_op jit(solution)/shard_map/psum | solution.py:438
  (238 other events, 9440.4 us)
Sparse Core Ops, SparseCore 0:
  69.1 59.0 all-gather.22
  131.5 60.7 all-gather.24
  195.5 63.7 all-gather.26
  262.5 70.8 all-gather.14
  336.6 78.7 all-gather.18
  418.8 79.0 all-gather.20
  923.0 55.3 reduce-scatter.20
  980.8 75.6 reduce-scatter.26
  1061.8 143.2 reduce-scatter.28
  1210.8 127.2 reduce-scatter.12
  1342.9 129.6 reduce-scatter.18
  1474.9 93.6 reduce-scatter.24
  1570.7 94.7 reduce-scatter.22
  1670.7 150.8 reduce-scatter.10
  1827.2 170.5 reduce-scatter.14
  2004.2 169.9 reduce-scatter.16
  2180.1 101.3 all-reduce.75
  2360.5 69.7 all-gather.30
  2433.7 56.5 all-gather.36
  2493.7 60.5 all-gather.38
  2557.6 59.3 all-gather.40
  2620.2 69.3 all-gather.28
  2693.0 78.7 all-gather.32
  2775.0 79.0 all-gather.34
  (7 shorter events, 195.9 us)
where the time goes:
time: 3320 us; the launch traced here: 3300 us
  waiting for transfers between devices  2030 us (61%)
  blocking collectives  378 us (11%)
  matrix products  325 us (10%)
  local copies, waits for them, and re-layouts  284 us (9%)
  other arithmetic  250 us (8%)
    reduce_scatter x1, waiting for transfers between devices, body(): lax.psum_scatter(grads[3], 'dp', scatter_dimension=0, tiled=True)  176 us
    reduce_scatter x1, waiting for transfers between devices, body(): lax.psum_scatter(grads[2], 'dp', scatter_dimension=0, tiled=True)  176 us
    reduce_scatter x1, waiting for transfers between devices, body(): lax.psum_scatter(grads[0], 'dp', scatter_dimension=0, tiled=True)  156 us
    reduce_scatter x1, waiting for transfers between devices, body(): lax.psum_scatter(grads[9], 'dp', scatter_dimension=0, tiled=True)  149 us
    psum x2, blocking collectives, body(): loss_sum, mask_count = lax.psum((loss_part, count_part), ('dp', 'mp'))  142 us
    reduce_scatter x1, waiting for transfers between devices, body(): lax.psum_scatter(grads[4], 'dp', scatter_dimension=0, tiled=True)  135 us
    reduce_scatter x1, waiting for transfers between devices, body(): lax.psum_scatter(grads[1], 'dp', scatter_dimension=0, tiled=True)  133 us
    psum x5, waiting for transfers between devices, body(): gram_sum = lax.psum(jnp.dot(iterate.T, iterate, precision=HIGH), 'mp')  110 us
  transfers between devices with their start and end apart: 32, of which 26 were waited for; matrix products, arithmetic and copies ran while one was open for 5% of the time, Pallas kernels for 0%

commit v1 on v0

--- a/solution.py
+++ b/solution.py
@@ -4,7 +4,10 @@
 
 import jax
 import jax.numpy as jnp
+import numpy as np
 from jax import lax
+from jax.experimental import pallas as pl
+from jax.experimental.pallas import tpu as pltpu
 from jax.sharding import PartitionSpec as P
 
 D = 768
@@ -279,6 +282,928 @@
         first_moment / (1.0 - 0.5**STEP) / (jnp.sqrt(second_moment / (1.0 - 0.95**STEP)) + 1e-08)
     )
     return (weight - LR_ADAM * (direction + decay * weight), first_moment, second_moment)
+
+
+MESH_ID = pl.DeviceIdType.MESH
+VEC_ROWS, VEC_COLS = 16, 256
+GATHER_TURNS = (2, 2, 0, 1, 2, 0, 0, 1, 2, 1, 2)
+REDUCE_TURNS = (2, 2, 0, 1, 2, 0, 0, 1, 0, 1, 2)
+OWNERS = (0, 3, 5, 6, 8, 11, 13, 14)
+SLOTS = 160
+
+
+def bit_count(devices):
+    return devices.bit_length() - 1
+
+
+def bit_order(levels, turn):
+    down = list(range(levels - 1, -1, -1))
+    turn = turn % levels
+    return down[levels - turn :] + down[: levels - turn]
+
+
+def own_bits(levels):
+    me = lax.axis_index("dp")
+    return me, [lax.rem(lax.div(me, 2**bit), 2) for bit in range(levels)]
+
+
+def place(levels, free, own, flip=None):
+    spots = []
+    for bit in range(levels - 1, -1, -1):
+        if bit in free:
+            spots.append(slice(None))
+        elif bit == flip:
+            spots.append(1 - own[bit])
+        else:
+            spots.append(own[bit])
+    return tuple(spots)
+
+
+def partner(me, own, bit):
+    return me + (1 - 2 * own[bit]) * 2**bit
+
+
+def greet(me, own, levels, core):
+    barrier = pltpu.get_barrier_semaphore()
+    for bit in range(levels):
+        pl.semaphore_signal(
+            barrier,
+            inc=1,
+            device_id={"dp": partner(me, own, bit), "mp": core},
+            device_id_type=MESH_ID,
+        )
+    pl.semaphore_signal(barrier, inc=1, device_id={"dp": me, "mp": 1 - core}, device_id_type=MESH_ID)
+    pl.semaphore_wait(barrier, levels + 1)
+
+
+def add_up(me, own, core, levels, total, landing, send_sem, recv_sem):
+    for stage in range(levels + 1):
+        if stage < levels:
+            to = {"dp": partner(me, own, stage), "mp": core}
+        else:
+            to = {"dp": me, "mp": 1 - core}
+        swap = pltpu.make_async_remote_copy(
+            src_ref=total,
+            dst_ref=landing.at[stage],
+            send_sem=send_sem.at[stage],
+            recv_sem=recv_sem.at[stage],
+            device_id=to,
+            device_id_type=MESH_ID,
+        )
+        swap.start()
+        swap.wait()
+        total[...] = total[...] + landing[stage]
+
+
+def gather_kernel(levels, turns, count, *refs):
+    shards, tally = refs[:count], refs[count]
+    wholes, tally_out = refs[count + 1 : 2 * count + 1], refs[2 * count + 1]
+    here_sem, send_sem, recv_sem, cross_send, cross_recv = refs[2 * count + 2 : 2 * count + 7]
+    tally_land, tally_send, tally_recv = refs[2 * count + 7 :]
+    me, own = own_bits(levels)
+    core = lax.axis_index("mp")
+    greet(me, own, levels, core)
+    orders = [bit_order(levels, turn) for turn in turns]
+
+    def half(number, which):
+        width = shards[number].shape[1] // 2
+        return (slice(None), pl.ds(pl.multiple_of(which * width, 128), width))
+
+    def hop(number, stage, flip):
+        order = orders[number]
+        spot = place(levels, order[:stage], own, order[stage] if flip else None)
+        target = wholes[number].at[spot + half(number, core)]
+        source = target if stage or flip else shards[number].at[half(number, core)]
+        return pltpu.make_async_remote_copy(
+            src_ref=source,
+            dst_ref=target,
+            send_sem=send_sem.at[number, stage],
+            recv_sem=recv_sem.at[number, stage],
+            device_id={"dp": partner(me, own, order[stage]), "mp": core},
+            device_id_type=MESH_ID,
+        )
+
+    def cross(number, stage, which):
+        order = orders[number]
+        spot = place(levels, order[:stage], own, order[stage])
+        target = wholes[number].at[spot + half(number, which)]
+        return pltpu.make_async_remote_copy(
+            src_ref=target,
+            dst_ref=target,
+            send_sem=cross_send.at[number, stage],
+            recv_sem=cross_recv.at[number, stage],
+            device_id={"dp": me, "mp": 1 - core},
+            device_id_type=MESH_ID,
+        )
+
+    def keep(number):
+        spot = place(levels, (), own)
+        return pltpu.make_async_copy(shards[number], wholes[number].at[spot], here_sem.at[number])
+
+    for number in range(count):
+        hop(number, 0, False).start()
+    for number in range(count):
+        keep(number).start()
+    tally_out[...] = tally[...]
+    add_up(me, own, core, levels, tally_out, tally_land, tally_send, tally_recv)
+    for number in range(count):
+        keep(number).wait()
+    for stage in range(levels):
+        for number in range(count):
+            hop(number, stage, True).wait_recv()
+            if stage + 1 < levels:
+                hop(number, stage + 1, False).start()
+            cross(number, stage, core).start()
+    for stage in range(levels):
+        for number in range(count):
+            hop(number, stage, False).wait_send()
+            cross(number, stage, core).wait_send()
+            cross(number, stage, 1 - core).wait_recv()
+
+
+def gather_rows(shards, tally, devices, turns):
+    levels, count = bit_count(devices), len(shards)
+    lead = (2,) * levels
+    dma = pltpu.SemaphoreType.DMA
+    vmem = pl.BlockSpec(memory_space=pltpu.VMEM)
+    found = pl.pallas_call(
+        functools.partial(gather_kernel, levels, turns, count),
+        out_shape=[jax.ShapeDtypeStruct(lead + shard.shape, shard.dtype) for shard in shards]
+        + [jax.ShapeDtypeStruct((8, 128), jnp.float32)],
+        in_specs=[pl.BlockSpec(memory_space=pl.ANY)] * count + [vmem],
+        out_specs=[pl.BlockSpec(memory_space=pl.ANY)] * count + [vmem],
+        scratch_shapes=[dma((count,))]
+        + [dma((count, levels))] * 4
+        + [pltpu.VMEM((levels + 1, 8, 128), jnp.float32)]
+        + [dma((levels + 1,))] * 2,
+        compiler_params=pltpu.CompilerParams(collective_id=1, has_side_effects=True),
+        name="gather_rows",
+    )(*shards, tally)
+    return found[:count], found[count]
+
+
+def reduce_kernel(levels, turns, count, *refs):
+    grads, stats_in = refs[:count], refs[count]
+    sums, stats_out = refs[count + 1 : 2 * count + 1], refs[2 * count + 1]
+    rest = refs[2 * count + 2 :]
+    mine, theirs, rest = rest[:count], rest[count : 2 * count], rest[2 * count :]
+    kept, rest = rest[:count], rest[count:]
+    landing, rest = rest[: count * levels], rest[count * levels :]
+    stats_land, here_sem, pair_send, pair_recv, send_sem, recv_sem, last_send, last_recv, stats_send, stats_recv = rest
+    me, own = own_bits(levels)
+    core = lax.axis_index("mp")
+    greet(me, own, levels, core)
+    orders = [bit_order(levels, turn)[::-1] for turn in turns]
+
+    def half(number, which):
+        width = grads[number].shape[-1] // 2
+        return (slice(None), pl.ds(pl.multiple_of(which * width, 128), width))
+
+    every = (slice(None),) * levels
+
+    def pair(number):
+        return pltpu.make_async_remote_copy(
+            src_ref=grads[number].at[every + half(number, 1 - core)],
+            dst_ref=theirs[number],
+            send_sem=pair_send.at[number],
+            recv_sem=pair_recv.at[number],
+            device_id={"dp": me, "mp": 1 - core},
+            device_id_type=MESH_ID,
+        )
+
+    def load(number):
+        return pltpu.make_async_copy(
+            grads[number].at[every + half(number, core)], mine[number], here_sem.at[number]
+        )
+
+    def hop(number, stage):
+        order = orders[number]
+        spot = place(levels, order[stage + 1 :], own, order[stage])
+        return pltpu.make_async_remote_copy(
+            src_ref=theirs[number].at[spot],
+            dst_ref=landing[number * levels + stage],
+            send_sem=send_sem.at[number, stage],
+            recv_sem=recv_sem.at[number, stage],
+            device_id={"dp": partner(me, own, order[stage]), "mp": core},
+            device_id_type=MESH_ID,
+        )
+
+    def share(number, which):
+        region = sums[number].at[half(number, which)]
+        return pltpu.make_async_remote_copy(
+            src_ref=region,
+            dst_ref=region,
+            send_sem=last_send.at[number],
+            recv_sem=last_recv.at[number],
+            device_id={"dp": me, "mp": 1 - core},
+            device_id_type=MESH_ID,
+        )
+
+    def fold(number, stage):
+        order = orders[number]
+        free = order[stage:]
+        loose = [bit for bit in range(levels - 1, -1, -1) if bit in free and bit != order[stage]]
+
+        @pl.loop(0, 2 ** len(loose))
+        def add_block(block):
+            found = {
+                bit: lax.rem(lax.div(block, 2 ** (len(loose) - 1 - i)), 2) for i, bit in enumerate(loose)
+            }
+
+            def total(way):
+                now = dict(found)
+                now[order[stage]] = way
+                full = tuple(now.get(bit, own[bit]) for bit in range(levels - 1, -1, -1))
+                if stage == 0:
+                    value = mine[number][full].astype(jnp.float32) + theirs[number][full].astype(jnp.float32)
+                else:
+                    spot = tuple(
+                        now.get(bit, own[bit]) for bit in range(levels - 1, -1, -1) if bit != order[0]
+                    )
+                    land = tuple(now[bit] for bit in range(levels - 1, -1, -1) if bit in free)
+                    value = kept[number][spot] + landing[number * levels + stage - 1][land].astype(jnp.float32)
+                return full, value
+
+            full, value = total(1 - own[order[stage]])
+            theirs[number][full] = value.astype(theirs[number].dtype)
+            full, value = total(own[order[stage]])
+            spot = tuple(
+                found.get(bit, own[bit]) for bit in range(levels - 1, -1, -1) if bit != order[0]
+            )
+            kept[number][spot] = value
+
+    for number in range(count):
+        pair(number).start()
+        load(number).start()
+    for number in range(count):
+        load(number).wait()
+        pair(number).wait_recv()
+        fold(number, 0)
+        hop(number, 0).start()
+    for stage in range(levels - 1):
+        for number in range(count):
+            hop(number, stage).wait_recv()
+            fold(number, stage + 1)
+            hop(number, stage + 1).start()
+    squares = jnp.zeros((8, 128), jnp.float32)
+    for number in range(count):
+        hop(number, levels - 1).wait_recv()
+        spot = tuple(own[bit] for bit in range(levels - 1, -1, -1) if bit != orders[number][0])
+        total = kept[number][spot] + landing[number * levels + levels - 1][...].astype(jnp.float32)
+        sums[number][half(number, core)] = total
+        share(number, core).start()
+        rows, width = total.shape
+        for row in range(0, rows, 8):
+            for column in range(0, width, 128):
+                part = total[row : row + 8, column : column + 128]
+                squares = squares + part * part
+    stats_out[0:8, :] = squares
+    stats_out[8:16, :] = stats_in[...]
+    add_up(me, own, core, levels, stats_out, stats_land, stats_send, stats_recv)
+    for number in range(count):
+        pair(number).wait_send()
+        for stage in range(levels):
+            hop(number, stage).wait_send()
+        share(number, core).wait_send()
+        share(number, 1 - core).wait_recv()
+
+
+def reduce_rows(grads, stats, devices, turns):
+    levels, count = bit_count(devices), len(grads)
+    lead = (2,) * levels
+    dma = pltpu.SemaphoreType.DMA
+    shapes = [grad.shape[levels:] for grad in grads]
+    halves = [(rows, columns // 2) for rows, columns in shapes]
+    kinds = [grad.dtype for grad in grads]
+    scratch = [pltpu.VMEM(lead + shape, kind) for shape, kind in zip(halves, kinds)] * 2
+    scratch += [pltpu.VMEM(lead[1:] + shape, jnp.float32) for shape in halves]
+    for shape, kind in zip(halves, kinds):
+        for stage in range(levels):
+            scratch.append(pltpu.VMEM((2,) * (levels - 1 - stage) + shape, kind))
+    scratch.append(pltpu.VMEM((levels + 1, 16, 128), jnp.float32))
+    scratch += [dma((count,))] * 3 + [dma((count, levels))] * 2 + [dma((count,))] * 2
+    scratch += [dma((levels + 1,))] * 2
+    vmem = pl.BlockSpec(memory_space=pltpu.VMEM)
+    found = pl.pallas_call(
+        functools.partial(reduce_kernel, levels, turns, count),
+        out_shape=[jax.ShapeDtypeStruct(shape, jnp.float32) for shape in shapes]
+        + [jax.ShapeDtypeStruct((16, 128), jnp.float32)],
+        in_specs=[pl.BlockSpec(memory_space=pl.ANY)] * count + [vmem],
+        out_specs=[vmem] * (count + 1),
+        scratch_shapes=scratch,
+        compiler_params=pltpu.CompilerParams(
+            collective_id=2, has_side_effects=True, vmem_limit_bytes=56 * 2**20
+        ),
+        name="reduce_rows",
+    )(*grads, stats)
+    return found[:count], found[count]
+def send_kernel(owners, count, devices, *refs):
+    rows, wholes = refs[:count], refs[count : 2 * count]
+    here_sem, send_sem, recv_sem, cross_send, cross_recv = refs[2 * count :]
+    me, core = lax.axis_index("dp"), lax.axis_index("mp")
+    barrier = pltpu.get_barrier_semaphore()
+    owning = functools.reduce(jnp.logical_or, [me == owner for owner in owners])
+
+    @pl.when(owning)
+    def greet_all():
+        @pl.loop(0, devices)
+        def greet_one(other):
+            @pl.when(other != me)
+            def signal_one():
+                pl.semaphore_signal(
+                    barrier, inc=1, device_id={"dp": other, "mp": core}, device_id_type=MESH_ID
+                )
+
+        pl.semaphore_signal(
+            barrier, inc=1, device_id={"dp": me, "mp": 1 - core}, device_id_type=MESH_ID
+        )
+        pl.semaphore_wait(barrier, count)
+
+    @pl.when(jnp.logical_not(owning))
+    def wait_owners():
+        pl.semaphore_wait(barrier, count)
+
+    def half(number, which):
+        width = rows[number].shape[1] // 2
+        return (slice(None), pl.ds(pl.multiple_of(which * width, 128), width))
+
+    def hop(number, source):
+        return pltpu.make_async_remote_copy(
+            src_ref=rows[number].at[half(number, core)],
+            dst_ref=wholes[number].at[(source,) + half(number, core)],
+            send_sem=send_sem.at[number],
+            recv_sem=recv_sem.at[number, source],
+            device_id={"dp": owners[number], "mp": core},
+            device_id_type=MESH_ID,
+        )
+
+    def cross(number, source, which):
+        region = wholes[number].at[(source,) + half(number, which)]
+        return pltpu.make_async_remote_copy(
+            src_ref=region,
+            dst_ref=region,
+            send_sem=cross_send.at[number, source],
+            recv_sem=cross_recv.at[number, source],
+            device_id={"dp": me, "mp": 1 - core},
+            device_id_type=MESH_ID,
+        )
+
+    for number in range(count):
+
+        @pl.when(me != owners[number])
+        def start_one(number=number):
+            hop(number, me).start()
+
+    for number in range(count):
+
+        @pl.when(me == owners[number])
+        def collect(number=number):
+            own = pltpu.make_async_copy(rows[number], wholes[number].at[me], here_sem)
+            own.start()
+
+            @pl.loop(0, devices)
+            def forward(source):
+                @pl.when(source != me)
+                def forward_one():
+                    hop(number, source).wait_recv()
+                    cross(number, source, core).start()
+
+            own.wait()
+
+            @pl.loop(0, devices)
+            def finish(source):
+                @pl.when(source != me)
+                def finish_one():
+                    cross(number, source, core).wait_send()
+                    cross(number, source, 1 - core).wait_recv()
+
+    for number in range(count):
+
+        @pl.when(me != owners[number])
+        def end_one(number=number):
+            hop(number, me).wait_send()
+
+
+def send_to_owners(rows, owners, devices):
+    count = len(rows)
+    dma = pltpu.SemaphoreType.DMA
+    return pl.pallas_call(
+        functools.partial(send_kernel, owners, count, devices),
+        out_shape=[jax.ShapeDtypeStruct((devices,) + row.shape, row.dtype) for row in rows],
+        in_specs=[pl.BlockSpec(memory_space=pl.ANY)] * count,
+        out_specs=[pl.BlockSpec(memory_space=pl.ANY)] * count,
+        scratch_shapes=[dma, dma((count,))] + [dma((count, devices))] * 3,
+        compiler_params=pltpu.CompilerParams(collective_id=3, has_side_effects=True),
+        name="send_to_owners",
+    )(*rows)
+
+
+def return_kernel(owners, count, devices, *refs):
+    wholes, rows = refs[:count], refs[count : 2 * count]
+    here_sem, send_sem, recv_sem, cross_send, cross_recv = refs[2 * count :]
+    me, core = lax.axis_index("dp"), lax.axis_index("mp")
+    barrier = pltpu.get_barrier_semaphore()
+    owning = functools.reduce(jnp.logical_or, [me == owner for owner in owners])
+    for owner in owners:
+
+        @pl.when(me != owner)
+        def greet_owner(owner=owner):
+            pl.semaphore_signal(
+                barrier, inc=1, device_id={"dp": owner, "mp": core}, device_id_type=MESH_ID
+            )
+
+    pl.semaphore_signal(barrier, inc=1, device_id={"dp": me, "mp": 1 - core}, device_id_type=MESH_ID)
+
+    @pl.when(owning)
+    def wait_all():
+        pl.semaphore_wait(barrier, devices)
+
+    @pl.when(jnp.logical_not(owning))
+    def wait_pair():
+        pl.semaphore_wait(barrier, 1)
+
+    def half(number, which):
+        width = rows[number].shape[1] // 2
+        return (slice(None), pl.ds(pl.multiple_of(which * width, 128), width))
+
+    def hop(number, target):
+        return pltpu.make_async_remote_copy(
+            src_ref=wholes[number].at[(target,) + half(number, core)],
+            dst_ref=rows[number].at[half(number, core)],
+            send_sem=send_sem.at[number, target],
+            recv_sem=recv_sem.at[number],
+            device_id={"dp": target, "mp": core},
+            device_id_type=MESH_ID,
+        )
+
+    def cross(number, which):
+        region = rows[number].at[half(number, which)]
+        return pltpu.make_async_remote_copy(
+            src_ref=region,
+            dst_ref=region,
+            send_sem=cross_send.at[number],
+            recv_sem=cross_recv.at[number],
+            device_id={"dp": me, "mp": 1 - core},
+            device_id_type=MESH_ID,
+        )
+
+    for number in range(count):
+
+        @pl.when(me == owners[number])
+        def hand_out(number=number):
+            own = pltpu.make_async_copy(
+                wholes[number].at[(me,) + half(number, core)], rows[number].at[half(number, core)], here_sem
+            )
+            own.start()
+
+            @pl.loop(0, devices)
+            def start_one(target):
+                @pl.when(target != me)
+                def start_other():
+                    hop(number, target).start()
+
+            own.wait()
+
+    for number in range(count):
+
+        @pl.when(me != owners[number])
+        def arrive(number=number):
+            hop(number, me).wait_recv()
+
+        cross(number, core).start()
+    for number in range(count):
+        cross(number, core).wait_send()
+        cross(number, 1 - core).wait_recv()
+
+        @pl.when(me == owners[number])
+        def end_out(number=number):
+            @pl.loop(0, devices)
+            def end_one(target):
+                @pl.when(target != me)
+                def end_other():
+                    hop(number, target).wait_send()
+
+
+def return_rows(wholes, owners, devices):
+    count = len(wholes)
+    dma = pltpu.SemaphoreType.DMA
+    return pl.pallas_call(
+        functools.partial(return_kernel, owners, count, devices),
+        out_shape=[jax.ShapeDtypeStruct(whole.shape[1:], whole.dtype) for whole in wholes],
+        in_specs=[pl.BlockSpec(memory_space=pl.ANY)] * count,
+        out_specs=[pl.BlockSpec(memory_space=pltpu.VMEM)] * count,
+        scratch_shapes=[dma, dma((count, devices)), dma((count,)), dma((count,)), dma((count,))],
+        compiler_params=pltpu.CompilerParams(collective_id=4, has_side_effects=True),
+        name="return_rows",
+    )(*wholes)
+
+
+def muon_kernel(owners, shapes, *refs):
+    count = len(owners)
+    mats, outs = refs[:count], refs[count : 2 * count]
+    exact, wide, wide_low, tall, wide_out, tall_out, gram, square, poly, chain, left, right, sem = refs[2 * count :]
+    me, core = lax.axis_index("dp"), lax.axis_index("mp")
+    side = gram.shape[0]
+    step = 256
+    bf = jnp.bfloat16
+
+    def dims(number):
+        height, breadth = shapes[number]
+        return height, breadth, LONG_COLS[number]
+
+    def span(index):
+        return pl.ds(pl.multiple_of(index * step, step), step)
+
+    def split(value):
+        high = value.astype(bf)
+        return high, (value - high.astype(jnp.float32)).astype(bf)
+
+    gram[...] = jnp.zeros_like(gram)
+    for number in range(count):
+
+        @pl.when(me == owners[number])
+        def start(number=number):
+            height, breadth, long_cols = dims(number)
+            short = min(height, breadth)
+            held = (wide if long_cols else tall).at[:height, :breadth]
+            fine = mats[number].dtype == jnp.float32
+            load = pltpu.make_async_copy(mats[number], exact if fine else held, sem)
+            load.start()
+            load.wait()
+            if fine:
+                rest = wide_low
+
+                @pl.loop(0, height // step)
+                def part_rows(index):
+                    high, low = split(exact[span(index), :])
+                    held[span(index), :] = high
+                    rest[span(index), :] = low
+
+            @pl.loop(0, short // step)
+            def gram_rows(index):
+                if long_cols:
+                    part = held[span(index), :]
+                    dims_in = (((1,), (1,)), ((), ()))
+                else:
+                    part = held[:, span(index)]
+                    dims_in = (((0,), (0,)), ((), ()))
+                total = lax.dot_general(part, held[...], dims_in, preferred_element_type=jnp.float32)
+                if fine:
+                    total = total + lax.dot_general(
+                        part, rest[...], dims_in, preferred_element_type=jnp.float32
+                    )
+                    total = total + lax.dot_general(
+                        rest[span(index), :], held[...], dims_in, preferred_element_type=jnp.float32
+                    )
+                gram[span(index), :short] = total
+
+    owning = functools.reduce(jnp.logical_or, [me == owner for owner in owners])
+
+    @pl.when(owning)
+    def iterate():
+        def eye(index):
+            row = lax.broadcasted_iota(jnp.int32, (step, side), 0) + index * step
+            column = lax.broadcasted_iota(jnp.int32, (step, side), 1)
+            return row == column
+
+        trace = jnp.float32(0.0)
+        for index in range(side // step):
+            trace = trace + jnp.sum(jnp.where(eye(index), gram[index * step : (index + 1) * step, :], 0.0))
+        scale = 1.0 / (jnp.sqrt(jnp.full((8, 128), trace, jnp.float32)) + 1e-07)
+        scale = scale[0:1, 0:1]
+        square_scale = scale * scale
+
+        @pl.loop(0, side // step)
+        def prepare(index):
+            gram[span(index), :] = gram[span(index), :] * square_scale
+
+        def set_left(source):
+            @pl.loop(0, side // step)
+            def set_rows(index):
+                high, low = split(source[span(index), :])
+                left[span(index), 0:side] = high
+                left[span(index), side : 2 * side] = high
+                left[span(index), 2 * side : 3 * side] = low
+
+        def set_right(source):
+            @pl.loop(0, side // step)
+            def set_rows(index):
+                high, low = split(source[span(index), :])
+                right[pl.ds(pl.multiple_of(index * step, step), step), :] = high
+                right[pl.ds(pl.multiple_of(side + index * step, step), step), :] = low
+                right[pl.ds(pl.multiple_of(2 * side + index * step, step), step), :] = high
+
+        def multiply(target):
+            @pl.loop(0, side // step)
+            def rows(index):
+                target[span(index), :] = jnp.dot(
+                    left[span(index), :], right[...], preferred_element_type=jnp.float32
+                )
+
+        @pl.loop(0, NS_ITERS)
+        def newton(iteration):
+            set_left(gram)
+            set_right(gram)
+            multiply(square)
+
+            @pl.loop(0, side // step)
+            def polynomial(index):
+                ones = jnp.where(
+                    lax.broadcasted_iota(jnp.int32, (step, side), 0) + index * step
+                    == lax.broadcasted_iota(jnp.int32, (step, side), 1),
+                    NS_A,
+                    0.0,
+                )
+                poly[span(index), :] = ones + NS_B * gram[span(index), :] + NS_C * square[span(index), :]
+
+            set_right(poly)
+
+            @pl.when(iteration < NS_ITERS - 1)
+            def advance():
+                multiply(square)
+                set_left(square)
+                multiply(gram)
+
+            @pl.when(iteration == 0)
+            def first():
+                chain[...] = poly[...]
+
+            @pl.when(iteration > 0)
+            def later():
+                set_left(chain)
+                multiply(chain)
+
+        @pl.loop(0, side // step)
+        def finish(index):
+            high, low = split(chain[span(index), :] * scale)
+            left[span(index), 0:side] = high
+            left[span(index), side : 2 * side] = low
+
+    for number in range(count):
+
+        @pl.when(me == owners[number])
+        def end(number=number):
+            height, breadth, long_cols = dims(number)
+            short = min(height, breadth)
+            width = breadth // 2
+            part = pl.ds(pl.multiple_of(core * width, 128), width)
+            if long_cols:
+                held, made = wide.at[:height, :breadth], wide_out.at[:height, :width]
+
+                @pl.loop(0, height // step)
+                def wide_rows(index):
+                    total = jnp.dot(
+                        left[span(index), :short], held[:, part], preferred_element_type=jnp.float32
+                    ) + jnp.dot(
+                        left[span(index), side : side + short],
+                        held[:, part],
+                        preferred_element_type=jnp.float32,
+                    )
+                    if mats[number].dtype == jnp.float32:
+                        total = total + jnp.dot(
+                            left[span(index), :short],
+                            wide_low[:, part],
+                            preferred_element_type=jnp.float32,
+                        )
+                    made[span(index), :] = total.astype(bf)
+            else:
+                held, made = tall.at[:height, :breadth], tall_out.at[:height, :width]
+
+                @pl.loop(0, height // step)
+                def tall_rows(index):
+                    low = pl.ds(pl.multiple_of(side + core * width, 128), width)
+                    total = jnp.dot(
+                        held[span(index), :], left[:short, part], preferred_element_type=jnp.float32
+                    ) + jnp.dot(
+                        held[span(index), :], left[:short, low], preferred_element_type=jnp.float32
+                    )
+                    made[span(index), :] = total.astype(bf)
+
+            save = pltpu.make_async_copy(made, outs[number].at[:, part], sem)
+            save.start()
+            save.wait()
+
+
+def orthogonalize(mats, owners):
+    count = len(mats)
+    shapes = [mat.shape for mat in mats]
+    side = max(min(shape) for shape in shapes)
+    longest = max(max(shape) for shape in shapes)
+    square = pltpu.VMEM((side, side), jnp.float32)
+    (fine,) = [mat.shape for mat in mats if mat.dtype == jnp.float32]
+    return pl.pallas_call(
+        functools.partial(muon_kernel, owners, shapes),
+        out_shape=[jax.ShapeDtypeStruct(shape, jnp.bfloat16) for shape in shapes],
+        in_specs=[pl.BlockSpec(memory_space=pl.ANY)] * count,
+        out_specs=[pl.BlockSpec(memory_space=pl.ANY)] * count,
+        scratch_shapes=[
+            pltpu.VMEM(fine, jnp.float32),
+            pltpu.VMEM((side, longest), jnp.bfloat16),
+            pltpu.VMEM(fine, jnp.bfloat16),
+            pltpu.VMEM((longest, side), jnp.bfloat16),
+            pltpu.VMEM((side, longest // 2), jnp.bfloat16),
+            pltpu.VMEM((longest, side // 2), jnp.bfloat16),
+            square,
+            square,
+            square,
+            square,
+            pltpu.VMEM((side, 3 * side), jnp.bfloat16),
+            pltpu.VMEM((3 * side, side), jnp.bfloat16),
+            pltpu.SemaphoreType.DMA,
+        ],
+        compiler_params=pltpu.CompilerParams(vmem_limit_bytes=56 * 2**20),
+        name="orthogonalize",
+    )(*mats)
+
+
+def window_place(position):
+    time_row = (position // GF + GT - SHIFT) % GT
+    freq_col = (position % GF + GF - SHIFT) % GF
+    window = (time_row // WIN) * (GF // WIN) + freq_col // WIN
+    return window * (WIN * WIN) + (time_row % WIN) * WIN + freq_col % WIN
+
+
+def window_sinusoid(channels):
+    quarter = channels // 4
+    frequency = 1.0 / 10000.0 ** (np.arange(quarter) / quarter)
+    position = np.arange(NPATCH)
+    time_rows = (position // GF)[:, None] * frequency
+    freq_cols = (position % GF)[:, None] * frequency
+    table = np.concatenate([np.sin(time_rows), np.cos(time_rows), np.sin(freq_cols), np.cos(freq_cols)], axis=1)
+    moved = np.zeros_like(table)
+    moved[window_place(position)] = table
+    return moved.astype(np.float32)
+
+
+def window_patches(spec):
+    grid = spec.reshape(spec.shape[0], GT, PS, GF, PS)
+    grid = jnp.roll(grid, (-SHIFT, -SHIFT), axis=(1, 3))
+    grid = grid.reshape(spec.shape[0], GT // WIN, WIN, PS, GF // WIN, WIN, PS)
+    return grid.transpose(0, 1, 4, 2, 5, 3, 6).reshape(spec.shape[0], NPATCH, PATCH)
+
+
+@jax.custom_vjp
+def times(inputs, matrix):
+    return jnp.dot(inputs.astype(jnp.bfloat16), matrix.astype(jnp.bfloat16), preferred_element_type=jnp.float32)
+
+
+def times_keep(inputs, matrix):
+    short = inputs.astype(jnp.bfloat16)
+    return jnp.dot(short, matrix.astype(jnp.bfloat16), preferred_element_type=jnp.float32), (short, matrix)
+
+
+def times_back(kept, grad):
+    short, matrix = kept
+    grad = grad.astype(jnp.bfloat16)
+    back = lax.dot_general(
+        grad, matrix.astype(jnp.bfloat16), (((1,), (1,)), ((), ())), preferred_element_type=jnp.float32
+    )
+    gain = lax.dot_general(short, grad, (((0,), (0,)), ((), ())), preferred_element_type=jnp.float32)
+    return back, gain.astype(matrix.dtype)
+
+
+times.defvjp(times_keep, times_back)
+
+
+def pair_product(spec, left_spec, right_spec):
+    @jax.custom_vjp
+    def apply(left, right):
+        return jnp.einsum(
+            spec, left.astype(jnp.bfloat16), right.astype(jnp.bfloat16), preferred_element_type=jnp.float32
+        )
+
+    def keep(left, right):
+        left, right = left.astype(jnp.bfloat16), right.astype(jnp.bfloat16)
+        return jnp.einsum(spec, left, right, preferred_element_type=jnp.float32), (left, right)
+
+    def back(kept, grad):
+        left, right = kept
+        grad = grad.astype(jnp.bfloat16)
+        return (
+            jnp.einsum(left_spec, grad, right, preferred_element_type=jnp.float32),
+            jnp.einsum(right_spec, grad, left, preferred_element_type=jnp.float32),
+        )
+
+    apply.defvjp(keep, back)
+    return apply
+
+
+scores_of = pair_product("bqhd,bkhd->bhqk", "bhqk,bkhd->bqhd", "bhqk,bqhd->bkhd")
+mix_of = pair_product("bhqk,bkhd->bqhd", "bqhd,bkhd->bhqk", "bqhd,bhqk->bkhd")
+
+
+def attend_short(queries, key_rows, values, allowed, scaling):
+    scores = scores_of(queries, key_rows) * scaling
+    scores = jnp.where(allowed, scores, -1e30)
+    scores = scores - jnp.max(scores, axis=-1, keepdims=True)
+    exponent = jnp.exp(scores)
+    return mix_of(exponent / jnp.sum(exponent, axis=-1, keepdims=True), values)
+
+
+def local_loss(weights, patches, keep, counts):
+    clips = patches.shape[0]
+    pieces = unpack(weights[10])
+    keep = jnp.pad(keep, ((0, 0), (0, SLOTS - VIS)))
+    spot = window_place(keep)
+    chosen = (spot[:, :, None] == jnp.arange(NPATCH)[None, None, :]).astype(jnp.float32)
+    shown = chosen * (jnp.arange(SLOTS)[None, :] < counts[:, None])[:, :, None]
+    picked = jnp.einsum("cjp,cpv->cjv", chosen.astype(jnp.bfloat16), patches, preferred_element_type=jnp.float32)
+    where = jnp.einsum("cjp,pd->cjd", chosen, window_sinusoid(D), precision=HIGH)
+    hidden = times(picked.reshape(-1, PATCH), weights[8][:, :D]) + pieces[11] + where.reshape(-1, D)
+    normed = layer_norm(hidden, pieces[0], pieces[1])
+    joined = times(normed, weights[0])
+    queries = (joined[:, :D] + pieces[2]).reshape(clips, SLOTS, HEADS, HEAD)
+    key_rows = joined[:, D : 2 * D].reshape(clips, SLOTS, HEADS, HEAD)
+    values = (joined[:, 2 * D :] + pieces[3]).reshape(clips, SLOTS, HEADS, HEAD)
+    visible = (jnp.arange(SLOTS)[None, :] < counts[:, None])[:, None, None, :]
+    attended = attend_short(queries, key_rows, values, visible, HEAD ** (-0.5)).reshape(-1, D)
+    hidden = hidden + times(attended, weights[1]) + pieces[4]
+    normed = layer_norm(hidden, pieces[5], pieces[6])
+    inner = jax.nn.gelu(times(normed, weights[2]) + pieces[7], approximate=False)
+    hidden = hidden + times(inner, weights[3]) + pieces[8]
+    latent = layer_norm(hidden, pieces[9], pieces[10])
+
+    pieces = pieces[12:]
+    placed = times(latent, weights[9]) + pieces[0]
+    filled = jnp.einsum("cjp,cjd->cpd", shown, placed.reshape(clips, SLOTS, DD), precision=HIGH)
+    cells = jnp.sum(shown, axis=1)
+    hidden = filled + (1.0 - cells)[..., None] * pieces[1] + window_sinusoid(DD)
+    hidden = hidden.reshape(-1, DD)
+    normed = layer_norm(hidden, pieces[2], pieces[3])
+    windows = times(normed, weights[4])
+    queries = (windows[:, :DD] + pieces[4]).reshape(-1, WIN * WIN, DHEADS, DHEAD)
+    key_rows = windows[:, DD : 2 * DD].reshape(-1, WIN * WIN, DHEADS, DHEAD)
+    values = (windows[:, 2 * DD :] + pieces[5]).reshape(-1, WIN * WIN, DHEADS, DHEAD)
+    allowed = jnp.tile(window_mask(), (clips, 1, 1))[:, None, :, :]
+    attended = attend_short(queries, key_rows, values, allowed, DHEAD ** (-0.5)).reshape(-1, DD)
+    hidden = hidden + times(attended, weights[5]) + pieces[6]
+    normed = layer_norm(hidden, pieces[7], pieces[8])
+    inner = jax.nn.gelu(times(normed, weights[6]) + pieces[9], approximate=False)
+    hidden = hidden + times(inner, weights[7]) + pieces[10]
+    normed = layer_norm(hidden, pieces[11], pieces[12])
+    predicted = times(normed, weights[8][:, D:].T) + pieces[13]
+    patches = patches.astype(jnp.float32).reshape(-1, PATCH)
+    centred = patches - jnp.mean(patches, axis=-1, keepdims=True)
+    target = centred * lax.rsqrt(jnp.mean(centred * centred, axis=-1, keepdims=True) + 1e-06)
+    deviation = predicted - target
+    patch_error = jnp.mean(deviation * deviation, axis=-1)
+    return jnp.sum((1.0 - cells.reshape(-1)) * patch_error)
+
+
+def quick_body(
+    spectrogram, keep, counts, *rest
+):
+    masters = rest[:8] + (rest[16], rest[19], rest[22])
+    moments = rest[8:16]
+    devices = lax.axis_size("dp")
+    lead = (2,) * bit_count(devices)
+    own = [weight.astype(jnp.bfloat16) for weight in masters]
+    vector_rows = own[10].shape[0]
+    spare = VEC_ROWS * VEC_COLS
+    own[10] = jnp.pad(own[10], (0, spare - vector_rows)).reshape(VEC_ROWS, VEC_COLS)
+    row = lax.broadcasted_iota(jnp.int32, (8, 128), 0)
+    column = lax.broadcasted_iota(jnp.int32, (8, 128), 1)
+    first = jnp.logical_and(row == 0, column == 0)
+    count_part = jnp.sum(NPATCH - counts).astype(jnp.float32)
+    gathered, tally = gather_rows(own, jnp.where(first, count_part, 0.0), devices, GATHER_TURNS)
+    mask_count = tally[0, 0]
+    weights = [piece.reshape(-1, piece.shape[-1]) for piece in gathered[:10]]
+    weights[4] = weights[4].astype(jnp.float32)
+    vectors = gathered[10].reshape(devices, spare)[:, :vector_rows].reshape(-1).astype(jnp.float32)
+    patches = window_patches(spectrogram)
+    loss_part, pull = jax.vjp(
+        lambda *params: local_loss(params, patches, keep, counts), *weights, vectors
+    )
+    grads = list(pull(1.0 / mask_count))
+    grads[10] = jnp.pad(grads[10].reshape(devices, vector_rows), ((0, 0), (0, spare - vector_rows)))
+    grads[10] = grads[10].reshape(lead + (VEC_ROWS, VEC_COLS))
+    for number in range(10):
+        grad = grads[number]
+        grads[number] = grad.reshape(lead + (grad.shape[0] // devices, grad.shape[1]))
+    reduced, stats = reduce_rows(grads, jnp.where(first, loss_part, 0.0), devices, REDUCE_TURNS)
+    reduced = list(reduced)
+    reduced[10] = reduced[10].reshape(-1)[:vector_rows]
+    loss_sum = stats[8, 0]
+    grad_norm = jnp.sqrt(jnp.sum(stats[:8]))
+    factor = jnp.minimum(1.0, CLIP_MAX / (grad_norm + 1e-06))
+    clipped = [gradient * factor for gradient in reduced]
+    renewed = [0.5 * moments[number] + clipped[number] for number in range(8)]
+    sent = [piece if number == 4 else piece.astype(jnp.bfloat16) for number, piece in enumerate(renewed)]
+    collected = send_to_owners(sent, OWNERS, devices)
+    made = orthogonalize([piece.reshape(-1, piece.shape[2]) for piece in collected], OWNERS)
+    made = [piece.reshape(devices, -1, piece.shape[1]) for piece in made]
+    whole = return_rows(made, OWNERS, devices)
+    new_weights = []
+    for number in range(8):
+        height, breadth = masters[number].shape
+        step_rate = LR_MUON * 0.2 * math.sqrt(max(height * devices, breadth))
+        new_weights.append(
+            masters[number] * (1.0 - LR_MUON * DECAY) - step_rate * whole[number].astype(jnp.float32)
+        )
+    patch_new = adam_update(*rest[16:19], clipped[8], DECAY)
+    embed_new = adam_update(*rest[19:22], clipped[9], DECAY)
+    vector_new = adam_update(*rest[22:25], clipped[10], 0.0)
+    return (loss_sum, mask_count, grad_norm, *new_weights, *renewed, *patch_new, *embed_new, *vector_new)
 
 
 def body(
@@ -541,7 +1466,7 @@
         P("dp"),
     )
     return jax.shard_map(
-        body,
+        quick_body if mesh.shape["dp"] == 16 else body,
         mesh=mesh,
         in_specs=placed,
         out_specs=(

time: 3320 us -> 941 us (0.28)
  the two profiles are of different devices: /device:TPU:15 before, /device:TPU:31 now
where the time goes in v1:
time: 941 us; the launch traced here: 929 us
  Pallas kernels  446 us (47%)
  matrix products  197 us (21%)
  local copies, waits for them, and re-layouts  183 us (19%)
  other arithmetic  96.5 us (10%)
    pallas_call x1, Pallas kernels, gather_rows(): pl.pallas_call(functools.partial(gather_kernel, levels, turns, count), ou...  148 us
    pallas_call x1, Pallas kernels, reduce_rows(): pl.pallas_call(functools.partial(reduce_kernel, levels, turns, count), ou...  138 us
    pallas_call x1, Pallas kernels, return_rows(): pl.pallas_call(functools.partial(return_kernel, owners, count, devices),...  137 us
    dot_general x11, matrix products, times_keep(): jnp.dot(short, matrix.astype(jnp.bfloat16), preferred_element_type=jnp.fl...  53.1 us
    transpose x4, local copies, waits for them, and re-layouts, attend_short(): scores = scores_of(queries, key_rows) * scaling  27.4 us
    convert_element_type x9, local copies, waits for them, and re-layouts, keep(): left, right = (left.astype(jnp.bfloat16), right.astype(jnp.bfloat16))  26.1 us
    dot_general x4, matrix products, attend_short(): return mix_of(exponent / jnp.sum(exponent, axis=-1, keepdims=True), values)  24.5 us
    pallas_call x1, Pallas kernels, send_to_owners(): pl.pallas_call(functools.partial(send_kernel, owners, count, devices), ou...  23.2 us

profile of v1, /device:TPU:31, one launch (start us, length us, event | category | flops | bytes accessed | tf_op | source)
XLA Modules:
  0.0 929.1 jit_solution(4616573816714349755)
XLA Ops:
  41.5 6.9 copy.150
  71.8 6.7 copy.165
  78.5 7.0 reshape.768
  85.5 147.7 %gather_rows.1 = (bf16[2,2,2,2,48,2304]{5,4,3,2,1,0:T(8,128)(2,1)}, bf16[2,2,2,2,48,768]{5,4,3,2,1,0:T(8,128)(2,1)}, bf16[2,2,2,2,48,3072]{5,4,3,2,1,0:T(8,128)(...) custom-call(bf16[48,2304]{1,0:T(8,128)(2,1)} %convert_element_type.3, ...), custom_call_target="tpu_custom_call" | custom-call | tf_op jit(solution)/shard_map/gather_rows/pallas_call | solution.py:429
  267.7 13.4 %multiply_convert_fusion.3 = (bf16[320,3072]{1,0:T(8,128)(2,1)S(1)}, f32[320,3072]{1,0:T(8,128)}, f32[320,3072]{1,0:T(8,128)}) fusion(f32[3072]{0:T(1024)S(1)} %slice.195, bf16[768,3072]{1,0:T(8,128)(2,1)} %bitcast.267, f32[320,768]{1,0:T(8,128)S(1)} %get-tuple-element.246, f32[768]{0:T(1024)S(1)} %get-tuple-element.224, f32[768]{0:T(1024)S(1)} %get-tuple-element.225, ...), kind=kOutput, calls=%fused_computation.41 | convolution fusion | flops 1576058880 | bytes 15553024 | tf_op jit(solution)/shard_map/jvp()/dot_general | solution.py:1052
  308.9 6.8 fusion.7
  330.9 6.8 convert_element_type.382
  340.5 22.7 %multiply_convert_fusion.1 = (bf16[1024,2048]{1,0:T(8,128)(2,1)S(1)}, f32[1024,2048]{1,0:T(8,128)}, f32[1024,2048]{1,0:T(8,128)}) fusion(f32[2048]{0:T(1024)S(1)} %slice.211, bf16[512,2048]{1,0:T(8,128)(2,1)S(1)} %bitcast.279, f32[1024,512]{1,0:T(8,128)S(1)} %get-tuple-element.255, f32[512]{0:T(512)S(1)} %copy-done.152, f32[512]{0:T(512)S(1)} %get-tuple-element.213, ...), kind=kOutput, calls=%fused_computation.8 | convolution fusion | flops 2288517120 | bytes 25186304 | tf_op jit(solution)/shard_map/jvp()/dot_general | solution.py:1052
  374.2 9.5 %fusion.148 = (f32[2048]{0:T(1024)}, bf16[1024,2048]{1,0:T(8,128)(2,1)S(1)}) fusion(f32[1024,2048]{1,0:T(8,128)} %get-tuple-element.193, bf16[2048,512]{1,0:T(8,128)(2,1)S(1)} %bitcast.282, f32[1024,512]{1,0:T(8,128)S(1)} %get-tuple-element.191, f32[1024]{0:T(1024)S(1)} %negate_multiply_fusion.4, f32[1024,2048]{1,0:T(8,128)} %get-tuple-element.256, ...), kind=kOutput, calls=%fused_computation.354 | convolution fusion | flops 2182084608 | bytes 25186304 | tf_op jit(solution)/shard_map/transpose(jvp())/dot_general | solution.py:1142
  402.7 14.7 %convert_reduce_fusion = (f32[64,16,16]{2,1,0:T(8,128)}, pred[64,16,16,16]{2,3,1,0:T(8,128)(4,1)}, f32[64,16,16]{2,1,0:T(8,128)}, f32[64,16,16,16]{2,3,1,0:T(8,128)}) fusion(f32[64,16,16]{2,1,0:T(8,128)S(1)} %get-tuple-element.252, f32[64,16,16,16]{2,3,1,0:T(8,128)S(1)} %bitcast.201, pred[64,16,16]{1,2,0:T(8,128)(4,1)S(1)} %bitcast.219, ...), kind=kOutput, calls=%fused_computation.3 | convolution fusion | flops 19103744 | bytes 4734976 | tf_op jit(solution)/shard_map/transpose(jvp(bqhd,bkhd->bhqk))/dot_general | solution.py:1100
  418.5 9.0 fusion.128
  434.8 11.2 %fusion.25 = f32[64,16,16,32]{3,1,2,0:T(8,128)} fusion(bf16[64,16,16,32]{3,2,1,0:T(8,128)(2,1)} %convert_element_type.377, f32[64,16,16,16]{2,3,1,0:T(8,128)} %get-tuple-element.185, pred[64,16,16,16]{2,3,1,0:T(8,128)(4,1)} %get-tuple-element.187, f32[64,16,16]{2,1,0:T(8,128)S(1)} %negate_divide_fusion, pred[64,16,16]{1,2,0:T(8,128)(4,1)S(1)} %bitcast.222), kind=kOutput, calls=%fused_computation.70 | convolution fusion | flops 18087936 | bytes 4538368 | tf_op jit(solution)/shard_map/transpose(jvp(bhqk,bqhd->bkhd))/dot_general | solution.py:1096
  446.0 8.4 fusion.146
  455.1 10.6 %copy.174 = f32[64,16,16,32]{3,2,1,0:T(8,128)} copy(f32[64,16,16,32]{3,1,2,0:T(8,128)} %fusion.25) | data formatting | bytes 4194304 | tf_op jit(solution)/shard_map/transpose(jvp(bhqk,bqhd->bkhd))/transpose | solution.py:1096
  465.7 7.3 reshape.733
  473.0 10.6 %copy.177 = f32[64,16,16,32]{3,2,1,0:T(8,128)} copy(f32[64,16,16,32]{3,1,2,0:T(8,128)} %get-tuple-element.276) | data formatting | bytes 4194304 | tf_op jit(solution)/shard_map/transpose(jvp(bhqk,bkhd->bqhd))/transpose | solution.py:1096
  483.6 7.5 reshape.734
  491.1 10.6 %copy.171 = f32[64,16,16,32]{3,2,1,0:T(8,128)} copy(f32[64,16,16,32]{3,1,2,0:T(8,128)} %get-tuple-element.278) | data formatting | bytes 4194304 | tf_op jit(solution)/shard_map/transpose(jvp(bqhd,bhqk->bkhd))/transpose | solution.py:1100
  501.7 7.7 reshape.732
  509.5 7.2 multiply_reduce_fusion.4
  541.8 6.6 fusion.31.refs_4_
  597.6 137.8 %reduce_rows.1 = (f32[48,2304]{1,0:T(8,128)}, f32[48,768]{1,0:T(8,128)}, f32[48,3072]{1,0:T(8,128)}, f32[192,768]{1,0:T(8,128)}, f32[32,1536]{1,0:T(8,128)}, /*i...) custom-call(bf16[2,2,2,2,48,2304]{5,4,3,2,1,0:T(8,128)(2,1)} %bitcas, ...), custom_call_target="tpu_custom_call" | custom-call | tf_op jit(solution)/shard_map/reduce_rows/pallas_call | solution.py:587
  754.6 23.2 %send_to_owners.1 = (bf16[16,48,2304]{2,1,0:T(8,128)(2,1)}, bf16[16,48,768]{2,1,0:T(8,128)(2,1)}, bf16[16,48,3072]{2,1,0:T(8,128)(2,1)}, bf16[16,192,768]{2,1,0:...) custom-call(bf16[48,2304]{1,0:T(8,128)(2,1)} %get-tuple-element.164., ...), custom_call_target="tpu_custom_call" | custom-call | tf_op jit(solution)/shard_map/send_to_owners/pallas_call | solution.py:690
  778.4 136.7 %return_rows.1 = (bf16[48,2304]{1,0:T(8,128)(2,1)}, bf16[48,768]{1,0:T(8,128)(2,1)}, bf16[48,3072]{1,0:T(8,128)(2,1)}, bf16[192,768]{1,0:T(8,128)(2,1)}, bf16[32...) custom-call(bf16[16,48,2304]{2,1,0:T(8,128)(2,1)} %bitcast.212, ...), custom_call_target="tpu_custom_call" | custom-call | tf_op jit(solution)/shard_map/return_rows/pallas_call | solution.py:790
  (572 shorter events, 285.8 us)
Async XLA Ops:
  3.6 280.4 %copy-start.83 = (s32[2,160]{1,0:T(2,128)}, s32[2,160]{1,0:T(2,128)S(1)}, u32[]{:S(2)}) copy-start(s32[2,160]{1,0:T(2,128)S(1)} %fusion.91) | copy-start | bytes 3844
  4.3 254.1 %copy-start.78 = (pred[2,160]{1,0:T(4,128)(4,1)}, pred[2,160]{1,0:T(4,128)(4,1)S(1)}, u32[]{:S(2)}) copy-start(pred[2,160]{1,0:T(4,128)(4,1)S(1)} %get-tuple-element.240) | copy-start | bytes 964
  4.3 279.6 %copy-start.88 = (f32[2,160]{1,0:T(2,128)}, f32[2,160]{1,0:T(2,128)S(1)}, u32[]{:S(2)}) copy-start(f32[2,160]{1,0:T(2,128)S(1)} %get-tuple-element.239) | copy-start | bytes 3844
  71.8 166.1 %copy-start.50 = (bf16[2,160,256]{2,1,0:T(8,128)(2,1)}, bf16[2,160,256]{2,1,0:T(8,128)(2,1)S(1)}, u32[]{:S(2)}) copy-start(bf16[2,160,256]{2,1,0:T(8,128)(2,1)S(1)} %convolution_convert_fusion.13) | copy-start | bytes 491524
  78.5 159.5 %copy-start.26 = (f32[2,160,768]{2,1,0:T(8,128)S(1)}, f32[2,160,768]{2,1,0:T(8,128)}, u32[]{:S(2)}) copy-start(f32[2,160,768]{2,1,0:T(8,128)} %fusion.62) | copy-start | bytes 2949124
  237.3 51.5 %copy-start.90 = (f32[512]{0:T(512)}, f32[512]{0:T(512)S(1)}, u32[]{:S(2)}) copy-start(f32[512]{0:T(512)S(1)} %get-tuple-element.218) | copy-start | bytes 6148
  237.3 51.5 %copy-start.120 = (f32[512]{0:T(512)}, f32[512]{0:T(512)S(1)}, u32[]{:S(2)}) copy-start(f32[512]{0:T(512)S(1)} %get-tuple-element.217) | copy-start | bytes 6148
  287.1 50.6 %copy-start.2 = (f32[2,512,512]{2,1,0:T(8,128)}, f32[2,512,512]{2,1,0:T(8,128)S(1)}, u32[]{:S(2)}) copy-start(f32[2,512,512]{2,1,0:T(8,128)S(1)} %get-tuple-element.251) | copy-start | bytes 6291460
  597.5 145.0 %copy-start.72 = (f32[32,1536]{1,0:T(8,128)S(1)}, f32[32,1536]{1,0:T(8,128)}, u32[]{:S(2)}) copy-start(f32[32,1536]{1,0:T(8,128)} %param.45) | copy-start | bytes 589828
  597.5 146.7 %copy-start.63 = (f32[48,2304]{1,0:T(8,128)S(1)}, f32[48,2304]{1,0:T(8,128)}, u32[]{:S(2)}) copy-start(f32[48,2304]{1,0:T(8,128)} %param.41) | copy-start | bytes 1327108
  597.5 148.6 %copy-start.73 = (f32[48,768]{1,0:T(8,128)S(1)}, f32[48,768]{1,0:T(8,128)}, u32[]{:S(2)}) copy-start(f32[48,768]{1,0:T(8,128)} %param.42) | copy-start | bytes 442372
  597.5 150.2 %copy-start.65 = (f32[16,1280]{1,0:T(8,128)S(1)}, f32[16,1280]{1,0:T(8,128)}, u32[]{:S(2)}) copy-start(f32[16,1280]{1,0:T(8,128)} %param.49) | copy-start | bytes 245764
  597.5 150.2 %copy-start.80 = (f32[16,1280]{1,0:T(8,128)S(1)}, f32[16,1280]{1,0:T(8,128)}, u32[]{:S(2)}) copy-start(f32[16,1280]{1,0:T(8,128)} %param.50) | copy-start | bytes 245764
  597.5 150.2 %copy-start.81 = (f32[16,1280]{1,0:T(8,128)S(1)}, f32[16,1280]{1,0:T(8,128)}, u32[]{:S(2)}) copy-start(f32[16,1280]{1,0:T(8,128)} %param.51) | copy-start | bytes 245764
  597.5 151.8 %copy-start.64 = (f32[48,512]{1,0:T(8,128)S(1)}, f32[48,512]{1,0:T(8,128)}, u32[]{:S(2)}) copy-start(f32[48,512]{1,0:T(8,128)} %param.52) | copy-start | bytes 294916
  597.5 151.8 %copy-start.76 = (f32[48,512]{1,0:T(8,128)S(1)}, f32[48,512]{1,0:T(8,128)}, u32[]{:S(2)}) copy-start(f32[48,512]{1,0:T(8,128)} %param.53) | copy-start | bytes 294916
  597.6 151.8 %copy-start.77 = (f32[48,512]{1,0:T(8,128)S(1)}, f32[48,512]{1,0:T(8,128)}, u32[]{:S(2)}) copy-start(f32[48,512]{1,0:T(8,128)} %param.54) | copy-start | bytes 294916
  778.3 136.8 %copy-start.71 = (f32[32,512]{1,0:T(8,128)S(1)}, f32[32,512]{1,0:T(8,128)}, u32[]{:S(2)}) copy-start(f32[32,512]{1,0:T(8,128)} %param.38) | copy-start | bytes 196612
  778.3 138.3 %copy-start.57 = (f32[48,768]{1,0:T(8,128)S(1)}, f32[48,768]{1,0:T(8,128)}, u32[]{:S(2)}) copy-start(f32[48,768]{1,0:T(8,128)} %param.34) | copy-start | bytes 442372
  778.3 139.8 %copy-start.49 = (f32[32,1536]{1,0:T(8,128)S(1)}, f32[32,1536]{1,0:T(8,128)}, u32[]{:S(2)}) copy-start(f32[32,1536]{1,0:T(8,128)} %param.37) | copy-start | bytes 589828
  778.3 141.4 %copy-start.37 = (f32[48,2304]{1,0:T(8,128)S(1)}, f32[48,2304]{1,0:T(8,128)}, u32[]{:S(2)}) copy-start(f32[48,2304]{1,0:T(8,128)} %param.33) | copy-start | bytes 1327108
  778.4 143.2 %copy-start.44 = (f32[32,2048]{1,0:T(8,128)S(1)}, f32[32,2048]{1,0:T(8,128)}, u32[]{:S(2)}) copy-start(f32[32,2048]{1,0:T(8,128)} %param.39) | copy-start | bytes 786436
  778.4 144.8 %copy-start.45 = (f32[128,512]{1,0:T(8,128)S(1)}, f32[128,512]{1,0:T(8,128)}, u32[]{:S(2)}) copy-start(f32[128,512]{1,0:T(8,128)} %param.40) | copy-start | bytes 786436
  778.4 146.5 %copy-start.31 = (f32[48,3072]{1,0:T(8,128)S(1)}, f32[48,3072]{1,0:T(8,128)}, u32[]{:S(2)}) copy-start(f32[48,3072]{1,0:T(8,128)} %param.35) | copy-start | bytes 1769476
  (156 other events, 1004.3 us)

commit v2 on v1

--- a/solution.py
+++ b/solution.py
@@ -286,9 +286,17 @@
 
 MESH_ID = pl.DeviceIdType.MESH
 VEC_ROWS, VEC_COLS = 16, 256
-GATHER_TURNS = (2, 2, 0, 1, 2, 0, 0, 1, 2, 1, 2)
-REDUCE_TURNS = (2, 2, 0, 1, 2, 0, 0, 1, 0, 1, 2)
-OWNERS = (0, 3, 5, 6, 8, 11, 13, 14)
+AXIS_ORDERS = ((3, 2, 1, 0), (3, 2, 0, 1), (0, 3, 2, 1), (1, 3, 2, 0), (0, 1, 3, 2), (1, 0, 3, 2))
+GATHER_PARTS = (3, 1, 4, 4, 1, 1, 2, 2, 1, 1, 1)
+REDUCE_PARTS = (3, 1, 4, 4, 2, 1, 2, 2, 1, 1, 1)
+TALL = (3, 7)
+GATHER_TURNS = (5, 1, 3, 2, 1, 0, 3, 0, 1, 5, 1, 5, 1, 5, 1, 0, 0, 1, 0, 5, 3)
+GATHER_FIRST = (3, 2, 17, 15, 4, 7, 10, 6, 19, 9, 16, 12, 8, 13, 20, 11, 0, 5, 14, 1, 18)
+GATHER_STEPS = ((3, 0), (2, 0), (17, 0), (6, 0), (19, 0), (15, 0), (9, 0), (13, 0), (20, 0), (11, 0), (4, 0), (0, 0), (19, 1), (7, 0), (9, 1), (10, 0), (13, 1), (16, 0), (11, 1), (12, 0), (0, 1), (8, 0), (5, 0), (14, 0), (1, 0), (18, 0), (3, 1), (17, 1), (2, 1), (15, 1), (6, 1), (20, 1), (4, 1), (17, 2), (15, 2), (7, 1), (19, 2), (4, 2), (10, 1), (17, 3), (9, 2), (15, 3), (7, 2), (13, 2), (16, 1), (10, 2), (4, 3), (12, 1), (11, 2), (7, 3), (16, 2), (8, 1), (12, 2), (0, 2), (5, 1), (14, 1), (10, 3), (1, 1), (18, 1), (16, 3), (3, 2), (8, 2), (2, 2), (12, 3), (14, 2), (6, 2), (5, 2), (20, 2), (1, 2), (18, 2), (19, 3), (2, 3), (3, 3), (9, 3), (6, 3), (13, 3), (8, 3), (5, 3), (11, 3), (14, 3), (20, 3), (18, 3), (0, 3), (1, 3))
+REDUCE_TURNS = (1, 0, 1, 1, 1, 1, 2, 1, 0, 1, 4, 0, 3, 2, 2, 3, 3, 3, 5, 4, 3, 0)
+REDUCE_FIRST = (10, 1, 13, 9, 18, 6, 7, 5, 11, 21, 8, 12, 16, 0, 17, 3, 20, 19, 4, 14, 2, 15)
+REDUCE_STEPS = ((10, 0), (1, 0), (13, 0), (18, 0), (11, 0), (21, 0), (9, 0), (10, 1), (13, 1), (8, 0), (6, 0), (18, 1), (19, 0), (12, 0), (7, 0), (13, 2), (6, 1), (19, 1), (16, 0), (5, 0), (12, 1), (1, 1), (6, 2), (17, 0), (16, 1), (20, 0), (1, 2), (0, 0), (12, 2), (17, 1), (15, 0), (16, 2), (20, 1), (3, 0), (1, 3), (9, 1), (18, 2), (17, 2), (15, 1), (4, 0), (7, 1), (13, 3), (20, 2), (9, 2), (11, 1), (5, 1), (6, 3), (15, 2), (7, 2), (14, 0), (21, 1), (9, 3), (11, 2), (0, 1), (5, 2), (7, 3), (3, 1), (14, 1), (21, 2), (2, 0), (11, 3), (0, 2), (10, 2), (4, 1), (5, 3), (3, 2), (8, 1), (14, 2), (21, 3), (19, 2), (2, 1), (12, 3), (10, 3), (0, 3), (16, 3), (4, 2), (18, 3), (14, 3), (17, 3), (19, 3), (20, 3), (3, 3), (15, 3), (8, 2), (2, 2), (4, 3), (8, 3), (2, 3))
+OWNERS = (4, 11, 5, 10, 6, 9, 7, 8)
 SLOTS = 160
 
 
@@ -296,10 +304,16 @@
     return devices.bit_length() - 1
 
 
-def bit_order(levels, turn):
-    down = list(range(levels - 1, -1, -1))
-    turn = turn % levels
-    return down[levels - turn :] + down[: levels - turn]
+def cut_pieces(parts, shapes):
+    found = []
+    for number, count in enumerate(parts):
+        rows, width = shapes[number]
+        for part in range(count):
+            if number in TALL:
+                found.append((number, part * (rows // count), rows // count, 0, width))
+            else:
+                found.append((number, 0, rows, part * (width // count), width // count))
+    return found
 
 
 def own_bits(levels):
@@ -355,135 +369,185 @@
         total[...] = total[...] + landing[stage]
 
 
-def gather_kernel(levels, turns, count, *refs):
+def gather_kernel(levels, pieces, count, *refs):
     shards, tally = refs[:count], refs[count]
     wholes, tally_out = refs[count + 1 : 2 * count + 1], refs[2 * count + 1]
-    here_sem, send_sem, recv_sem, cross_send, cross_recv = refs[2 * count + 2 : 2 * count + 7]
-    tally_land, tally_send, tally_recv = refs[2 * count + 7 :]
+    short, rest = refs[2 * count + 2 : 3 * count + 2], refs[3 * count + 2 :]
+    here_sem, send_sem, recv_sem, cross_send, cross_recv, tally_land, tally_send, tally_recv = rest
     me, own = own_bits(levels)
     core = lax.axis_index("mp")
     greet(me, own, levels, core)
-    orders = [bit_order(levels, turn) for turn in turns]
-
-    def half(number, which):
+    orders = [AXIS_ORDERS[turn] for turn in GATHER_TURNS]
+
+    def cut(piece, which):
+        number, row, rows, column, columns = pieces[piece]
         width = shards[number].shape[1] // 2
-        return (slice(None), pl.ds(pl.multiple_of(which * width, 128), width))
-
-    def hop(number, stage, flip):
-        order = orders[number]
+        return (pl.ds(row, rows), pl.ds(pl.multiple_of(which * width + column, 128), columns))
+
+    def hop(piece, stage, flip):
+        order, number = orders[piece], pieces[piece][0]
         spot = place(levels, order[:stage], own, order[stage] if flip else None)
-        target = wholes[number].at[spot + half(number, core)]
-        source = target if stage or flip else shards[number].at[half(number, core)]
+        target = wholes[number].at[spot + cut(piece, core)]
+        source = target if stage or flip else short[number].at[cut(piece, core)]
         return pltpu.make_async_remote_copy(
             src_ref=source,
             dst_ref=target,
-            send_sem=send_sem.at[number, stage],
-            recv_sem=recv_sem.at[number, stage],
+            send_sem=send_sem.at[piece, stage],
+            recv_sem=recv_sem.at[piece, stage],
             device_id={"dp": partner(me, own, order[stage]), "mp": core},
             device_id_type=MESH_ID,
         )
 
-    def cross(number, stage, which):
-        order = orders[number]
+    def cross(piece, stage, which):
+        order, number = orders[piece], pieces[piece][0]
         spot = place(levels, order[:stage], own, order[stage])
-        target = wholes[number].at[spot + half(number, which)]
+        target = wholes[number].at[spot + cut(piece, which)]
         return pltpu.make_async_remote_copy(
             src_ref=target,
             dst_ref=target,
-            send_sem=cross_send.at[number, stage],
-            recv_sem=cross_recv.at[number, stage],
+            send_sem=cross_send.at[piece, stage],
+            recv_sem=cross_recv.at[piece, stage],
             device_id={"dp": me, "mp": 1 - core},
             device_id_type=MESH_ID,
         )
 
     def keep(number):
         spot = place(levels, (), own)
-        return pltpu.make_async_copy(shards[number], wholes[number].at[spot], here_sem.at[number])
-
-    for number in range(count):
-        hop(number, 0, False).start()
-    for number in range(count):
-        keep(number).start()
+        return pltpu.make_async_copy(short[number], wholes[number].at[spot], here_sem.at[number])
+
+    ready = set()
+    for piece in GATHER_FIRST:
+        number = pieces[piece][0]
+        if number not in ready:
+            ready.add(number)
+            short[number][...] = shards[number][...].astype(jnp.bfloat16)
+            keep(number).start()
+        hop(piece, 0, False).start()
     tally_out[...] = tally[...]
     add_up(me, own, core, levels, tally_out, tally_land, tally_send, tally_recv)
     for number in range(count):
         keep(number).wait()
-    for stage in range(levels):
-        for number in range(count):
-            hop(number, stage, True).wait_recv()
-            if stage + 1 < levels:
-                hop(number, stage + 1, False).start()
-            cross(number, stage, core).start()
-    for stage in range(levels):
-        for number in range(count):
-            hop(number, stage, False).wait_send()
-            cross(number, stage, core).wait_send()
-            cross(number, stage, 1 - core).wait_recv()
-
-
-def gather_rows(shards, tally, devices, turns):
+    for piece, stage in GATHER_STEPS:
+        hop(piece, stage, True).wait_recv()
+        if stage + 1 < levels:
+            hop(piece, stage + 1, False).start()
+        cross(piece, stage, core).start()
+    for piece in range(len(pieces)):
+        for stage in range(levels):
+            hop(piece, stage, False).wait_send()
+            cross(piece, stage, core).wait_send()
+            cross(piece, stage, 1 - core).wait_recv()
+
+
+def gather_rows(shards, tally, devices):
     levels, count = bit_count(devices), len(shards)
     lead = (2,) * levels
+    pieces = cut_pieces(GATHER_PARTS, [(shard.shape[0], shard.shape[1] // 2) for shard in shards])
     dma = pltpu.SemaphoreType.DMA
     vmem = pl.BlockSpec(memory_space=pltpu.VMEM)
     found = pl.pallas_call(
-        functools.partial(gather_kernel, levels, turns, count),
-        out_shape=[jax.ShapeDtypeStruct(lead + shard.shape, shard.dtype) for shard in shards]
+        functools.partial(gather_kernel, levels, pieces, count),
+        out_shape=[jax.ShapeDtypeStruct(lead + shard.shape, jnp.bfloat16) for shard in shards]
         + [jax.ShapeDtypeStruct((8, 128), jnp.float32)],
-        in_specs=[pl.BlockSpec(memory_space=pl.ANY)] * count + [vmem],
+        in_specs=[vmem] * (count + 1),
         out_specs=[pl.BlockSpec(memory_space=pl.ANY)] * count + [vmem],
-        scratch_shapes=[dma((count,))]
-        + [dma((count, levels))] * 4
+        scratch_shapes=[pltpu.VMEM(shard.shape, jnp.bfloat16) for shard in shards]
+        + [dma((count,))]
+        + [dma((len(pieces), levels))] * 4
         + [pltpu.VMEM((levels + 1, 8, 128), jnp.float32)]
         + [dma((levels + 1,))] * 2,
-        compiler_params=pltpu.CompilerParams(collective_id=1, has_side_effects=True),
+        compiler_params=pltpu.CompilerParams(
+            collective_id=1, has_side_effects=True, vmem_limit_bytes=32 * 2**20
+        ),
         name="gather_rows",
     )(*shards, tally)
     return found[:count], found[count]
 
 
-def reduce_kernel(levels, turns, count, *refs):
-    grads, stats_in = refs[:count], refs[count]
-    sums, stats_out = refs[count + 1 : 2 * count + 1], refs[2 * count + 1]
-    rest = refs[2 * count + 2 :]
+def reduce_kernel(levels, pieces, count, owners, devices, *refs):
+    blocks = len(owners)
+    grads, stats_in, old = refs[:count], refs[count], refs[count + 1 : count + 1 + blocks]
+    rest = refs[count + 1 + blocks :]
+    sums, stats_out, wholes = rest[:count], rest[count], rest[count + 1 : count + 1 + blocks]
+    rest = rest[count + 1 + blocks :]
     mine, theirs, rest = rest[:count], rest[count : 2 * count], rest[2 * count :]
     kept, rest = rest[:count], rest[count:]
-    landing, rest = rest[: count * levels], rest[count * levels :]
-    stats_land, here_sem, pair_send, pair_recv, send_sem, recv_sem, last_send, last_recv, stats_send, stats_recv = rest
+    landing, rest = rest[: len(pieces) * levels], rest[len(pieces) * levels :]
+    staged, rest = rest[:blocks], rest[blocks:]
+    stats_land, here_sem, pair_send, pair_recv, send_sem, recv_sem, last_send, last_recv = rest[:8]
+    stats_send, stats_recv, own_sem, out_send, out_recv, cross_send, cross_recv = rest[8:]
     me, own = own_bits(levels)
     core = lax.axis_index("mp")
-    greet(me, own, levels, core)
-    orders = [bit_order(levels, turn)[::-1] for turn in turns]
+    orders = [AXIS_ORDERS[turn][::-1] for turn in REDUCE_TURNS]
+    owning = functools.reduce(jnp.logical_or, [me == owner for owner in owners])
+    barrier = pltpu.get_barrier_semaphore()
+    for bit in range(levels):
+        pl.semaphore_signal(
+            barrier,
+            inc=1,
+            device_id={"dp": partner(me, own, bit), "mp": core},
+            device_id_type=MESH_ID,
+        )
+    pl.semaphore_signal(barrier, inc=1, device_id={"dp": me, "mp": 1 - core}, device_id_type=MESH_ID)
+
+    @pl.when(owning)
+    def greet_all():
+        @pl.loop(0, devices)
+        def greet_one(other):
+            @pl.when(other != me)
+            def signal_one():
+                pl.semaphore_signal(
+                    barrier, inc=1, device_id={"dp": other, "mp": core}, device_id_type=MESH_ID
+                )
+
+        pl.semaphore_wait(barrier, levels + blocks)
+
+    @pl.when(jnp.logical_not(owning))
+    def wait_owners():
+        pl.semaphore_wait(barrier, levels + 1 + blocks)
 
     def half(number, which):
-        width = grads[number].shape[-1] // 2
+        width = sums[number].shape[1] // 2
         return (slice(None), pl.ds(pl.multiple_of(which * width, 128), width))
 
+    def cut(piece):
+        number, row, rows, column, columns = pieces[piece]
+        return (pl.ds(row, rows), pl.ds(column, columns))
+
+    def side(piece, which):
+        number, row, rows, column, columns = pieces[piece]
+        width = sums[number].shape[1] // 2
+        return (pl.ds(row, rows), pl.ds(pl.multiple_of(which * width + column, 128), columns))
+
     every = (slice(None),) * levels
 
-    def pair(number):
+    def pair(piece):
+        number = pieces[piece][0]
         return pltpu.make_async_remote_copy(
-            src_ref=grads[number].at[every + half(number, 1 - core)],
-            dst_ref=theirs[number],
-            send_sem=pair_send.at[number],
-            recv_sem=pair_recv.at[number],
+            src_ref=grads[number].at[every + side(piece, 1 - core)],
+            dst_ref=theirs[number].at[every + cut(piece)],
+            send_sem=pair_send.at[piece],
+            recv_sem=pair_recv.at[piece],
             device_id={"dp": me, "mp": 1 - core},
             device_id_type=MESH_ID,
         )
 
-    def load(number):
+    def load(piece):
+        number = pieces[piece][0]
         return pltpu.make_async_copy(
-            grads[number].at[every + half(number, core)], mine[number], here_sem.at[number]
-        )
-
-    def hop(number, stage):
-        order = orders[number]
+            grads[number].at[every + side(piece, core)],
+            mine[number].at[every + cut(piece)],
+            here_sem.at[piece],
+        )
+
+    def hop(piece, stage):
+        order = orders[piece]
         spot = place(levels, order[stage + 1 :], own, order[stage])
         return pltpu.make_async_remote_copy(
-            src_ref=theirs[number].at[spot],
-            dst_ref=landing[number * levels + stage],
-            send_sem=send_sem.at[number, stage],
-            recv_sem=recv_sem.at[number, stage],
+            src_ref=theirs[pieces[piece][0]].at[spot + cut(piece)],
+            dst_ref=landing[piece * levels + stage],
+            send_sem=send_sem.at[piece, stage],
+            recv_sem=recv_sem.at[piece, stage],
             device_id={"dp": partner(me, own, order[stage]), "mp": core},
             device_id_type=MESH_ID,
         )
@@ -499,142 +563,19 @@
             device_id_type=MESH_ID,
         )
 
-    def fold(number, stage):
-        order = orders[number]
-        free = order[stage:]
-        loose = [bit for bit in range(levels - 1, -1, -1) if bit in free and bit != order[stage]]
-
-        @pl.loop(0, 2 ** len(loose))
-        def add_block(block):
-            found = {
-                bit: lax.rem(lax.div(block, 2 ** (len(loose) - 1 - i)), 2) for i, bit in enumerate(loose)
-            }
-
-            def total(way):
-                now = dict(found)
-                now[order[stage]] = way
-                full = tuple(now.get(bit, own[bit]) for bit in range(levels - 1, -1, -1))
-                if stage == 0:
-                    value = mine[number][full].astype(jnp.float32) + theirs[number][full].astype(jnp.float32)
-                else:
-                    spot = tuple(
-                        now.get(bit, own[bit]) for bit in range(levels - 1, -1, -1) if bit != order[0]
-                    )
-                    land = tuple(now[bit] for bit in range(levels - 1, -1, -1) if bit in free)
-                    value = kept[number][spot] + landing[number * levels + stage - 1][land].astype(jnp.float32)
-                return full, value
-
-            full, value = total(1 - own[order[stage]])
-            theirs[number][full] = value.astype(theirs[number].dtype)
-            full, value = total(own[order[stage]])
-            spot = tuple(
-                found.get(bit, own[bit]) for bit in range(levels - 1, -1, -1) if bit != order[0]
-            )
-            kept[number][spot] = value
-
-    for number in range(count):
-        pair(number).start()
-        load(number).start()
-    for number in range(count):
-        load(number).wait()
-        pair(number).wait_recv()
-        fold(number, 0)
-        hop(number, 0).start()
-    for stage in range(levels - 1):
-        for number in range(count):
-            hop(number, stage).wait_recv()
-            fold(number, stage + 1)
-            hop(number, stage + 1).start()
-    squares = jnp.zeros((8, 128), jnp.float32)
-    for number in range(count):
-        hop(number, levels - 1).wait_recv()
-        spot = tuple(own[bit] for bit in range(levels - 1, -1, -1) if bit != orders[number][0])
-        total = kept[number][spot] + landing[number * levels + levels - 1][...].astype(jnp.float32)
-        sums[number][half(number, core)] = total
-        share(number, core).start()
-        rows, width = total.shape
-        for row in range(0, rows, 8):
-            for column in range(0, width, 128):
-                part = total[row : row + 8, column : column + 128]
-                squares = squares + part * part
-    stats_out[0:8, :] = squares
-    stats_out[8:16, :] = stats_in[...]
-    add_up(me, own, core, levels, stats_out, stats_land, stats_send, stats_recv)
-    for number in range(count):
-        pair(number).wait_send()
-        for stage in range(levels):
-            hop(number, stage).wait_send()
-        share(number, core).wait_send()
-        share(number, 1 - core).wait_recv()
-
-
-def reduce_rows(grads, stats, devices, turns):
-    levels, count = bit_count(devices), len(grads)
-    lead = (2,) * levels
-    dma = pltpu.SemaphoreType.DMA
-    shapes = [grad.shape[levels:] for grad in grads]
-    halves = [(rows, columns // 2) for rows, columns in shapes]
-    kinds = [grad.dtype for grad in grads]
-    scratch = [pltpu.VMEM(lead + shape, kind) for shape, kind in zip(halves, kinds)] * 2
-    scratch += [pltpu.VMEM(lead[1:] + shape, jnp.float32) for shape in halves]
-    for shape, kind in zip(halves, kinds):
-        for stage in range(levels):
-            scratch.append(pltpu.VMEM((2,) * (levels - 1 - stage) + shape, kind))
-    scratch.append(pltpu.VMEM((levels + 1, 16, 128), jnp.float32))
-    scratch += [dma((count,))] * 3 + [dma((count, levels))] * 2 + [dma((count,))] * 2
-    scratch += [dma((levels + 1,))] * 2
-    vmem = pl.BlockSpec(memory_space=pltpu.VMEM)
-    found = pl.pallas_call(
-        functools.partial(reduce_kernel, levels, turns, count),
-        out_shape=[jax.ShapeDtypeStruct(shape, jnp.float32) for shape in shapes]
-        + [jax.ShapeDtypeStruct((16, 128), jnp.float32)],
-        in_specs=[pl.BlockSpec(memory_space=pl.ANY)] * count + [vmem],
-        out_specs=[vmem] * (count + 1),
-        scratch_shapes=scratch,
-        compiler_params=pltpu.CompilerParams(
-            collective_id=2, has_side_effects=True, vmem_limit_bytes=56 * 2**20
-        ),
-        name="reduce_rows",
-    )(*grads, stats)
-    return found[:count], found[count]
-def send_kernel(owners, count, devices, *refs):
-    rows, wholes = refs[:count], refs[count : 2 * count]
-    here_sem, send_sem, recv_sem, cross_send, cross_recv = refs[2 * count :]
-    me, core = lax.axis_index("dp"), lax.axis_index("mp")
-    barrier = pltpu.get_barrier_semaphore()
-    owning = functools.reduce(jnp.logical_or, [me == owner for owner in owners])
-
-    @pl.when(owning)
-    def greet_all():
-        @pl.loop(0, devices)
-        def greet_one(other):
-            @pl.when(other != me)
-            def signal_one():
-                pl.semaphore_signal(
-                    barrier, inc=1, device_id={"dp": other, "mp": core}, device_id_type=MESH_ID
-                )
-
-        pl.semaphore_signal(
-            barrier, inc=1, device_id={"dp": me, "mp": 1 - core}, device_id_type=MESH_ID
-        )
-        pl.semaphore_wait(barrier, count)
-
-    @pl.when(jnp.logical_not(owning))
-    def wait_owners():
-        pl.semaphore_wait(barrier, count)
-
-    def half(number, which):
-        width = rows[number].shape[1] // 2
-        return (slice(None), pl.ds(pl.multiple_of(which * width, 128), width))
-
-    def hop(number, source):
+    def deliver(number, source):
         return pltpu.make_async_remote_copy(
-            src_ref=rows[number].at[half(number, core)],
+            src_ref=staged[number],
             dst_ref=wholes[number].at[(source,) + half(number, core)],
-            send_sem=send_sem.at[number],
-            recv_sem=recv_sem.at[number, source],
+            send_sem=out_send.at[number],
+            recv_sem=out_recv.at[number, source],
             device_id={"dp": owners[number], "mp": core},
             device_id_type=MESH_ID,
+        )
+
+    def deliver_here(number):
+        return pltpu.make_async_copy(
+            staged[number], wholes[number].at[(me,) + half(number, core)], own_sem
         )
 
     def cross(number, source, which):
@@ -648,59 +589,156 @@
             device_id_type=MESH_ID,
         )
 
-    for number in range(count):
+    def kept_spot(order, found):
+        return tuple(found.get(bit, own[bit]) for bit in range(levels - 1, -1, -1) if bit != order[0])
+
+    def fold(piece, stage):
+        order, number = orders[piece], pieces[piece][0]
+        free = order[stage:]
+        loose = [bit for bit in range(levels - 1, -1, -1) if bit in free and bit != order[stage]]
+        region = cut(piece)
+
+        @pl.loop(0, 2 ** len(loose))
+        def add_block(block):
+            found = {
+                bit: lax.rem(lax.div(block, 2 ** (len(loose) - 1 - i)), 2) for i, bit in enumerate(loose)
+            }
+
+            def total(way):
+                now = dict(found)
+                now[order[stage]] = way
+                full = tuple(now.get(bit, own[bit]) for bit in range(levels - 1, -1, -1)) + region
+                if stage == 0:
+                    value = mine[number][full].astype(jnp.float32) + theirs[number][full].astype(jnp.float32)
+                else:
+                    land = tuple(now[bit] for bit in range(levels - 1, -1, -1) if bit in free)
+                    arrived = landing[piece * levels + stage - 1][land].astype(jnp.float32)
+                    value = kept[number][kept_spot(order, now) + region] + arrived
+                return full, value
+
+            full, value = total(1 - own[order[stage]])
+            theirs[number][full] = value.astype(theirs[number].dtype)
+            full, value = total(own[order[stage]])
+            kept[number][kept_spot(order, found) + region] = value
+
+    for piece in REDUCE_FIRST:
+        pair(piece).start()
+        load(piece).start()
+    for piece in REDUCE_FIRST:
+        load(piece).wait()
+        pair(piece).wait_recv()
+        fold(piece, 0)
+        hop(piece, 0).start()
+    squares = jnp.zeros((8, 128), jnp.float32)
+    for piece, stage in REDUCE_STEPS:
+        hop(piece, stage).wait_recv()
+        if stage + 1 < levels:
+            fold(piece, stage + 1)
+            hop(piece, stage + 1).start()
+        else:
+            number = pieces[piece][0]
+            arrived = landing[piece * levels + stage][...].astype(jnp.float32)
+            total = kept[number][kept_spot(orders[piece], {}) + cut(piece)] + arrived
+            sums[number][side(piece, core)] = total
+            rows, width = total.shape
+            for row in range(0, rows, 8):
+                for column in range(0, width, 128):
+                    part = total[row : row + 8, column : column + 128]
+                    squares = squares + part * part
+    for number in range(blocks, count):
+        share(number, core).start()
+    stats_out[0:8, :] = squares
+    stats_out[8:16, :] = stats_in[...]
+    add_up(me, own, core, levels, stats_out, stats_land, stats_send, stats_recv)
+    norm = jnp.sqrt(jnp.sum(jnp.sum(stats_out[0:8, :], axis=0, keepdims=True), axis=1, keepdims=True))
+    factor = jnp.minimum(1.0, CLIP_MAX / (norm + 1e-06))
+    for number in range(blocks):
+        region = half(number, core)
+        renewed = 0.5 * old[number][region] + factor * sums[number][region]
+        sums[number][region] = renewed
+        staged[number][...] = renewed.astype(staged[number].dtype)
+        share(number, core).start()
 
         @pl.when(me != owners[number])
         def start_one(number=number):
-            hop(number, me).start()
-
-    for number in range(count):
+            deliver(number, me).start()
+
+        @pl.when(me == owners[number])
+        def start_here(number=number):
+            deliver_here(number).start()
+
+    for piece in range(len(pieces)):
+        pair(piece).wait_send()
+        for stage in range(levels):
+            hop(piece, stage).wait_send()
+    for number in range(blocks):
 
         @pl.when(me == owners[number])
         def collect(number=number):
-            own = pltpu.make_async_copy(rows[number], wholes[number].at[me], here_sem)
-            own.start()
+            deliver_here(number).wait()
 
             @pl.loop(0, devices)
             def forward(source):
                 @pl.when(source != me)
-                def forward_one():
-                    hop(number, source).wait_recv()
-                    cross(number, source, core).start()
-
-            own.wait()
+                def arrived():
+                    deliver(number, source).wait_recv()
+
+                cross(number, source, core).start()
 
             @pl.loop(0, devices)
             def finish(source):
-                @pl.when(source != me)
-                def finish_one():
-                    cross(number, source, core).wait_send()
-                    cross(number, source, 1 - core).wait_recv()
-
-    for number in range(count):
+                cross(number, source, core).wait_send()
+                cross(number, source, 1 - core).wait_recv()
 
         @pl.when(me != owners[number])
         def end_one(number=number):
-            hop(number, me).wait_send()
-
-
-def send_to_owners(rows, owners, devices):
-    count = len(rows)
+            deliver(number, me).wait_send()
+
+    for number in range(count):
+        share(number, core).wait_send()
+        share(number, 1 - core).wait_recv()
+
+
+def reduce_rows(grads, stats, old, owners, devices):
+    levels, count, blocks = bit_count(devices), len(grads), len(old)
+    lead = (2,) * levels
     dma = pltpu.SemaphoreType.DMA
-    return pl.pallas_call(
-        functools.partial(send_kernel, owners, count, devices),
-        out_shape=[jax.ShapeDtypeStruct((devices,) + row.shape, row.dtype) for row in rows],
-        in_specs=[pl.BlockSpec(memory_space=pl.ANY)] * count,
-        out_specs=[pl.BlockSpec(memory_space=pl.ANY)] * count,
-        scratch_shapes=[dma, dma((count,))] + [dma((count, devices))] * 3,
-        compiler_params=pltpu.CompilerParams(collective_id=3, has_side_effects=True),
-        name="send_to_owners",
-    )(*rows)
-
-
-def return_kernel(owners, count, devices, *refs):
-    wholes, rows = refs[:count], refs[count : 2 * count]
-    here_sem, send_sem, recv_sem, cross_send, cross_recv = refs[2 * count :]
+    shapes = [grad.shape[levels:] for grad in grads]
+    halves = [(rows, columns // 2) for rows, columns in shapes]
+    kinds = [grad.dtype for grad in grads]
+    pieces = cut_pieces(REDUCE_PARTS, halves)
+    scratch = [pltpu.VMEM(lead + shape, kind) for shape, kind in zip(halves, kinds)] * 2
+    scratch += [pltpu.VMEM(lead[1:] + shape, jnp.float32) for shape in halves]
+    for number, row, rows, column, columns in pieces:
+        for stage in range(levels):
+            scratch.append(pltpu.VMEM((2,) * (levels - 1 - stage) + (rows, columns), kinds[number]))
+    scratch += [pltpu.VMEM(halves[number], kinds[number]) for number in range(blocks)]
+    scratch.append(pltpu.VMEM((levels + 1, 16, 128), jnp.float32))
+    scratch += [dma((len(pieces),))] * 3 + [dma((len(pieces), levels))] * 2 + [dma((count,))] * 2
+    scratch += [dma((levels + 1,))] * 2 + [dma, dma((blocks,))] + [dma((blocks, devices))] * 3
+    vmem, anywhere = pl.BlockSpec(memory_space=pltpu.VMEM), pl.BlockSpec(memory_space=pl.ANY)
+    found = pl.pallas_call(
+        functools.partial(reduce_kernel, levels, pieces, count, owners, devices),
+        out_shape=[jax.ShapeDtypeStruct(shape, jnp.float32) for shape in shapes]
+        + [jax.ShapeDtypeStruct((16, 128), jnp.float32)]
+        + [jax.ShapeDtypeStruct((devices,) + shapes[number], kinds[number]) for number in range(blocks)],
+        in_specs=[anywhere] * count + [vmem] * (1 + blocks),
+        out_specs=[vmem] * (count + 1) + [anywhere] * blocks,
+        scratch_shapes=scratch,
+        compiler_params=pltpu.CompilerParams(
+            collective_id=2, has_side_effects=True, vmem_limit_bytes=60 * 2**20
+        ),
+        name="reduce_rows",
+    )(*grads, stats, *old)
+    return found[:blocks], found[blocks:count], found[count], found[count + 1 :]
+
+
+def return_kernel(owners, count, devices, rates, *refs):
+    wholes, masters, rest = refs[:count], refs[count : 2 * count], refs[2 * count :]
+    stats, adam_in, rest = rest[0], rest[1:9], rest[9:]
+    updated, adam_out, rest = rest[:count], rest[count : count + 6], rest[count + 6 :]
+    rows, rest = rest[:count], rest[count:]
+    here_sem, send_sem, recv_sem, cross_send, cross_recv = rest
     me, core = lax.axis_index("dp"), lax.axis_index("mp")
     barrier = pltpu.get_barrier_semaphore()
     owning = functools.reduce(jnp.logical_or, [me == owner for owner in owners])
@@ -764,6 +802,13 @@
 
             own.wait()
 
+    norm = jnp.sqrt(jnp.sum(jnp.sum(stats[0:8, :], axis=0, keepdims=True), axis=1, keepdims=True))
+    factor = jnp.minimum(1.0, CLIP_MAX / (norm + 1e-06))
+    for place_in in range(2):
+        weight, first, second, grad = [ref[...] for ref in adam_in[4 * place_in : 4 * place_in + 4]]
+        made = adam_update(weight, first, second, grad * factor, DECAY)
+        for place_out in range(3):
+            adam_out[3 * place_in + place_out][...] = made[place_out]
     for number in range(count):
 
         @pl.when(me != owners[number])
@@ -774,6 +819,9 @@
     for number in range(count):
         cross(number, core).wait_send()
         cross(number, 1 - core).wait_recv()
+        updated[number][...] = masters[number][...] * (1.0 - LR_MUON * DECAY) - rates[number] * rows[
+            number
+        ][...].astype(jnp.float32)
 
         @pl.when(me == owners[number])
         def end_out(number=number):
@@ -784,18 +832,28 @@
                     hop(number, target).wait_send()
 
 
-def return_rows(wholes, owners, devices):
+def return_rows(wholes, masters, stats, adam, owners, devices):
     count = len(wholes)
+    rates = []
+    for whole in wholes:
+        rates.append(LR_MUON * 0.2 * math.sqrt(max(whole.shape[0] * whole.shape[1], whole.shape[2])))
     dma = pltpu.SemaphoreType.DMA
-    return pl.pallas_call(
-        functools.partial(return_kernel, owners, count, devices),
-        out_shape=[jax.ShapeDtypeStruct(whole.shape[1:], whole.dtype) for whole in wholes],
-        in_specs=[pl.BlockSpec(memory_space=pl.ANY)] * count,
-        out_specs=[pl.BlockSpec(memory_space=pltpu.VMEM)] * count,
-        scratch_shapes=[dma, dma((count, devices)), dma((count,)), dma((count,)), dma((count,))],
-        compiler_params=pltpu.CompilerParams(collective_id=4, has_side_effects=True),
+    vmem = pl.BlockSpec(memory_space=pltpu.VMEM)
+    moved = (adam[0], adam[1], adam[2], adam[4], adam[5], adam[6])
+    found = pl.pallas_call(
+        functools.partial(return_kernel, owners, count, devices, rates),
+        out_shape=[jax.ShapeDtypeStruct(master.shape, jnp.float32) for master in masters]
+        + [jax.ShapeDtypeStruct(piece.shape, jnp.float32) for piece in moved],
+        in_specs=[pl.BlockSpec(memory_space=pl.ANY)] * count + [vmem] * (count + 9),
+        out_specs=[vmem] * (count + 6),
+        scratch_shapes=[pltpu.VMEM(whole.shape[1:], whole.dtype) for whole in wholes]
+        + [dma, dma((count, devices)), dma((count,)), dma((count,)), dma((count,))],
+        compiler_params=pltpu.CompilerParams(
+            collective_id=4, has_side_effects=True, vmem_limit_bytes=40 * 2**20
+        ),
         name="return_rows",
-    )(*wholes)
+    )(*wholes, *masters, stats, *adam)
+    return found[:count], found[count : count + 3], found[count + 3 :]
 
 
 def muon_kernel(owners, shapes, *refs):
@@ -1036,10 +1094,25 @@
 
 
 def window_patches(spec):
-    grid = spec.reshape(spec.shape[0], GT, PS, GF, PS)
-    grid = jnp.roll(grid, (-SHIFT, -SHIFT), axis=(1, 3))
-    grid = grid.reshape(spec.shape[0], GT // WIN, WIN, PS, GF // WIN, WIN, PS)
-    return grid.transpose(0, 1, 4, 2, 5, 3, 6).reshape(spec.shape[0], NPATCH, PATCH)
+    position = np.arange(NPATCH)
+    row = np.empty(NPATCH, np.int32)
+    row[window_place(position)] = position
+    rows = row[:, None]
+    take = (rows // GF == np.arange(GT)[None, :]).astype(np.float32)
+    column = lax.broadcasted_iota(jnp.int32, (NPATCH, PS * GF * PS), 1)
+    inside = (column // PS) % GF == jnp.asarray(rows % GF)
+    source = np.arange(PS * GF * PS)[:, None]
+    target = np.arange(PATCH)[None, :]
+    fold = np.logical_and(source // (GF * PS) == target // PS, source % PS == target % PS)
+    lines = spec.reshape(spec.shape[0], GT, PS * GF * PS)
+    spread = jnp.einsum(
+        "rt,ctl->crl", jnp.asarray(take, jnp.bfloat16), lines, preferred_element_type=jnp.float32
+    )
+    spread = jnp.where(inside, spread, 0.0).astype(jnp.bfloat16)
+    found = jnp.einsum(
+        "crl,lq->crq", spread, jnp.asarray(fold, jnp.bfloat16), preferred_element_type=jnp.float32
+    )
+    return found.astype(jnp.bfloat16)
 
 
 @jax.custom_vjp
@@ -1065,39 +1138,266 @@
 times.defvjp(times_keep, times_back)
 
 
-def pair_product(spec, left_spec, right_spec):
+def soft_rows(scores, allowed, scaling):
+    scores = jnp.where(allowed, scores * scaling, -1e30)
+    exponent = jnp.exp(scores - jnp.max(scores, axis=-1, keepdims=True))
+    return exponent / jnp.sum(exponent, axis=-1, keepdims=True)
+
+
+def dot_rows(left, right):
+    return lax.dot_general(left, right, (((1,), (1,)), ((), ())), preferred_element_type=jnp.float32)
+
+
+def dot_columns(left, right):
+    return lax.dot_general(left, right, (((0,), (0,)), ((), ())), preferred_element_type=jnp.float32)
+
+
+def head_lanes(value, head, size):
+    lane = lax.broadcasted_iota(jnp.int32, value.shape, 1)
+    return jnp.where(lane // size == head, value, jnp.zeros_like(value))
+
+
+def attention_kernel(size, joined, allowed, out):
+    width = out.shape[1]
+    per = 128 // size
+    allow = jnp.broadcast_to(allowed[...], (out.shape[0], allowed.shape[1])) > 0.0
+    for lane in range(0, width, 128):
+        queries = joined[:, lane : lane + 128]
+        key_rows = joined[:, width + lane : width + lane + 128]
+        values = joined[:, 2 * width + lane : 2 * width + lane + 128]
+        total = jnp.zeros(queries.shape, jnp.float32)
+        for head in range(per):
+            scores = dot_rows(queries, head_lanes(key_rows, head, size))
+            soft = soft_rows(scores, allow, size ** (-0.5)).astype(jnp.bfloat16)
+            total = total + jnp.dot(
+                soft, head_lanes(values, head, size), preferred_element_type=jnp.float32
+            )
+        out[:, lane : lane + 128] = total.astype(jnp.bfloat16)
+
+
+def attention_back_kernel(size, joined, allowed, grad, out, query_sum, value_sum):
+    width = grad.shape[1]
+    per = 128 // size
+    scaling = size ** (-0.5)
+    allow = jnp.broadcast_to(allowed[...], (grad.shape[0], allowed.shape[1])) > 0.0
+
+    @pl.when(pl.program_id(0) == 0)
+    def clear():
+        query_sum[...] = jnp.zeros_like(query_sum)
+        value_sum[...] = jnp.zeros_like(value_sum)
+
+    for lane in range(0, width, 128):
+        queries = joined[:, lane : lane + 128]
+        key_rows = joined[:, width + lane : width + lane + 128]
+        values = joined[:, 2 * width + lane : 2 * width + lane + 128]
+        pull = grad[:, lane : lane + 128]
+        query_grad = jnp.zeros(queries.shape, jnp.float32)
+        key_grad = jnp.zeros(queries.shape, jnp.float32)
+        value_grad = jnp.zeros(queries.shape, jnp.float32)
+        for head in range(per):
+            keys_here = head_lanes(key_rows, head, size)
+            soft = soft_rows(dot_rows(queries, keys_here), allow, scaling)
+            soft_grad = dot_rows(pull, head_lanes(values, head, size))
+            score_grad = soft * (soft_grad - jnp.sum(soft * soft_grad, axis=-1, keepdims=True))
+            score_grad = (score_grad * scaling).astype(jnp.bfloat16)
+            query_grad = query_grad + jnp.dot(score_grad, keys_here, preferred_element_type=jnp.float32)
+            key_grad = key_grad + dot_columns(score_grad, head_lanes(queries, head, size))
+            value_grad = value_grad + dot_columns(soft.astype(jnp.bfloat16), head_lanes(pull, head, size))
+        out[:, lane : lane + 128] = query_grad.astype(jnp.bfloat16)
+        out[:, width + lane : width + lane + 128] = key_grad.astype(jnp.bfloat16)
+        out[:, 2 * width + lane : 2 * width + lane + 128] = value_grad.astype(jnp.bfloat16)
+        query_sum[0:1, lane : lane + 128] += jnp.sum(query_grad, axis=0, keepdims=True)
+        value_sum[0:1, lane : lane + 128] += jnp.sum(value_grad, axis=0, keepdims=True)
+
+
+def window_fold(value, heads):
+    lane = lax.broadcasted_iota(jnp.int32, (1, 1, value.shape[1]), 2) // (WIN * WIN)
+    value = value.reshape(heads, 8, WIN * WIN, value.shape[1])
+    found = value[:, 0]
+    for window in range(1, 8):
+        found = jnp.where(lane == window, value[:, window], found)
+    return found
+
+
+def window_spread(value):
+    heads = value.shape[0]
+    short = value.astype(jnp.bfloat16)
+    lane = lax.broadcasted_iota(jnp.int32, short.shape, 2) // (WIN * WIN)
+    parts = []
+    for head in range(heads):
+        for window in range(8):
+            parts.append(
+                jnp.where(lane[head] == window, short[head], jnp.zeros_like(short[head]))
+            )
+    return jnp.concatenate(parts, axis=0)
+
+
+def stack_heads(value, size):
+    per = value.shape[1] // size
+    return jnp.concatenate([head_lanes(value, head, size) for head in range(per)], axis=0)
+
+
+def unstack_heads(value, size):
+    rows = value.shape[1]
+    per = value.shape[0] // rows
+    lane = lax.broadcasted_iota(jnp.int32, (rows, rows), 1) // size
+    found = value[:rows]
+    for head in range(1, per):
+        found = jnp.where(lane == head, value[head * rows : (head + 1) * rows], found)
+    return found
+
+
+def soft_fold(queries, keys_here, allow, size):
+    scores = window_fold(dot_rows(keys_here, queries), 128 // size)
+    scores = jnp.where(allow, scores * size ** (-0.5), -1e30)
+    exponent = jnp.exp(scores - jnp.max(scores, axis=1, keepdims=True))
+    return exponent / jnp.sum(exponent, axis=1, keepdims=True)
+
+
+def window_kernel(size, joined, allowed, out):
+    width = out.shape[1]
+    allow = allowed[...][None] > 0.0
+    for lane in range(0, width, 128):
+        queries = joined[:, lane : lane + 128]
+        keys_here = stack_heads(joined[:, width + lane : width + lane + 128], size)
+        values_here = stack_heads(joined[:, 2 * width + lane : 2 * width + lane + 128], size)
+        soft = window_spread(soft_fold(queries, keys_here, allow, size))
+        out[:, lane : lane + 128] = dot_columns(soft, values_here).astype(jnp.bfloat16)
+
+
+def window_back_kernel(size, joined, allowed, grad, out, query_sum, value_sum):
+    width = grad.shape[1]
+    allow = allowed[...][None] > 0.0
+
+    @pl.when(pl.program_id(0) == 0)
+    def clear():
+        query_sum[...] = jnp.zeros_like(query_sum)
+        value_sum[...] = jnp.zeros_like(value_sum)
+
+    for lane in range(0, width, 128):
+        queries = joined[:, lane : lane + 128]
+        keys_here = stack_heads(joined[:, width + lane : width + lane + 128], size)
+        values_here = stack_heads(joined[:, 2 * width + lane : 2 * width + lane + 128], size)
+        pull = grad[:, lane : lane + 128]
+        soft = soft_fold(queries, keys_here, allow, size)
+        soft_grad = window_fold(dot_rows(values_here, pull), 128 // size)
+        score_grad = soft * (soft_grad - jnp.sum(soft * soft_grad, axis=1, keepdims=True))
+        score_grad = window_spread(score_grad * size ** (-0.5))
+        soft = window_spread(soft)
+        query_grad = dot_columns(score_grad, keys_here)
+        key_grad = unstack_heads(jnp.dot(score_grad, queries, preferred_element_type=jnp.float32), size)
+        value_grad = unstack_heads(jnp.dot(soft, pull, preferred_element_type=jnp.float32), size)
+        out[:, lane : lane + 128] = query_grad.astype(jnp.bfloat16)
+        out[:, width + lane : width + lane + 128] = key_grad.astype(jnp.bfloat16)
+        out[:, 2 * width + lane : 2 * width + lane + 128] = value_grad.astype(jnp.bfloat16)
+        query_sum[0:1, lane : lane + 128] += jnp.sum(query_grad, axis=0, keepdims=True)
+        value_sum[0:1, lane : lane + 128] += jnp.sum(value_grad, axis=0, keepdims=True)
+
+
+def attention_parts(joined, allowed, rows):
+    steps = joined.shape[0] // rows
+    period = allowed.shape[0]
+    wide = pl.BlockSpec((rows, joined.shape[1]), lambda step: (step, 0))
+    mask = pl.BlockSpec((None,) + allowed.shape[1:], lambda step: (lax.rem(step, period), 0, 0))
+    narrow_rows = pl.BlockSpec((rows, joined.shape[1] // 3), lambda step: (step, 0))
+    return steps, wide, mask, narrow_rows
+
+
+def attention_forward(kernel, joined, allowed, rows, size):
+    steps, wide, mask, part = attention_parts(joined, allowed, rows)
+    return pl.pallas_call(
+        functools.partial(kernel, size),
+        grid=(steps,),
+        out_shape=jax.ShapeDtypeStruct((joined.shape[0], joined.shape[1] // 3), jnp.bfloat16),
+        in_specs=[wide, mask],
+        out_specs=part,
+        compiler_params=pltpu.CompilerParams(vmem_limit_bytes=40 * 2**20),
+        name="attention_forward",
+    )(joined, allowed)
+
+
+def attention_backward(kernel, joined, allowed, grad, rows, size):
+    steps, wide, mask, part = attention_parts(joined, allowed, rows)
+    width = joined.shape[1] // 3
+    total = pl.BlockSpec((8, width), lambda step: (0, 0))
+    return pl.pallas_call(
+        functools.partial(kernel, size),
+        grid=(steps,),
+        out_shape=[
+            jax.ShapeDtypeStruct(joined.shape, jnp.bfloat16),
+            jax.ShapeDtypeStruct((8, width), jnp.float32),
+            jax.ShapeDtypeStruct((8, width), jnp.float32),
+        ],
+        in_specs=[wide, mask, part],
+        out_specs=[wide, total, total],
+        compiler_params=pltpu.CompilerParams(vmem_limit_bytes=40 * 2**20),
+        name="attention_backward",
+    )(joined, allowed, grad)
+
+
+def attention_block(forward, backward, rows, size):
+    def join(normed, matrix, query_bias, value_bias):
+        width = matrix.shape[1] // 3
+        bias = jnp.concatenate([query_bias, jnp.zeros((width,), jnp.float32), value_bias])
+        joined = jnp.dot(normed, matrix.astype(jnp.bfloat16), preferred_element_type=jnp.float32)
+        return (joined + bias).astype(jnp.bfloat16)
+
     @jax.custom_vjp
-    def apply(left, right):
-        return jnp.einsum(
-            spec, left.astype(jnp.bfloat16), right.astype(jnp.bfloat16), preferred_element_type=jnp.float32
-        )
-
-    def keep(left, right):
-        left, right = left.astype(jnp.bfloat16), right.astype(jnp.bfloat16)
-        return jnp.einsum(spec, left, right, preferred_element_type=jnp.float32), (left, right)
+    def apply(normed, matrix, query_bias, value_bias, allowed):
+        joined = join(normed.astype(jnp.bfloat16), matrix, query_bias, value_bias)
+        return attention_forward(forward, joined, allowed, rows, size).astype(jnp.float32)
+
+    def keep(normed, matrix, query_bias, value_bias, allowed):
+        short = normed.astype(jnp.bfloat16)
+        joined = join(short, matrix, query_bias, value_bias)
+        made = attention_forward(forward, joined, allowed, rows, size).astype(jnp.float32)
+        return made, (short, matrix, joined, allowed)
 
     def back(kept, grad):
-        left, right = kept
-        grad = grad.astype(jnp.bfloat16)
-        return (
-            jnp.einsum(left_spec, grad, right, preferred_element_type=jnp.float32),
-            jnp.einsum(right_spec, grad, left, preferred_element_type=jnp.float32),
-        )
+        short, matrix, joined, allowed = kept
+        pulled, query_sum, value_sum = attention_backward(
+            backward, joined, allowed, grad.astype(jnp.bfloat16), rows, size
+        )
+        normed_grad = dot_rows(pulled, matrix.astype(jnp.bfloat16))
+        matrix_grad = dot_columns(short, pulled).astype(matrix.dtype)
+        return normed_grad, matrix_grad, query_sum[0], value_sum[0], jnp.zeros_like(allowed)
 
     apply.defvjp(keep, back)
     return apply
 
 
-scores_of = pair_product("bqhd,bkhd->bhqk", "bhqk,bkhd->bqhd", "bhqk,bqhd->bkhd")
-mix_of = pair_product("bhqk,bkhd->bqhd", "bqhd,bkhd->bhqk", "bqhd,bhqk->bkhd")
-
-
-def attend_short(queries, key_rows, values, allowed, scaling):
-    scores = scores_of(queries, key_rows) * scaling
-    scores = jnp.where(allowed, scores, -1e30)
-    scores = scores - jnp.max(scores, axis=-1, keepdims=True)
-    exponent = jnp.exp(scores)
-    return mix_of(exponent / jnp.sum(exponent, axis=-1, keepdims=True), values)
+encoder_attention = attention_block(attention_kernel, attention_back_kernel, SLOTS, HEAD)
+decoder_attention = attention_block(window_kernel, window_back_kernel, 8 * WIN * WIN, DHEAD)
+
+
+def window_allowed():
+    position = np.arange(NPATCH)
+    window, inner = position // (WIN * WIN), position % (WIN * WIN)
+    time_row = window // (GF // WIN) * WIN + inner // WIN
+    freq_col = window % (GF // WIN) * WIN + inner % WIN
+    region = (time_row >= GT - WIN).astype(np.int32) + (time_row >= GT - SHIFT)
+    region = region * 3 + (freq_col >= GF - WIN) + (freq_col >= GF - SHIFT)
+    region = region.reshape(-1, 8, 1, WIN * WIN)
+    same = region == region.transpose(0, 1, 3, 2)
+    return same.transpose(0, 2, 1, 3).reshape(-1, WIN * WIN, 8 * WIN * WIN).astype(np.float32)
+
+
+@jax.custom_vjp
+def gelu(value):
+    return value * (0.5 + 0.5 * lax.erf(value * math.sqrt(0.5)))
+
+
+def gelu_keep(value):
+    portion = 0.5 + 0.5 * lax.erf(value * math.sqrt(0.5))
+    slope = portion + value * jnp.exp(-0.5 * value * value) * (1.0 / math.sqrt(2.0 * math.pi))
+    return value * portion, slope
+
+
+def gelu_back(slope, grad):
+    return (grad * slope,)
+
+
+gelu.defvjp(gelu_keep, gelu_back)
 
 
 def local_loss(weights, patches, keep, counts):
@@ -1111,15 +1411,11 @@
     where = jnp.einsum("cjp,pd->cjd", chosen, window_sinusoid(D), precision=HIGH)
     hidden = times(picked.reshape(-1, PATCH), weights[8][:, :D]) + pieces[11] + where.reshape(-1, D)
     normed = layer_norm(hidden, pieces[0], pieces[1])
-    joined = times(normed, weights[0])
-    queries = (joined[:, :D] + pieces[2]).reshape(clips, SLOTS, HEADS, HEAD)
-    key_rows = joined[:, D : 2 * D].reshape(clips, SLOTS, HEADS, HEAD)
-    values = (joined[:, 2 * D :] + pieces[3]).reshape(clips, SLOTS, HEADS, HEAD)
-    visible = (jnp.arange(SLOTS)[None, :] < counts[:, None])[:, None, None, :]
-    attended = attend_short(queries, key_rows, values, visible, HEAD ** (-0.5)).reshape(-1, D)
+    visible = (jnp.arange(SLOTS)[None, :] < counts[:, None]).astype(jnp.float32)[:, None, :]
+    attended = encoder_attention(normed, weights[0], pieces[2], pieces[3], visible)
     hidden = hidden + times(attended, weights[1]) + pieces[4]
     normed = layer_norm(hidden, pieces[5], pieces[6])
-    inner = jax.nn.gelu(times(normed, weights[2]) + pieces[7], approximate=False)
+    inner = gelu(times(normed, weights[2]) + pieces[7])
     hidden = hidden + times(inner, weights[3]) + pieces[8]
     latent = layer_norm(hidden, pieces[9], pieces[10])
 
@@ -1130,15 +1426,10 @@
     hidden = filled + (1.0 - cells)[..., None] * pieces[1] + window_sinusoid(DD)
     hidden = hidden.reshape(-1, DD)
     normed = layer_norm(hidden, pieces[2], pieces[3])
-    windows = times(normed, weights[4])
-    queries = (windows[:, :DD] + pieces[4]).reshape(-1, WIN * WIN, DHEADS, DHEAD)
-    key_rows = windows[:, DD : 2 * DD].reshape(-1, WIN * WIN, DHEADS, DHEAD)
-    values = (windows[:, 2 * DD :] + pieces[5]).reshape(-1, WIN * WIN, DHEADS, DHEAD)
-    allowed = jnp.tile(window_mask(), (clips, 1, 1))[:, None, :, :]
-    attended = attend_short(queries, key_rows, values, allowed, DHEAD ** (-0.5)).reshape(-1, DD)
+    attended = decoder_attention(normed, weights[4], pieces[4], pieces[5], jnp.asarray(window_allowed()))
     hidden = hidden + times(attended, weights[5]) + pieces[6]
     normed = layer_norm(hidden, pieces[7], pieces[8])
-    inner = jax.nn.gelu(times(normed, weights[6]) + pieces[9], approximate=False)
+    inner = gelu(times(normed, weights[6]) + pieces[9])
     hidden = hidden + times(inner, weights[7]) + pieces[10]
     normed = layer_norm(hidden, pieces[11], pieces[12])
     predicted = times(normed, weights[8][:, D:].T) + pieces[13]
@@ -1157,7 +1448,7 @@
     moments = rest[8:16]
     devices = lax.axis_size("dp")
     lead = (2,) * bit_count(devices)
-    own = [weight.astype(jnp.bfloat16) for weight in masters]
+    own = list(masters)
     vector_rows = own[10].shape[0]
     spare = VEC_ROWS * VEC_COLS
     own[10] = jnp.pad(own[10], (0, spare - vector_rows)).reshape(VEC_ROWS, VEC_COLS)
@@ -1165,7 +1456,7 @@
     column = lax.broadcasted_iota(jnp.int32, (8, 128), 1)
     first = jnp.logical_and(row == 0, column == 0)
     count_part = jnp.sum(NPATCH - counts).astype(jnp.float32)
-    gathered, tally = gather_rows(own, jnp.where(first, count_part, 0.0), devices, GATHER_TURNS)
+    gathered, tally = gather_rows(own, jnp.where(first, count_part, 0.0), devices)
     mask_count = tally[0, 0]
     weights = [piece.reshape(-1, piece.shape[-1]) for piece in gathered[:10]]
     weights[4] = weights[4].astype(jnp.float32)
@@ -1180,29 +1471,18 @@
     for number in range(10):
         grad = grads[number]
         grads[number] = grad.reshape(lead + (grad.shape[0] // devices, grad.shape[1]))
-    reduced, stats = reduce_rows(grads, jnp.where(first, loss_part, 0.0), devices, REDUCE_TURNS)
-    reduced = list(reduced)
-    reduced[10] = reduced[10].reshape(-1)[:vector_rows]
+    renewed, others, stats, collected = reduce_rows(
+        grads, jnp.where(first, loss_part, 0.0), moments, OWNERS, devices
+    )
     loss_sum = stats[8, 0]
     grad_norm = jnp.sqrt(jnp.sum(stats[:8]))
     factor = jnp.minimum(1.0, CLIP_MAX / (grad_norm + 1e-06))
-    clipped = [gradient * factor for gradient in reduced]
-    renewed = [0.5 * moments[number] + clipped[number] for number in range(8)]
-    sent = [piece if number == 4 else piece.astype(jnp.bfloat16) for number, piece in enumerate(renewed)]
-    collected = send_to_owners(sent, OWNERS, devices)
     made = orthogonalize([piece.reshape(-1, piece.shape[2]) for piece in collected], OWNERS)
     made = [piece.reshape(devices, -1, piece.shape[1]) for piece in made]
-    whole = return_rows(made, OWNERS, devices)
-    new_weights = []
-    for number in range(8):
-        height, breadth = masters[number].shape
-        step_rate = LR_MUON * 0.2 * math.sqrt(max(height * devices, breadth))
-        new_weights.append(
-            masters[number] * (1.0 - LR_MUON * DECAY) - step_rate * whole[number].astype(jnp.float32)
-        )
-    patch_new = adam_update(*rest[16:19], clipped[8], DECAY)
-    embed_new = adam_update(*rest[19:22], clipped[9], DECAY)
-    vector_new = adam_update(*rest[22:25], clipped[10], 0.0)
+    adam = (*rest[16:19], others[0], *rest[19:22], others[1])
+    new_weights, patch_new, embed_new = return_rows(made, masters[:8], stats, adam, OWNERS, devices)
+    vector_grad = others[2].reshape(-1)[:vector_rows] * factor
+    vector_new = adam_update(*rest[22:25], vector_grad, 0.0)
     return (loss_sum, mask_count, grad_norm, *new_weights, *renewed, *patch_new, *embed_new, *vector_new)
 
 

time: 941 us -> 617 us (0.66)
  the two profiles are of different devices: /device:TPU:31 before, /device:TPU:15 now
where the time goes in v2:
time: 617 us; the launch traced here: 606 us
  Pallas kernels  423 us (69%)
  matrix products  99.4 us (16%)
  local copies, waits for them, and re-layouts  55.3 us (9%)
  other arithmetic  22.2 us (4%)
  between operations  6.28 us (1%)
    pallas_call x1, Pallas kernels, reduce_rows(): pl.pallas_call(functools.partial(reduce_kernel, levels, pieces, count, ow...  172 us
    pallas_call x1, Pallas kernels, gather_rows(): pl.pallas_call(functools.partial(gather_kernel, levels, pieces, count), o...  105 us
    pallas_call x1, Pallas kernels, orthogonalize(): pl.pallas_call(functools.partial(muon_kernel, owners, shapes), out_shape=...  75.2 us
    unnamed x332, local copies, waits for them, and re-layouts  42 us
    pallas_call x1, Pallas kernels, return_rows(): pl.pallas_call(functools.partial(return_kernel, owners, count, devices, r...  39.2 us
    dot_general x9, matrix products, times_keep(): jnp.dot(short, matrix.astype(jnp.bfloat16), preferred_element_type=jnp.fl...  19.4 us
    dot_general x2, matrix products, local_loss(): hidden = hidden + times(inner, weights[7]) + pieces[10]  16.3 us
    pallas_call x1, Pallas kernels, local_loss(): decoder_attention(normed, weights[4], pieces[4], pieces[5], jnp.asarray(w...  13.5 us

profile of v2, /device:TPU:15, one launch (start us, length us, event | category | flops | bytes accessed | tf_op | source)
XLA Modules:
  0.0 606.0 jit_solution(7572345362591671192)
XLA Ops:
  7.8 3.5 fusion.36
  12.1 2.5 convert_reduce_fusion
  17.5 105.1 %gather_rows.1 = (bf16[2,2,2,2,48,2304]{5,4,3,2,1,0:T(8,128)(2,1)S(1)}, bf16[2,2,2,2,48,768]{5,4,3,2,1,0:T(8,128)(2,1)S(1)}, bf16[2,2,2,2,48,3072]{5,4,3,2,1,0:T...) custom-call(f32[48,2304]{1,0:T(8,128)S(1)} %copy-done.4, ...), custom_call_target="tpu_custom_call" | custom-call | tf_op jit(solution)/shard_map/gather_rows/pallas_call | solution.py:448
  145.2 2.8 jvp_attention_forward_.2
  149.1 4.2 multiply_convert_fusion.1
  156.8 2.5 fusion.97
  163.7 7.2 %jvp_attention_forward_.3 = bf16[1024,512]{1,0:T(8,128)(2,1)S(1)} custom-call(bf16[1024,1536]{1,0:T(8,128)(2,1)S(1)} %add_convert_fusion.joined, f32[4,16,128]{2,1,0:T(8,128)S(1)} %copy-done.23), custom_call_target="tpu_custom_call" | custom-call | tf_op jit(solution)/shard_map/jvp(attention_forward)/pallas_call | solution.py:1308
  174.1 6.1 %multiply_convert_fusion = (bf16[1024,2048]{1,0:T(8,128)(2,1)S(1)}, f32[1024,2048]{1,0:T(8,128)}) fusion(f32[2048]{0:T(1024)S(1)} %slice.171, bf16[512,2048]{1,0:T(8,128)(2,1)S(1)} %bitcast.170, f32[1024,512]{1,0:T(8,128)S(1)} %get-tuple-element.237, f32[512]{0:T(512)S(1)} %get-tuple-element.197, f32[512]{0:T(512)S(1)} %get-tuple-element.198, ...), kind=kOutput, calls=%fused_computation.7 | convolution fusion | flops 2162688000 | bytes 16797696 | tf_op jit(solution)/shard_map/jvp()/dot_general | solution.py:1125
  180.2 2.4 fusion.99
  192.8 9.5 %fusion.101 = (f32[2048]{0:T(1024)}, bf16[1024,2048]{1,0:T(8,128)(2,1)}) fusion(f32[1024,2048]{1,0:T(8,128)} %get-tuple-element.241, f32[2048]{0:T(1024)S(1)} %slice.171, bf16[2048,512]{1,0:T(8,128)(2,1)S(1)} %bitcast.173, f32[1024,512]{1,0:T(8,128)} %get-tuple-element.187, f32[1024]{0:T(1024)S(1)} %negate_multiply_fusion.2), kind=kOutput, calls=%fused_computation.255 | convolution fusion | flops 2173696000 | bytes 16797696 | tf_op jit(solution)/shard_map/transpose(jvp())/dot_general | solution.py:1433
  202.3 6.7 %convolution_convert_fusion.3 = bf16[2048,512]{1,0:T(8,128)(2,1)} fusion(bf16[1024,2048]{1,0:T(8,128)(2,1)} %copy-done.144, f32[1024,512]{1,0:T(8,128)} %get-tuple-element.187, f32[1024]{0:T(1024)S(1)} %negate_multiply_fusion.2), kind=kOutput, calls=%fused_computation.38 | convolution fusion | flops 2149580800 | bytes 8392704 | tf_op jit(solution)/shard_map/transpose(jvp())/dot_general | solution.py:1433
  209.0 3.4 multiply_reduce_fusion.2
  212.4 4.0 convolution_convert_fusion.4
  221.4 13.5 %transpose_jvp_attention_backward__.2 = (bf16[1024,1536]{1,0:T(8,128)(2,1)S(1)}, f32[8,512]{1,0:T(8,128)S(1)}, f32[8,512]{1,0:T(8,128)S(1)}) custom-call(bf16[1024,1536]{1,0:T(8,128)(2,1)S(1)} %add_convert_fusion.joined, f32[4,16,128]{2,1,0:T(8,128)S(1)} %copy-done.23, bf16[1024,512]{1,0:T(8,128)(2,1)S(1)} %convolution_convert_fusion.6.grad), custom_call_target="tpu_custom_call" | custom-call | tf_op jit(solution)/shard_map/transpose(jvp(attention_backward))/pallas_call | solution.py:1429
  236.5 4.6 multiply_reduce_fusion.1
  248.7 4.0 fusion.100
  256.2 8.2 %transpose_jvp_attention_backward__.3 = (bf16[320,2304]{1,0:T(8,128)(2,1)S(1)}, f32[8,768]{1,0:T(8,128)S(1)}, f32[8,768]{1,0:T(8,128)S(1)}) custom-call(bf16[320,2304]{1,0:T(8,128)(2,1)S(1)} %fusion.9.joined, f32[2,1,160]{2,1,0:T(1,128)S(1)} %compare_convert_fusion.allowed, bf16[320,768]{1,0:T(8,128)(2,1)S(1)} %convolution_convert_fusion.9.grad), custom_call_target="tpu_custom_call" | custom-call | tf_op jit(solution)/shard_map/transpose(jvp(attention_backward))/pallas_call | solution.py:1415
  272.9 5.8 fusion.14.refs_4_
  278.7 4.0 convolution_convert_fusion
  282.8 4.7 convolution_convert_fusion.2
  287.5 4.6 convolution_convert_fusion.1
  292.1 171.6 %reduce_rows.1 = (f32[48,2304]{1,0:T(8,128)}, f32[48,768]{1,0:T(8,128)}, f32[48,3072]{1,0:T(8,128)}, f32[192,768]{1,0:T(8,128)}, f32[32,1536]{1,0:T(8,128)}, /*i...) custom-call(bf16[2,2,2,2,48,2304]{5,4,3,2,1,0:T(8,128)(2,1)} %bitcas, ...), custom_call_target="tpu_custom_call" | custom-call | tf_op jit(solution)/shard_map/reduce_rows/pallas_call | solution.py:720
  467.0 75.2 %orthogonalize.1 = (bf16[768,2304]{1,0:T(8,128)(2,1)}, bf16[768,768]{1,0:T(8,128)(2,1)}, bf16[768,3072]{1,0:T(8,128)(2,1)}, bf16[3072,768]{1,0:T(8,128)(2,1)}, b...) custom-call(bf16[768,2304]{1,0:T(8,128)(2,1)} %bitcast.187, ...), custom_call_target="tpu_custom_call" | custom-call | tf_op jit(solution)/shard_map/orthogonalize/pallas_call | solution.py:1052
  549.2 39.2 %return_rows.1 = (f32[48,2304]{1,0:T(8,128)S(1)}, f32[48,768]{1,0:T(8,128)S(1)}, f32[48,3072]{1,0:T(8,128)S(1)}, f32[192,768]{1,0:T(8,128)S(1)}, f32[32,1536]{1,...) custom-call(bf16[16,48,2304]{2,1,0:T(8,128)(2,1)} %bitcast.189, ...), custom_call_target="tpu_custom_call" | custom-call | tf_op jit(solution)/shard_map/return_rows/pallas_call | solution.py:843
  (445 shorter events, 104.3 us)
Async XLA Ops:
  0.7 10.7 %copy-start.130 = (s32[512]{0:T(512)S(1)}, s32[512]{0:T(512)}, u32[]{:S(2)}) copy-start(s32[512]{0:T(512)} %constant.280) | copy-start | bytes 6148
  140.6 20.5 %copy-start.80 = (f32[512]{0:T(512)}, f32[512]{0:T(512)S(1)}, u32[]{:S(2)}) copy-start(f32[512]{0:T(512)S(1)} %get-tuple-element.203) | copy-start | bytes 6148
  140.6 20.5 %copy-start.108 = (f32[512]{0:T(512)}, f32[512]{0:T(512)S(1)}, u32[]{:S(2)}) copy-start(f32[512]{0:T(512)S(1)} %get-tuple-element.202) | copy-start | bytes 6148
  141.5 14.1 %copy-start.98 = (f32[768]{0:T(1024)}, f32[768]{0:T(1024)S(1)}, u32[]{:S(2)}) copy-start(f32[768]{0:T(1024)S(1)} %get-tuple-element.206) | copy-start | bytes 9220
  141.5 14.1 %copy-start.124 = (f32[768]{0:T(1024)}, f32[768]{0:T(1024)S(1)}, u32[]{:S(2)}) copy-start(f32[768]{0:T(1024)S(1)} %get-tuple-element.207) | copy-start | bytes 9220
  159.4 11.5 %copy-start.46 = (f32[2,512,512]{2,1,0:T(8,128)}, f32[2,512,512]{2,1,0:T(8,128)S(1)}, u32[]{:S(2)}) copy-start(f32[2,512,512]{2,1,0:T(8,128)S(1)} %get-tuple-element.235) | copy-start | bytes 6291460
  221.4 15.1 %copy-start.47 = (f32[2,512,512]{2,1,0:T(8,128)S(1)}, f32[2,512,512]{2,1,0:T(8,128)}, u32[]{:S(2)}) copy-start(f32[2,512,512]{2,1,0:T(8,128)} %copy-done.46) | copy-start | bytes 6291460
  466.9 75.3 %copy-start.8 = (f32[32,2048]{1,0:T(8,128)S(1)}, f32[32,2048]{1,0:T(8,128)}, u32[]{:S(2)}) copy-start(f32[32,2048]{1,0:T(8,128)} %refs_14_.3) | copy-start | bytes 786436
  466.9 75.3 %copy-start.10 = (f32[128,512]{1,0:T(8,128)S(1)}, f32[128,512]{1,0:T(8,128)}, u32[]{:S(2)}) copy-start(f32[128,512]{1,0:T(8,128)} %refs_15_.3) | copy-start | bytes 786436
  466.9 75.3 %copy-start.15 = (f32[48,768]{1,0:T(8,128)S(1)}, f32[48,768]{1,0:T(8,128)}, u32[]{:S(2)}) copy-start(f32[48,768]{1,0:T(8,128)} %refs_9_.3) | copy-start | bytes 442372
  466.9 75.3 %copy-start.18 = (f32[48,512]{1,0:T(8,128)S(1)}, f32[48,512]{1,0:T(8,128)}, u32[]{:S(2)}) copy-start(f32[48,512]{1,0:T(8,128)} %refs_21_.1) | copy-start | bytes 294916
  466.9 75.3 %copy-start.20 = (f32[16,1280]{1,0:T(8,128)S(1)}, f32[16,1280]{1,0:T(8,128)}, u32[]{:S(2)}) copy-start(f32[16,1280]{1,0:T(8,128)} %refs_17_.3) | copy-start | bytes 245764
  466.9 75.3 %copy-start.22 = (f32[32,512]{1,0:T(8,128)S(1)}, f32[32,512]{1,0:T(8,128)}, u32[]{:S(2)}) copy-start(f32[32,512]{1,0:T(8,128)} %refs_13_.3) | copy-start | bytes 196612
  466.9 75.3 %copy-start.25 = (f32[48,512]{1,0:T(8,128)S(1)}, f32[48,512]{1,0:T(8,128)}, u32[]{:S(2)}) copy-start(f32[48,512]{1,0:T(8,128)} %refs_22_.1) | copy-start | bytes 294916
  466.9 75.3 %copy-start.26 = (f32[48,512]{1,0:T(8,128)S(1)}, f32[48,512]{1,0:T(8,128)}, u32[]{:S(2)}) copy-start(f32[48,512]{1,0:T(8,128)} %refs_23_.1) | copy-start | bytes 294916
  466.9 75.3 %copy-start.27 = (f32[48,512]{1,0:T(8,128)S(1)}, f32[48,512]{1,0:T(8,128)}, u32[]{:S(2)}) copy-start(f32[48,512]{1,0:T(8,128)} %get-tuple-element.124.refs_24_) | copy-start | bytes 294916
  467.0 75.3 %copy-start.28 = (f32[16,1280]{1,0:T(8,128)S(1)}, f32[16,1280]{1,0:T(8,128)}, u32[]{:S(2)}) copy-start(f32[16,1280]{1,0:T(8,128)} %refs_18_.3) | copy-start | bytes 245764
  467.0 75.3 %copy-start.29 = (f32[16,1280]{1,0:T(8,128)S(1)}, f32[16,1280]{1,0:T(8,128)}, u32[]{:S(2)}) copy-start(f32[16,1280]{1,0:T(8,128)} %refs_19_.3) | copy-start | bytes 245764
  467.0 75.3 %copy-start.30 = (f32[16,1280]{1,0:T(8,128)S(1)}, f32[16,1280]{1,0:T(8,128)}, u32[]{:S(2)}) copy-start(f32[16,1280]{1,0:T(8,128)} %get-tuple-element.123.refs_20_) | copy-start | bytes 245764
  467.0 75.3 %copy-start.31 = (f32[16,128]{1,0:T(8,128)S(1)}, f32[16,128]{1,0:T(8,128)}, u32[]{:S(2)}) copy-start(f32[16,128]{1,0:T(8,128)} %get-tuple-element.106.refs_16_) | copy-start | bytes 24580
  549.2 39.2 %copy-start.100 = (f32[16,256]{1,0:T(8,128)S(1)}, f32[16,256]{1,0:T(8,128)}, u32[]{:S(2)}) copy-start(f32[16,256]{1,0:T(8,128)} %get-tuple-element.147) | copy-start | bytes 49156
  549.2 39.2 %copy-start.76 = (f32[1248]{0:T(1024)S(1)}, f32[1248]{0:T(1024)}, u32[]{:S(2)}) copy-start(f32[1248]{0:T(1024)} %param.59) | copy-start | bytes 14980
  549.2 39.2 %copy-start.111 = (f32[1248]{0:T(1024)S(1)}, f32[1248]{0:T(1024)}, u32[]{:S(2)}) copy-start(f32[1248]{0:T(1024)} %param.60) | copy-start | bytes 14980
  549.2 39.2 %copy-start.112 = (f32[1248]{0:T(1024)S(1)}, f32[1248]{0:T(1024)}, u32[]{:S(2)}) copy-start(f32[1248]{0:T(1024)} %param.61) | copy-start | bytes 14980
  (127 other events, 442.8 us)

commit v3 on v2

--- a/solution.py
+++ b/solution.py
@@ -286,16 +286,16 @@
 
 MESH_ID = pl.DeviceIdType.MESH
 VEC_ROWS, VEC_COLS = 16, 256
-AXIS_ORDERS = ((3, 2, 1, 0), (3, 2, 0, 1), (0, 3, 2, 1), (1, 3, 2, 0), (0, 1, 3, 2), (1, 0, 3, 2))
+AXIS_ORDERS = ((0, 1, 2, 3), (0, 1, 3, 2), (0, 2, 1, 3), (0, 2, 3, 1), (0, 3, 1, 2), (0, 3, 2, 1), (1, 0, 2, 3), (1, 0, 3, 2), (1, 2, 0, 3), (1, 2, 3, 0), (1, 3, 0, 2), (1, 3, 2, 0), (2, 0, 1, 3), (2, 0, 3, 1), (2, 1, 0, 3), (2, 1, 3, 0), (2, 3, 0, 1), (2, 3, 1, 0), (3, 0, 1, 2), (3, 0, 2, 1), (3, 1, 0, 2), (3, 1, 2, 0), (3, 2, 0, 1), (3, 2, 1, 0))
 GATHER_PARTS = (3, 1, 4, 4, 1, 1, 2, 2, 1, 1, 1)
 REDUCE_PARTS = (3, 1, 4, 4, 2, 1, 2, 2, 1, 1, 1)
 TALL = (3, 7)
-GATHER_TURNS = (5, 1, 3, 2, 1, 0, 3, 0, 1, 5, 1, 5, 1, 5, 1, 0, 0, 1, 0, 5, 3)
-GATHER_FIRST = (3, 2, 17, 15, 4, 7, 10, 6, 19, 9, 16, 12, 8, 13, 20, 11, 0, 5, 14, 1, 18)
-GATHER_STEPS = ((3, 0), (2, 0), (17, 0), (6, 0), (19, 0), (15, 0), (9, 0), (13, 0), (20, 0), (11, 0), (4, 0), (0, 0), (19, 1), (7, 0), (9, 1), (10, 0), (13, 1), (16, 0), (11, 1), (12, 0), (0, 1), (8, 0), (5, 0), (14, 0), (1, 0), (18, 0), (3, 1), (17, 1), (2, 1), (15, 1), (6, 1), (20, 1), (4, 1), (17, 2), (15, 2), (7, 1), (19, 2), (4, 2), (10, 1), (17, 3), (9, 2), (15, 3), (7, 2), (13, 2), (16, 1), (10, 2), (4, 3), (12, 1), (11, 2), (7, 3), (16, 2), (8, 1), (12, 2), (0, 2), (5, 1), (14, 1), (10, 3), (1, 1), (18, 1), (16, 3), (3, 2), (8, 2), (2, 2), (12, 3), (14, 2), (6, 2), (5, 2), (20, 2), (1, 2), (18, 2), (19, 3), (2, 3), (3, 3), (9, 3), (6, 3), (13, 3), (8, 3), (5, 3), (11, 3), (14, 3), (20, 3), (18, 3), (0, 3), (1, 3))
-REDUCE_TURNS = (1, 0, 1, 1, 1, 1, 2, 1, 0, 1, 4, 0, 3, 2, 2, 3, 3, 3, 5, 4, 3, 0)
-REDUCE_FIRST = (10, 1, 13, 9, 18, 6, 7, 5, 11, 21, 8, 12, 16, 0, 17, 3, 20, 19, 4, 14, 2, 15)
-REDUCE_STEPS = ((10, 0), (1, 0), (13, 0), (18, 0), (11, 0), (21, 0), (9, 0), (10, 1), (13, 1), (8, 0), (6, 0), (18, 1), (19, 0), (12, 0), (7, 0), (13, 2), (6, 1), (19, 1), (16, 0), (5, 0), (12, 1), (1, 1), (6, 2), (17, 0), (16, 1), (20, 0), (1, 2), (0, 0), (12, 2), (17, 1), (15, 0), (16, 2), (20, 1), (3, 0), (1, 3), (9, 1), (18, 2), (17, 2), (15, 1), (4, 0), (7, 1), (13, 3), (20, 2), (9, 2), (11, 1), (5, 1), (6, 3), (15, 2), (7, 2), (14, 0), (21, 1), (9, 3), (11, 2), (0, 1), (5, 2), (7, 3), (3, 1), (14, 1), (21, 2), (2, 0), (11, 3), (0, 2), (10, 2), (4, 1), (5, 3), (3, 2), (8, 1), (14, 2), (21, 3), (19, 2), (2, 1), (12, 3), (10, 3), (0, 3), (16, 3), (4, 2), (18, 3), (14, 3), (17, 3), (19, 3), (20, 3), (3, 3), (15, 3), (8, 2), (2, 2), (4, 3), (8, 3), (2, 3))
+GATHER_TURNS = (19, 18, 22, 17, 13, 21, 22, 20, 3, 12, 11, 0, 17, 23, 16, 10, 23, 16, 11, 21, 21)
+GATHER_FIRST = (6, 17, 20, 11, 7, 16, 8, 13, 12, 1, 4, 9, 19, 10, 3, 2, 15, 5, 0, 14, 18)
+GATHER_STEPS = ((20, 11, 17, 6, 8, 10, 13, 15, 7, 16, 18, 19, 4, 1, 12, 9, 3, 2, 5, 14, 0), (20, 11, 7, 19, 4, 1, 17, 9, 6, 13, 8, 5, 0, 10, 16, 18, 15, 12, 3, 2, 14), (20, 7, 1, 17, 9, 13, 6, 16, 15, 11, 19, 4, 3, 12, 2, 8, 14, 10, 18, 5, 0), (20, 17, 13, 16, 6, 19, 7, 3, 4, 2, 1, 14, 12, 8, 18, 9, 10, 5, 15, 0, 11))
+REDUCE_TURNS = (14, 1, 1, 6, 7, 2, 12, 8, 20, 3, 21, 6, 6, 0, 0, 21, 10, 13, 2, 0, 17, 4)
+REDUCE_FIRST = (17, 21, 12, 9, 15, 18, 19, 4, 3, 11, 1, 10, 13, 20, 0, 7, 5, 16, 8, 14, 6, 2)
+REDUCE_STEPS = ((21, 17, 12, 9, 19, 15, 18, 4, 20, 3, 11, 10, 1, 0, 7, 14, 16, 5, 8, 13, 6, 2), (21, 17, 19, 15, 9, 12, 10, 14, 1, 20, 0, 18, 4, 8, 3, 7, 11, 13, 2, 16, 6, 5), (21, 17, 19, 20, 15, 18, 9, 14, 0, 10, 12, 8, 7, 16, 1, 6, 4, 5, 3, 11, 13, 2), (21, 17, 20, 15, 9, 19, 10, 18, 14, 0, 12, 8, 1, 16, 7, 6, 4, 5, 3, 2, 13, 11))
 OWNERS = (4, 11, 5, 10, 6, 9, 7, 8)
 SLOTS = 160
 
@@ -350,23 +350,49 @@
     pl.semaphore_wait(barrier, levels + 1)
 
 
-def add_up(me, own, core, levels, total, landing, send_sem, recv_sem):
-    for stage in range(levels + 1):
-        if stage < levels:
-            to = {"dp": partner(me, own, stage), "mp": core}
-        else:
-            to = {"dp": me, "mp": 1 - core}
-        swap = pltpu.make_async_remote_copy(
+def add_up(me, core, devices, total, landing, send_sem, recv_sem, own_sem):
+    def send(source, target):
+        return pltpu.make_async_remote_copy(
             src_ref=total,
-            dst_ref=landing.at[stage],
-            send_sem=send_sem.at[stage],
-            recv_sem=recv_sem.at[stage],
-            device_id=to,
+            dst_ref=landing.at[source],
+            send_sem=send_sem.at[target],
+            recv_sem=recv_sem.at[source],
+            device_id={"dp": target, "mp": core},
             device_id_type=MESH_ID,
         )
-        swap.start()
-        swap.wait()
-        total[...] = total[...] + landing[stage]
+
+    @pl.loop(0, devices)
+    def start_one(other):
+        @pl.when(other != me)
+        def start_other():
+            send(me, other).start()
+
+    own = pltpu.make_async_copy(total, landing.at[me], own_sem)
+    own.start()
+    own.wait()
+
+    @pl.loop(0, devices)
+    def wait_one(other):
+        @pl.when(other != me)
+        def wait_other():
+            send(other, me).wait_recv()
+            send(me, other).wait_send()
+
+    found = landing[0]
+    for device in range(1, devices):
+        found = found + landing[device]
+    total[...] = found
+    swap = pltpu.make_async_remote_copy(
+        src_ref=total,
+        dst_ref=landing.at[devices],
+        send_sem=send_sem.at[devices],
+        recv_sem=recv_sem.at[devices],
+        device_id={"dp": me, "mp": 1 - core},
+        device_id_type=MESH_ID,
+    )
+    swap.start()
+    swap.wait()
+    total[...] = total[...] + landing[devices]
 
 
 def gather_kernel(levels, pieces, count, *refs):
@@ -424,14 +450,37 @@
             keep(number).start()
         hop(piece, 0, False).start()
     tally_out[...] = tally[...]
-    add_up(me, own, core, levels, tally_out, tally_land, tally_send, tally_recv)
+
+    def swap(stage):
+        if stage < levels:
+            to = {"dp": partner(me, own, stage), "mp": core}
+        else:
+            to = {"dp": me, "mp": 1 - core}
+        return pltpu.make_async_remote_copy(
+            src_ref=tally_out,
+            dst_ref=tally_land.at[stage],
+            send_sem=tally_send.at[stage],
+            recv_sem=tally_recv.at[stage],
+            device_id=to,
+            device_id_type=MESH_ID,
+        )
+
+    def swap_end(stage):
+        swap(stage).wait()
+        tally_out[...] = tally_out[...] + tally_land[stage]
+
+    swap(levels).start()
     for number in range(count):
         keep(number).wait()
-    for piece, stage in GATHER_STEPS:
-        hop(piece, stage, True).wait_recv()
-        if stage + 1 < levels:
-            hop(piece, stage + 1, False).start()
-        cross(piece, stage, core).start()
+    swap_end(levels)
+    for stage, order in enumerate(GATHER_STEPS):
+        swap(stage).start()
+        for piece in order:
+            hop(piece, stage, True).wait_recv()
+            if stage + 1 < levels:
+                hop(piece, stage + 1, False).start()
+            cross(piece, stage, core).start()
+        swap_end(stage)
     for piece in range(len(pieces)):
         for stage in range(levels):
             hop(piece, stage, False).wait_send()
@@ -478,33 +527,19 @@
     stats_send, stats_recv, own_sem, out_send, out_recv, cross_send, cross_recv = rest[8:]
     me, own = own_bits(levels)
     core = lax.axis_index("mp")
-    orders = [AXIS_ORDERS[turn][::-1] for turn in REDUCE_TURNS]
-    owning = functools.reduce(jnp.logical_or, [me == owner for owner in owners])
+    orders = [AXIS_ORDERS[turn] for turn in REDUCE_TURNS]
     barrier = pltpu.get_barrier_semaphore()
-    for bit in range(levels):
-        pl.semaphore_signal(
-            barrier,
-            inc=1,
-            device_id={"dp": partner(me, own, bit), "mp": core},
-            device_id_type=MESH_ID,
-        )
+
+    @pl.loop(0, devices)
+    def greet_one(other):
+        @pl.when(other != me)
+        def signal_one():
+            pl.semaphore_signal(
+                barrier, inc=1, device_id={"dp": other, "mp": core}, device_id_type=MESH_ID
+            )
+
     pl.semaphore_signal(barrier, inc=1, device_id={"dp": me, "mp": 1 - core}, device_id_type=MESH_ID)
-
-    @pl.when(owning)
-    def greet_all():
-        @pl.loop(0, devices)
-        def greet_one(other):
-            @pl.when(other != me)
-            def signal_one():
-                pl.semaphore_signal(
-                    barrier, inc=1, device_id={"dp": other, "mp": core}, device_id_type=MESH_ID
-                )
-
-        pl.semaphore_wait(barrier, levels + blocks)
-
-    @pl.when(jnp.logical_not(owning))
-    def wait_owners():
-        pl.semaphore_wait(barrier, levels + 1 + blocks)
+    pl.semaphore_wait(barrier, devices)
 
     def half(number, which):
         width = sums[number].shape[1] // 2
@@ -630,7 +665,7 @@
         fold(piece, 0)
         hop(piece, 0).start()
     squares = jnp.zeros((8, 128), jnp.float32)
-    for piece, stage in REDUCE_STEPS:
+    for piece, stage in [(piece, stage) for stage in range(levels) for piece in REDUCE_STEPS[stage]]:
         hop(piece, stage).wait_recv()
         if stage + 1 < levels:
             fold(piece, stage + 1)
@@ -647,10 +682,10 @@
                     squares = squares + part * part
     for number in range(blocks, count):
         share(number, core).start()
-    stats_out[0:8, :] = squares
-    stats_out[8:16, :] = stats_in[...]
-    add_up(me, own, core, levels, stats_out, stats_land, stats_send, stats_recv)
-    norm = jnp.sqrt(jnp.sum(jnp.sum(stats_out[0:8, :], axis=0, keepdims=True), axis=1, keepdims=True))
+    row = lax.broadcasted_iota(jnp.int32, (8, 128), 0)
+    stats_out[...] = jnp.where(row == 0, jnp.sum(squares, axis=0, keepdims=True), stats_in[...])
+    add_up(me, core, devices, stats_out, stats_land, stats_send, stats_recv, own_sem)
+    norm = jnp.sqrt(jnp.sum(stats_out[0:1, :], axis=1, keepdims=True))
     factor = jnp.minimum(1.0, CLIP_MAX / (norm + 1e-06))
     for number in range(blocks):
         region = half(number, core)
@@ -713,14 +748,14 @@
         for stage in range(levels):
             scratch.append(pltpu.VMEM((2,) * (levels - 1 - stage) + (rows, columns), kinds[number]))
     scratch += [pltpu.VMEM(halves[number], kinds[number]) for number in range(blocks)]
-    scratch.append(pltpu.VMEM((levels + 1, 16, 128), jnp.float32))
+    scratch.append(pltpu.VMEM((devices + 1, 8, 128), jnp.float32))
     scratch += [dma((len(pieces),))] * 3 + [dma((len(pieces), levels))] * 2 + [dma((count,))] * 2
-    scratch += [dma((levels + 1,))] * 2 + [dma, dma((blocks,))] + [dma((blocks, devices))] * 3
+    scratch += [dma((devices + 1,))] * 2 + [dma, dma((blocks,))] + [dma((blocks, devices))] * 3
     vmem, anywhere = pl.BlockSpec(memory_space=pltpu.VMEM), pl.BlockSpec(memory_space=pl.ANY)
     found = pl.pallas_call(
         functools.partial(reduce_kernel, levels, pieces, count, owners, devices),
         out_shape=[jax.ShapeDtypeStruct(shape, jnp.float32) for shape in shapes]
-        + [jax.ShapeDtypeStruct((16, 128), jnp.float32)]
+        + [jax.ShapeDtypeStruct((8, 128), jnp.float32)]
         + [jax.ShapeDtypeStruct((devices,) + shapes[number], kinds[number]) for number in range(blocks)],
         in_specs=[anywhere] * count + [vmem] * (1 + blocks),
         out_specs=[vmem] * (count + 1) + [anywhere] * blocks,
@@ -733,12 +768,9 @@
     return found[:blocks], found[blocks:count], found[count], found[count + 1 :]
 
 
-def return_kernel(owners, count, devices, rates, *refs):
-    wholes, masters, rest = refs[:count], refs[count : 2 * count], refs[2 * count :]
-    stats, adam_in, rest = rest[0], rest[1:9], rest[9:]
-    updated, adam_out, rest = rest[:count], rest[count : count + 6], rest[count + 6 :]
-    rows, rest = rest[:count], rest[count:]
-    here_sem, send_sem, recv_sem, cross_send, cross_recv = rest
+def return_kernel(owners, count, devices, *refs):
+    wholes, rows = refs[:count], refs[count : 2 * count]
+    here_sem, send_sem, recv_sem, cross_send, cross_recv = refs[2 * count :]
     me, core = lax.axis_index("dp"), lax.axis_index("mp")
     barrier = pltpu.get_barrier_semaphore()
     owning = functools.reduce(jnp.logical_or, [me == owner for owner in owners])
@@ -802,13 +834,6 @@
 
             own.wait()
 
-    norm = jnp.sqrt(jnp.sum(jnp.sum(stats[0:8, :], axis=0, keepdims=True), axis=1, keepdims=True))
-    factor = jnp.minimum(1.0, CLIP_MAX / (norm + 1e-06))
-    for place_in in range(2):
-        weight, first, second, grad = [ref[...] for ref in adam_in[4 * place_in : 4 * place_in + 4]]
-        made = adam_update(weight, first, second, grad * factor, DECAY)
-        for place_out in range(3):
-            adam_out[3 * place_in + place_out][...] = made[place_out]
     for number in range(count):
 
         @pl.when(me != owners[number])
@@ -819,9 +844,6 @@
     for number in range(count):
         cross(number, core).wait_send()
         cross(number, 1 - core).wait_recv()
-        updated[number][...] = masters[number][...] * (1.0 - LR_MUON * DECAY) - rates[number] * rows[
-            number
-        ][...].astype(jnp.float32)
 
         @pl.when(me == owners[number])
         def end_out(number=number):
@@ -832,34 +854,70 @@
                     hop(number, target).wait_send()
 
 
-def return_rows(wholes, masters, stats, adam, owners, devices):
+def return_rows(wholes, owners, devices):
     count = len(wholes)
-    rates = []
-    for whole in wholes:
-        rates.append(LR_MUON * 0.2 * math.sqrt(max(whole.shape[0] * whole.shape[1], whole.shape[2])))
     dma = pltpu.SemaphoreType.DMA
     vmem = pl.BlockSpec(memory_space=pltpu.VMEM)
-    moved = (adam[0], adam[1], adam[2], adam[4], adam[5], adam[6])
-    found = pl.pallas_call(
-        functools.partial(return_kernel, owners, count, devices, rates),
-        out_shape=[jax.ShapeDtypeStruct(master.shape, jnp.float32) for master in masters]
-        + [jax.ShapeDtypeStruct(piece.shape, jnp.float32) for piece in moved],
-        in_specs=[pl.BlockSpec(memory_space=pl.ANY)] * count + [vmem] * (count + 9),
-        out_specs=[vmem] * (count + 6),
-        scratch_shapes=[pltpu.VMEM(whole.shape[1:], whole.dtype) for whole in wholes]
-        + [dma, dma((count, devices)), dma((count,)), dma((count,)), dma((count,))],
+    return pl.pallas_call(
+        functools.partial(return_kernel, owners, count, devices),
+        out_shape=[jax.ShapeDtypeStruct(whole.shape[1:], whole.dtype) for whole in wholes],
+        in_specs=[pl.BlockSpec(memory_space=pl.ANY)] * count,
+        out_specs=[vmem] * count,
+        scratch_shapes=[dma, dma((count, devices)), dma((count,)), dma((count,)), dma((count,))],
         compiler_params=pltpu.CompilerParams(
-            collective_id=4, has_side_effects=True, vmem_limit_bytes=40 * 2**20
+            collective_id=4, has_side_effects=True, vmem_limit_bytes=60 * 2**20
         ),
         name="return_rows",
-    )(*wholes, *masters, stats, *adam)
-    return found[:count], found[count : count + 3], found[count + 3 :]
+    )(*wholes)
+
+
+def finish_kernel(count, rates, *refs):
+    rows, masters, updated = refs[:count], refs[count : 2 * count], refs[2 * count :]
+    for number in range(count):
+        change = rates[number] * rows[number][...].astype(jnp.float32)
+        updated[number][...] = masters[number][...] * (1.0 - LR_MUON * DECAY) - change
+
+
+def finish(rows, masters, devices):
+    count = len(rows)
+    rates = []
+    for master in masters:
+        rates.append(LR_MUON * 0.2 * math.sqrt(max(master.shape[0] * devices, master.shape[1])))
+    vmem = pl.BlockSpec(memory_space=pltpu.VMEM)
+    return pl.pallas_call(
+        functools.partial(finish_kernel, count, rates),
+        out_shape=[jax.ShapeDtypeStruct(master.shape, jnp.float32) for master in masters],
+        in_specs=[vmem] * (2 * count),
+        out_specs=[vmem] * count,
+        compiler_params=pltpu.CompilerParams(vmem_limit_bytes=56 * 2**20),
+        name="finish",
+    )(*rows, *masters)
 
 
 def muon_kernel(owners, shapes, *refs):
     count = len(owners)
-    mats, outs = refs[:count], refs[count : 2 * count]
-    exact, wide, wide_low, tall, wide_out, tall_out, gram, square, poly, chain, left, right, sem = refs[2 * count :]
+    mats, moved, stats, adam_in = refs[:count], refs[count : 2 * count], refs[2 * count], refs[2 * count + 1 :][:8]
+    rest = refs[2 * count + 9 :]
+    outs, moved_out, adam_out, rest = rest[:count], rest[count : 2 * count], rest[2 * count :][:6], rest[2 * count + 6 :]
+    exact, wide, wide_low, tall, wide_out, tall_out, gram = rest[:7]
+    base, poly, other, chain, sem, in_sem, out_sem = rest[7:14]
+    held_rows = rest[14:]
+
+    def move_in(number):
+        return pltpu.make_async_copy(moved[number], held_rows[number], in_sem.at[number])
+
+    def move_out(number):
+        return pltpu.make_async_copy(held_rows[number], moved_out[number], out_sem.at[number])
+
+    for number in range(count):
+        move_in(number).start()
+    norm = jnp.sqrt(jnp.sum(stats[0:1, :], axis=1, keepdims=True))
+    factor = jnp.minimum(1.0, CLIP_MAX / (norm + 1e-06))
+    for group in range(2):
+        weight, first, second, grad = [ref[...] for ref in adam_in[4 * group : 4 * group + 4]]
+        made = adam_update(weight, first, second, grad * factor, DECAY)
+        for place_out in range(3):
+            adam_out[3 * group + place_out][...] = made[place_out]
     me, core = lax.axis_index("dp"), lax.axis_index("mp")
     side = gram.shape[0]
     step = 256
@@ -897,105 +955,88 @@
                     held[span(index), :] = high
                     rest[span(index), :] = low
 
-            @pl.loop(0, short // step)
-            def gram_rows(index):
+            for index in range(short // step):
+                first, beyond = slice(index * step, (index + 1) * step), slice(index * step, short)
                 if long_cols:
-                    part = held[span(index), :]
-                    dims_in = (((1,), (1,)), ((), ()))
+                    total = dot_rows(held[first, :], held[beyond, :])
+                    if fine:
+                        total = total + dot_rows(held[first, :], rest[beyond, :])
+                        total = total + dot_rows(rest[first, :], held[beyond, :])
                 else:
-                    part = held[:, span(index)]
-                    dims_in = (((0,), (0,)), ((), ()))
-                total = lax.dot_general(part, held[...], dims_in, preferred_element_type=jnp.float32)
-                if fine:
-                    total = total + lax.dot_general(
-                        part, rest[...], dims_in, preferred_element_type=jnp.float32
-                    )
-                    total = total + lax.dot_general(
-                        rest[span(index), :], held[...], dims_in, preferred_element_type=jnp.float32
-                    )
-                gram[span(index), :short] = total
-
+                    total = dot_columns(held[:, first], held[:, beyond])
+                gram[first, beyond] = total
+
+    for number in range(count):
+        move_in(number).wait()
+        move_out(number).start()
     owning = functools.reduce(jnp.logical_or, [me == owner for owner in owners])
 
     @pl.when(owning)
     def iterate():
-        def eye(index):
-            row = lax.broadcasted_iota(jnp.int32, (step, side), 0) + index * step
-            column = lax.broadcasted_iota(jnp.int32, (step, side), 1)
-            return row == column
-
+        parts = [
+            (slice(index * step, (index + 1) * step), slice(index * step, side))
+            for index in range(side // step)
+        ]
+        ones = lax.broadcasted_iota(jnp.int32, (step, step), 0) == lax.broadcasted_iota(
+            jnp.int32, (step, step), 1
+        )
         trace = jnp.float32(0.0)
-        for index in range(side // step):
-            trace = trace + jnp.sum(jnp.where(eye(index), gram[index * step : (index + 1) * step, :], 0.0))
+        for first, beyond in parts:
+            trace = trace + jnp.sum(jnp.where(ones, gram[first, first], 0.0))
         scale = 1.0 / (jnp.sqrt(jnp.full((8, 128), trace, jnp.float32)) + 1e-07)
         scale = scale[0:1, 0:1]
-        square_scale = scale * scale
-
-        @pl.loop(0, side // step)
-        def prepare(index):
-            gram[span(index), :] = gram[span(index), :] * square_scale
-
-        def set_left(source):
-            @pl.loop(0, side // step)
-            def set_rows(index):
-                high, low = split(source[span(index), :])
-                left[span(index), 0:side] = high
-                left[span(index), side : 2 * side] = high
-                left[span(index), 2 * side : 3 * side] = low
-
-        def set_right(source):
-            @pl.loop(0, side // step)
-            def set_rows(index):
-                high, low = split(source[span(index), :])
-                right[pl.ds(pl.multiple_of(index * step, step), step), :] = high
-                right[pl.ds(pl.multiple_of(side + index * step, step), step), :] = low
-                right[pl.ds(pl.multiple_of(2 * side + index * step, step), step), :] = high
-
-        def multiply(target):
-            @pl.loop(0, side // step)
-            def rows(index):
-                target[span(index), :] = jnp.dot(
-                    left[span(index), :], right[...], preferred_element_type=jnp.float32
-                )
+
+        def store(target, index, value):
+            high, low = split(value)
+            target[0, parts[index][0], parts[index][1]] = high
+            target[1, parts[index][0], parts[index][1]] = low
+            for later in range(index + 1, side // step):
+                shift = (later - index) * step
+                high, low = split(value[:, shift : shift + step].T)
+                target[0, parts[later][0], parts[index][0]] = high
+                target[1, parts[later][0], parts[index][0]] = low
+
+        def product(left, right, index):
+            first, beyond = parts[index]
+            high, low = left[0, first, :], left[1, first, :]
+            total = jnp.dot(high, right[0, :, beyond], preferred_element_type=jnp.float32)
+            total = total + jnp.dot(high, right[1, :, beyond], preferred_element_type=jnp.float32)
+            return total + jnp.dot(low, right[0, :, beyond], preferred_element_type=jnp.float32)
+
+        for index, (first, beyond) in enumerate(parts):
+            store(base, index, gram[first, beyond] * (scale * scale))
 
         @pl.loop(0, NS_ITERS)
         def newton(iteration):
-            set_left(gram)
-            set_right(gram)
-            multiply(square)
-
-            @pl.loop(0, side // step)
-            def polynomial(index):
-                ones = jnp.where(
-                    lax.broadcasted_iota(jnp.int32, (step, side), 0) + index * step
-                    == lax.broadcasted_iota(jnp.int32, (step, side), 1),
-                    NS_A,
-                    0.0,
-                )
-                poly[span(index), :] = ones + NS_B * gram[span(index), :] + NS_C * square[span(index), :]
-
-            set_right(poly)
+            for index, (first, beyond) in enumerate(parts):
+                now = base[0, first, beyond].astype(jnp.float32) + base[1, first, beyond].astype(jnp.float32)
+                row = lax.broadcasted_iota(jnp.int32, now.shape, 0)
+                column = lax.broadcasted_iota(jnp.int32, now.shape, 1)
+                value = jnp.where(row == column, NS_A, 0.0) + NS_B * now
+                store(poly, index, value + NS_C * product(base, base, index))
 
             @pl.when(iteration < NS_ITERS - 1)
             def advance():
-                multiply(square)
-                set_left(square)
-                multiply(gram)
+                for index in range(len(parts)):
+                    store(other, index, product(base, poly, index))
+                for index in range(len(parts)):
+                    store(base, index, product(other, poly, index))
 
             @pl.when(iteration == 0)
-            def first():
+            def begin():
                 chain[...] = poly[...]
 
             @pl.when(iteration > 0)
-            def later():
-                set_left(chain)
-                multiply(chain)
-
-        @pl.loop(0, side // step)
-        def finish(index):
-            high, low = split(chain[span(index), :] * scale)
-            left[span(index), 0:side] = high
-            left[span(index), side : 2 * side] = low
+            def follow():
+                for index in range(len(parts)):
+                    store(other, index, product(chain, poly, index))
+                chain[...] = other[...]
+
+        for first, beyond in parts:
+            value = chain[0, first, :].astype(jnp.float32) + chain[1, first, :].astype(jnp.float32)
+            high, low = split(value * scale)
+            other[0, first, :] = high
+            other[1, first, :] = low
 
     for number in range(count):
 
@@ -1011,15 +1052,13 @@
                 @pl.loop(0, height // step)
                 def wide_rows(index):
                     total = jnp.dot(
-                        left[span(index), :short], held[:, part], preferred_element_type=jnp.float32
+                        other[0, span(index), :short], held[:, part], preferred_element_type=jnp.float32
                     ) + jnp.dot(
-                        left[span(index), side : side + short],
-                        held[:, part],
-                        preferred_element_type=jnp.float32,
+                        other[1, span(index), :short], held[:, part], preferred_element_type=jnp.float32
                     )
                     if mats[number].dtype == jnp.float32:
                         total = total + jnp.dot(
-                            left[span(index), :short],
+                            other[0, span(index), :short],
                             wide_low[:, part],
                             preferred_element_type=jnp.float32,
                         )
@@ -1029,11 +1068,10 @@
 
                 @pl.loop(0, height // step)
                 def tall_rows(index):
-                    low = pl.ds(pl.multiple_of(side + core * width, 128), width)
                     total = jnp.dot(
-                        held[span(index), :], left[:short, part], preferred_element_type=jnp.float32
+                        held[span(index), :], other[0, :short, part], preferred_element_type=jnp.float32
                     ) + jnp.dot(
-                        held[span(index), :], left[:short, low], preferred_element_type=jnp.float32
+                        held[span(index), :], other[1, :short, part], preferred_element_type=jnp.float32
                     )
                     made[span(index), :] = total.astype(bf)
 
@@ -1041,19 +1079,26 @@
             save.start()
             save.wait()
 
-
-def orthogonalize(mats, owners):
+    for number in range(count):
+        move_out(number).wait()
+
+
+def orthogonalize(mats, moved, stats, adam, owners):
     count = len(mats)
     shapes = [mat.shape for mat in mats]
     side = max(min(shape) for shape in shapes)
     longest = max(max(shape) for shape in shapes)
-    square = pltpu.VMEM((side, side), jnp.float32)
+    double = pltpu.VMEM((2, side, side), jnp.bfloat16)
     (fine,) = [mat.shape for mat in mats if mat.dtype == jnp.float32]
-    return pl.pallas_call(
+    vmem, anywhere = pl.BlockSpec(memory_space=pltpu.VMEM), pl.BlockSpec(memory_space=pl.ANY)
+    renewed = (adam[0], adam[1], adam[2], adam[4], adam[5], adam[6])
+    found = pl.pallas_call(
         functools.partial(muon_kernel, owners, shapes),
-        out_shape=[jax.ShapeDtypeStruct(shape, jnp.bfloat16) for shape in shapes],
-        in_specs=[pl.BlockSpec(memory_space=pl.ANY)] * count,
-        out_specs=[pl.BlockSpec(memory_space=pl.ANY)] * count,
+        out_shape=[jax.ShapeDtypeStruct(shape, jnp.bfloat16) for shape in shapes]
+        + [jax.ShapeDtypeStruct(piece.shape, piece.dtype) for piece in moved]
+        + [jax.ShapeDtypeStruct(piece.shape, piece.dtype) for piece in renewed],
+        in_specs=[anywhere] * (2 * count) + [vmem] * 9,
+        out_specs=[anywhere] * (2 * count) + [vmem] * 6,
         scratch_shapes=[
             pltpu.VMEM(fine, jnp.float32),
             pltpu.VMEM((side, longest), jnp.bfloat16),
@@ -1061,17 +1106,20 @@
             pltpu.VMEM((longest, side), jnp.bfloat16),
             pltpu.VMEM((side, longest // 2), jnp.bfloat16),
             pltpu.VMEM((longest, side // 2), jnp.bfloat16),
-            square,
-            square,
-            square,
-            square,
-            pltpu.VMEM((side, 3 * side), jnp.bfloat16),
-            pltpu.VMEM((3 * side, side), jnp.bfloat16),
+            pltpu.VMEM((side, side), jnp.float32),
+            double,
+            double,
+            double,
+            double,
             pltpu.SemaphoreType.DMA,
-        ],
-        compiler_params=pltpu.CompilerParams(vmem_limit_bytes=56 * 2**20),
+            pltpu.SemaphoreType.DMA((count,)),
+            pltpu.SemaphoreType.DMA((count,)),
+        ]
+        + [pltpu.VMEM(piece.shape, piece.dtype) for piece in moved],
+        compiler_params=pltpu.CompilerParams(vmem_limit_bytes=60 * 2**20),
         name="orthogonalize",
-    )(*mats)
+    )(*mats, *moved, stats, *adam)
+    return found[:count], found[count : 2 * count], found[2 * count : 2 * count + 3], found[2 * count + 3 :]
 
 
 def window_place(position):
@@ -1472,15 +1520,16 @@
         grad = grads[number]
         grads[number] = grad.reshape(lead + (grad.shape[0] // devices, grad.shape[1]))
     renewed, others, stats, collected = reduce_rows(
-        grads, jnp.where(first, loss_part, 0.0), moments, OWNERS, devices
-    )
-    loss_sum = stats[8, 0]
-    grad_norm = jnp.sqrt(jnp.sum(stats[:8]))
+        grads, jnp.where(jnp.logical_and(row == 1, column == 0), loss_part, 0.0), moments, OWNERS, devices
+    )
+    loss_sum = stats[1, 0]
+    grad_norm = jnp.sqrt(jnp.sum(stats[0]))
     factor = jnp.minimum(1.0, CLIP_MAX / (grad_norm + 1e-06))
-    made = orthogonalize([piece.reshape(-1, piece.shape[2]) for piece in collected], OWNERS)
+    adam = (*rest[16:19], others[0], *rest[19:22], others[1])
+    flat = [piece.reshape(-1, piece.shape[2]) for piece in collected]
+    made, renewed, patch_new, embed_new = orthogonalize(flat, renewed, stats, adam, OWNERS)
     made = [piece.reshape(devices, -1, piece.shape[1]) for piece in made]
-    adam = (*rest[16:19], others[0], *rest[19:22], others[1])
-    new_weights, patch_new, embed_new = return_rows(made, masters[:8], stats, adam, OWNERS, devices)
+    new_weights = finish(return_rows(made, OWNERS, devices), masters[:8], devices)
     vector_grad = others[2].reshape(-1)[:vector_rows] * factor
     vector_new = adam_update(*rest[22:25], vector_grad, 0.0)
     return (loss_sum, mask_count, grad_norm, *new_weights, *renewed, *patch_new, *embed_new, *vector_new)

time: 617 us -> 513 us (0.83)
  Pallas kernels: 423 us -> 360 us
  local copies, waits for them, and re-layouts: 55.3 us -> 22.5 us
  matrix products: 99.4 us -> 93.1 us
    pallas_call x1, Pallas kernels: 75.2 us -> 44.4 us  [orthogonalize(): pl.pallas_call(functools.partial(muon_kernel, owners, shapes), out_shape=...]
    unnamed x332 -> x226, local copies, waits for them, and re-layouts: 42 us -> 15.5 us
    pallas_call x1, Pallas kernels: 172 us -> 149 us  [reduce_rows(): pl.pallas_call(functools.partial(reduce_kernel, levels, pieces, count, ow...]
    pallas_call x1, Pallas kernels: 105 us -> 92.4 us  [gather_rows(): pl.pallas_call(functools.partial(gather_kernel, levels, pieces, count), o...]
    pallas_call x1 -> x2, Pallas kernels: 39.2 us -> 41.8 us  [the longest x1 38 us: return_rows(): pl.pallas_call(functools.partial(return_kernel, owners, count, devices),...]
where the time goes in v3:
time: 513 us; the launch traced here: 503 us
  Pallas kernels  360 us (70%)
  matrix products  93.1 us (18%)
  local copies, waits for them, and re-layouts  22.5 us (4%)
  other arithmetic  21.3 us (4%)
  between operations  6.13 us (1%)
    pallas_call x1, Pallas kernels, reduce_rows(): pl.pallas_call(functools.partial(reduce_kernel, levels, pieces, count, ow...  149 us
    pallas_call x1, Pallas kernels, gather_rows(): pl.pallas_call(functools.partial(gather_kernel, levels, pieces, count), o...  92.4 us
    pallas_call x1, Pallas kernels, orthogonalize(): pl.pallas_call(functools.partial(muon_kernel, owners, shapes), out_shape=...  44.4 us
    pallas_call x1, Pallas kernels, return_rows(): pl.pallas_call(functools.partial(return_kernel, owners, count, devices),...  38 us
    dot_general x9, matrix products, times_keep(): jnp.dot(short, matrix.astype(jnp.bfloat16), preferred_element_type=jnp.fl...  19 us
    unnamed x226, local copies, waits for them, and re-layouts  15.5 us
    dot_general x2, matrix products, local_loss(): hidden = hidden + times(inner, weights[7]) + pieces[10]  15.2 us
    pallas_call x1, Pallas kernels, local_loss(): decoder_attention(normed, weights[4], pieces[4], pieces[5], jnp.asarray(w...  13.5 us

profile of v3, /device:TPU:15, one launch (start us, length us, event | category | flops | bytes accessed | tf_op | source)
XLA Modules:
  0.0 502.6 jit_solution(7732325032314858418)
XLA Ops:
  8.3 3.5 fusion.36
  12.6 2.5 convert_reduce_fusion
  17.3 92.4 %gather_rows.1 = (bf16[2,2,2,2,48,2304]{5,4,3,2,1,0:T(8,128)(2,1)S(1)}, bf16[2,2,2,2,48,768]{5,4,3,2,1,0:T(8,128)(2,1)S(1)}, bf16[2,2,2,2,48,3072]{5,4,3,2,1,0:T...) custom-call(f32[48,2304]{1,0:T(8,128)S(1)} %copy-done.2, ...), custom_call_target="tpu_custom_call" | custom-call | tf_op jit(solution)/shard_map/gather_rows/pallas_call | solution.py:497
  122.6 2.8 jvp_attention_forward_.2
  126.5 4.1 multiply_convert_fusion.1
  134.0 2.4 fusion.97
  140.7 7.2 %jvp_attention_forward_.3 = bf16[1024,512]{1,0:T(8,128)(2,1)S(1)} custom-call(bf16[1024,1536]{1,0:T(8,128)(2,1)S(1)} %add_convert_fusion.joined, f32[4,16,128]{2,1,0:T(8,128)S(1)} %copy-done.10), custom_call_target="tpu_custom_call" | custom-call | tf_op jit(solution)/shard_map/jvp(attention_forward)/pallas_call | solution.py:1356
  151.1 6.0 %multiply_convert_fusion = (bf16[1024,2048]{1,0:T(8,128)(2,1)S(1)}, f32[1024,2048]{1,0:T(8,128)}) fusion(f32[2048]{0:T(1024)S(1)} %slice.171, bf16[512,2048]{1,0:T(8,128)(2,1)S(1)} %bitcast.165, f32[1024,512]{1,0:T(8,128)S(1)} %get-tuple-element.269, f32[512]{0:T(512)S(1)} %get-tuple-element.229, f32[512]{0:T(512)S(1)} %get-tuple-element.230, ...), kind=kOutput, calls=%fused_computation.7 | convolution fusion | flops 2162688000 | bytes 16797696 | tf_op jit(solution)/shard_map/jvp()/dot_general | solution.py:1173
  168.7 9.0 %fusion.101 = (f32[2048]{0:T(1024)S(1)}, bf16[1024,2048]{1,0:T(8,128)(2,1)}) fusion(f32[1024,2048]{1,0:T(8,128)} %get-tuple-element.273, f32[2048]{0:T(1024)S(1)} %slice.171, bf16[2048,512]{1,0:T(8,128)(2,1)S(1)} %bitcast.168, f32[1024,512]{1,0:T(8,128)} %get-tuple-element.219, f32[1024]{0:T(1024)S(1)} %negate_multiply_fusion.2), kind=kOutput, calls=%fused_computation.256 | convolution fusion | flops 2173696000 | bytes 16797696 | tf_op jit(solution)/shard_map/transpose(jvp())/dot_general | solution.py:1481
  177.8 6.1 %convolution_convert_fusion.3 = bf16[2048,512]{1,0:T(8,128)(2,1)} fusion(bf16[1024,2048]{1,0:T(8,128)(2,1)} %copy-done.102, f32[1024,512]{1,0:T(8,128)S(1)} %copy-done.34, f32[1024]{0:T(1024)S(1)} %negate_multiply_fusion.2), kind=kOutput, calls=%fused_computation.38 | convolution fusion | flops 2149580800 | bytes 8392704 | tf_op jit(solution)/shard_map/transpose(jvp())/dot_general | solution.py:1481
  184.0 2.8 multiply_reduce_fusion.2
  186.8 3.9 convolution_convert_fusion.4
  194.3 13.5 %transpose_jvp_attention_backward__.2 = (bf16[1024,1536]{1,0:T(8,128)(2,1)S(1)}, f32[8,512]{1,0:T(8,128)S(1)}, f32[8,512]{1,0:T(8,128)S(1)}) custom-call(bf16[1024,1536]{1,0:T(8,128)(2,1)S(1)} %add_convert_fusion.joined, f32[4,16,128]{2,1,0:T(8,128)S(1)} %copy-done.10, bf16[1024,512]{1,0:T(8,128)(2,1)S(1)} %convolution_convert_fusion.6.grad), custom_call_target="tpu_custom_call" | custom-call | tf_op jit(solution)/shard_map/transpose(jvp(attention_backward))/pallas_call | solution.py:1477
  207.9 3.2 multiply_reduce_fusion.1
  218.7 4.0 fusion.100
  226.1 8.2 %transpose_jvp_attention_backward__.3 = (bf16[320,2304]{1,0:T(8,128)(2,1)S(1)}, f32[8,768]{1,0:T(8,128)S(1)}, f32[8,768]{1,0:T(8,128)S(1)}) custom-call(bf16[320,2304]{1,0:T(8,128)(2,1)S(1)} %fusion.9.joined, f32[2,1,160]{2,1,0:T(1,128)S(1)} %compare_convert_fusion.allowed, bf16[320,768]{1,0:T(8,128)(2,1)S(1)} %convolution_convert_fusion.9.grad), custom_call_target="tpu_custom_call" | custom-call | tf_op jit(solution)/shard_map/transpose(jvp(attention_backward))/pallas_call | solution.py:1463
  243.4 4.8 fusion.14.refs_4_
  248.2 4.0 convolution_convert_fusion
  252.3 4.7 convolution_convert_fusion.2
  257.0 4.6 convolution_convert_fusion.1
  261.5 149.4 %reduce_rows.1 = (f32[48,2304]{1,0:T(8,128)}, f32[48,768]{1,0:T(8,128)}, f32[48,3072]{1,0:T(8,128)}, f32[192,768]{1,0:T(8,128)}, f32[32,1536]{1,0:T(8,128)}, /*i...) custom-call(bf16[2,2,2,2,48,2304]{5,4,3,2,1,0:T(8,128)(2,1)} %bitcas, ...), custom_call_target="tpu_custom_call" | custom-call | tf_op jit(solution)/shard_map/reduce_rows/pallas_call | solution.py:755
  414.1 44.4 %orthogonalize.1 = (bf16[768,2304]{1,0:T(8,128)(2,1)}, bf16[768,768]{1,0:T(8,128)(2,1)}, bf16[768,3072]{1,0:T(8,128)(2,1)}, bf16[3072,768]{1,0:T(8,128)(2,1)}, b...) custom-call(bf16[768,2304]{1,0:T(8,128)(2,1)} %bitcast.183, ...), custom_call_target="tpu_custom_call" | custom-call | tf_op jit(solution)/shard_map/orthogonalize/pallas_call | solution.py:1095
  458.5 38.0 %return_rows.1 = (bf16[48,2304]{1,0:T(8,128)(2,1)}, bf16[48,768]{1,0:T(8,128)(2,1)}, bf16[48,3072]{1,0:T(8,128)(2,1)}, bf16[192,768]{1,0:T(8,128)(2,1)}, bf16[32...) custom-call(bf16[16,48,2304]{2,1,0:T(8,128)(2,1)} %bitcast.182, ...), custom_call_target="tpu_custom_call" | custom-call | tf_op jit(solution)/shard_map/return_rows/pallas_call | solution.py:861
  497.2 3.8 finish.1
  (341 shorter events, 71.2 us)
Async XLA Ops:
  0.7 11.2 %copy-start.89 = (s32[512]{0:T(512)S(1)}, s32[512]{0:T(512)}, u32[]{:S(2)}) copy-start(s32[512]{0:T(512)} %constant.281) | copy-start | bytes 6148
  15.9 103.0 %copy-start.41 = (bf16[2,160,256]{2,1,0:T(8,128)(2,1)}, bf16[2,160,256]{2,1,0:T(8,128)(2,1)S(1)}, u32[]{:S(2)}) copy-start(bf16[2,160,256]{2,1,0:T(8,128)(2,1)S(1)} %convolution_convert_fusion.12) | copy-start | bytes 491524
  118.8 19.3 %copy-start.47 = (f32[512]{0:T(512)}, f32[512]{0:T(512)S(1)}, u32[]{:S(2)}) copy-start(f32[512]{0:T(512)S(1)} %get-tuple-element.235) | copy-start | bytes 6148
  118.9 19.3 %copy-start.73 = (f32[512]{0:T(512)}, f32[512]{0:T(512)S(1)}, u32[]{:S(2)}) copy-start(f32[512]{0:T(512)S(1)} %get-tuple-element.234) | copy-start | bytes 6148
  118.9 7.5 %copy-start.61 = (f32[768]{0:T(1024)}, f32[768]{0:T(1024)S(1)}, u32[]{:S(2)}) copy-start(f32[768]{0:T(1024)S(1)} %get-tuple-element.242) | copy-start | bytes 9220
  118.9 7.5 %copy-start.83 = (f32[768]{0:T(1024)}, f32[768]{0:T(1024)S(1)}, u32[]{:S(2)}) copy-start(f32[768]{0:T(1024)S(1)} %get-tuple-element.241) | copy-start | bytes 9220
  118.9 13.8 %copy-start.65 = (f32[768]{0:T(1024)}, f32[768]{0:T(1024)S(1)}, u32[]{:S(2)}) copy-start(f32[768]{0:T(1024)S(1)} %get-tuple-element.238) | copy-start | bytes 9220
  119.0 13.8 %copy-start.87 = (f32[768]{0:T(1024)}, f32[768]{0:T(1024)S(1)}, u32[]{:S(2)}) copy-start(f32[768]{0:T(1024)S(1)} %get-tuple-element.239) | copy-start | bytes 9220
  148.7 8.3 %copy-start.26 = (f32[1024,512]{1,0:T(8,128)}, f32[1024,512]{1,0:T(8,128)S(1)}, u32[]{:S(2)}) copy-start(f32[1024,512]{1,0:T(8,128)S(1)} %get-tuple-element.269) | copy-start | bytes 6291460
  168.7 9.0 %copy-start.34 = (f32[1024,512]{1,0:T(8,128)S(1)}, f32[1024,512]{1,0:T(8,128)}, u32[]{:S(2)}) copy-start(f32[1024,512]{1,0:T(8,128)} %get-tuple-element.219) | copy-start | bytes 6291460
  194.3 13.6 %copy-start.48 = (f32[512]{0:T(512)S(1)}, f32[512]{0:T(512)}, u32[]{:S(2)}) copy-start(f32[512]{0:T(512)} %copy-done.47) | copy-start | bytes 6148
  194.3 13.6 %copy-start.69 = (f32[1,4,2,128]{3,1,2,0:T(4,128)S(1)}, f32[1,4,2,128]{3,1,2,0:T(4,128)}, u32[]{:S(2)}) copy-start(f32[1,4,2,128]{3,1,2,0:T(4,128)} %copy.70) | copy-start | bytes 12292
  194.3 13.6 %copy-start.70 = (f32[1024]{0:T(1024)S(1)}, f32[1024]{0:T(1024)}, u32[]{:S(2)}) copy-start(f32[1024]{0:T(1024)} %rsqrt.82) | copy-start | bytes 12292
  194.3 13.6 %copy-start.74 = (f32[512]{0:T(512)S(1)}, f32[512]{0:T(512)}, u32[]{:S(2)}) copy-start(f32[512]{0:T(512)} %copy-done.73) | copy-start | bytes 6148
  211.1 7.1 %slice-start.4 = ((s8[4718592]{0:T(1024)(128)(4,1)}), s8[4194304]{0:T(1024)(128)(4,1)S(1)}, s32[]{:S(2)}) async-start(s8[4718592]{0:T(1024)(128)(4,1)} %bitcast.227), calls=%async_computation.4 | async-start | bytes 8388608
  216.6 8.6 %copy-start.37 = (f32[320,768]{1,0:T(8,128)}, f32[320,768]{1,0:T(8,128)S(1)}, u32[]{:S(2)}) copy-start(f32[320,768]{1,0:T(8,128)S(1)} %get-tuple-element.213) | copy-start | bytes 2949124
  225.5 8.8 %copy-start.29 = (f32[320,768]{1,0:T(8,128)S(1)}, f32[320,768]{1,0:T(8,128)}, u32[]{:S(2)}) copy-start(f32[320,768]{1,0:T(8,128)} %copy-done.28) | copy-start | bytes 2949124
  225.5 8.8 %copy-start.56 = (f32[320]{0:T(512)S(1)}, f32[320]{0:T(512)}, u32[]{:S(2)}) copy-start(f32[320]{0:T(512)} %copy-done.55) | copy-start | bytes 3844
  225.5 8.8 %copy-start.64 = (f32[768]{0:T(1024)S(1)}, f32[768]{0:T(1024)}, u32[]{:S(2)}) copy-start(f32[768]{0:T(1024)} %copy-done.63) | copy-start | bytes 9220
  225.5 8.8 %copy-start.78 = (f32[320]{0:T(512)S(1)}, f32[320]{0:T(512)}, u32[]{:S(2)}) copy-start(f32[320]{0:T(512)} %copy-done.77) | copy-start | bytes 3844
  458.5 38.0 %copy-start.67 = (f32[16,256]{1,0:T(8,128)S(1)}, f32[16,256]{1,0:T(8,128)}, u32[]{:S(2)}) copy-start(f32[16,256]{1,0:T(8,128)} %get-tuple-element.179) | copy-start | bytes 49156
  458.5 38.1 %copy-start.43 = (f32[1248]{0:T(1024)S(1)}, f32[1248]{0:T(1024)}, u32[]{:S(2)}) copy-start(f32[1248]{0:T(1024)} %param.59) | copy-start | bytes 14980
  458.5 38.1 %copy-start.75 = (f32[1248]{0:T(1024)S(1)}, f32[1248]{0:T(1024)}, u32[]{:S(2)}) copy-start(f32[1248]{0:T(1024)} %param.60) | copy-start | bytes 14980
  458.5 38.1 %copy-start.76 = (f32[1248]{0:T(1024)S(1)}, f32[1248]{0:T(1024)}, u32[]{:S(2)}) copy-start(f32[1248]{0:T(1024)} %param.61) | copy-start | bytes 14980
  (85 other events, 250.1 us)

commit v4 on v3

--- a/solution.py
+++ b/solution.py
@@ -395,10 +395,44 @@
     total[...] = total[...] + landing[devices]
 
 
+def cut_patches(lines, spots, take, freq, fold, table, picked_out, where_out, target_out):
+    part = 512
+    lane = lax.broadcasted_iota(jnp.int32, (NPATCH, part), 1)
+    inside = lax.rem(lax.div(lane, PS), GF) == freq[...]
+    for clip in range(lines.shape[0]):
+        patches = jnp.zeros((NPATCH, PATCH), jnp.float32)
+        for start in range(0, PS * GF * PS, part):
+            spread = jnp.dot(
+                take[...], lines[clip, :, start : start + part], preferred_element_type=jnp.float32
+            )
+            spread = jnp.where(inside, spread, 0.0).astype(jnp.bfloat16)
+            patches = patches + jnp.dot(
+                spread, fold[start : start + part, :], preferred_element_type=jnp.float32
+            )
+        slot = lax.broadcasted_iota(jnp.int32, (SLOTS, NPATCH), 1)
+        chosen = jnp.where(slot == spots[clip], 1.0, 0.0).astype(jnp.bfloat16)
+        picked = jnp.dot(chosen, patches.astype(jnp.bfloat16), preferred_element_type=jnp.float32)
+        picked_out[clip] = picked.astype(jnp.bfloat16)
+        where_out[clip] = jnp.dot(chosen, table[:, :D], preferred_element_type=jnp.float32) + jnp.dot(
+            chosen, table[:, D:], preferred_element_type=jnp.float32
+        )
+        centred = patches - jnp.mean(patches, axis=-1, keepdims=True)
+        spread = jnp.mean(centred * centred, axis=-1, keepdims=True)
+        target_out[clip] = centred * lax.rsqrt(spread + 1e-06)
+
+
 def gather_kernel(levels, pieces, count, *refs):
-    shards, tally = refs[:count], refs[count]
-    wholes, tally_out = refs[count + 1 : 2 * count + 1], refs[2 * count + 1]
-    short, rest = refs[2 * count + 2 : 3 * count + 2], refs[3 * count + 2 :]
+    sources, tally, rest = refs[:count] + refs[count + 1 : count + 7], refs[count], refs[count + 7 :]
+    outs, tally_out, made, rest = rest[:count], rest[count], rest[count + 1 : count + 4], rest[count + 4 :]
+    wholes, save_sem, rest = rest[:count], rest[count], rest[count + 1 :]
+    short, held, load_sem, rest = rest[:count], rest[count : 2 * count + 6], rest[2 * count + 6], rest[2 * count + 7 :]
+    shards, scene = held[:count], held[count:]
+
+    def load(number):
+        return pltpu.make_async_copy(sources[number], held[number], load_sem.at[number])
+
+    for number in range(count + 6):
+        load(number).start()
     here_sem, send_sem, recv_sem, cross_send, cross_recv, tally_land, tally_send, tally_recv = rest
     me, own = own_bits(levels)
     core = lax.axis_index("mp")
@@ -446,6 +480,7 @@
         number = pieces[piece][0]
         if number not in ready:
             ready.add(number)
+            load(number).wait()
             short[number][...] = shards[number][...].astype(jnp.bfloat16)
             keep(number).start()
         hop(piece, 0, False).start()
@@ -481,36 +516,63 @@
                 hop(piece, stage + 1, False).start()
             cross(piece, stage, core).start()
         swap_end(stage)
+        if stage == levels - 2:
+            for number in range(6):
+                load(count + number).wait()
+            cut_patches(*scene, *made)
+    def save(number):
+        return pltpu.make_async_copy(wholes[number], outs[number], save_sem.at[number])
+
+    last = {}
+    for place_in, piece in enumerate(GATHER_STEPS[levels - 1]):
+        last[pieces[piece][0]] = place_in
+    for number in sorted(last, key=lambda found: last[found]):
+        for piece in range(len(pieces)):
+            if pieces[piece][0] == number:
+                for stage in range(levels):
+                    cross(piece, stage, 1 - core).wait_recv()
+        save(number).start()
     for piece in range(len(pieces)):
         for stage in range(levels):
             hop(piece, stage, False).wait_send()
             cross(piece, stage, core).wait_send()
-            cross(piece, stage, 1 - core).wait_recv()
-
-
-def gather_rows(shards, tally, devices):
+    for number in range(count):
+        save(number).wait()
+
+
+def gather_rows(shards, tally, scene, devices):
     levels, count = bit_count(devices), len(shards)
     lead = (2,) * levels
+    clips = scene[0].shape[0]
     pieces = cut_pieces(GATHER_PARTS, [(shard.shape[0], shard.shape[1] // 2) for shard in shards])
     dma = pltpu.SemaphoreType.DMA
-    vmem = pl.BlockSpec(memory_space=pltpu.VMEM)
+    vmem, far = pl.BlockSpec(memory_space=pltpu.VMEM), pl.BlockSpec(memory_space=pltpu.HBM)
     found = pl.pallas_call(
         functools.partial(gather_kernel, levels, pieces, count),
         out_shape=[jax.ShapeDtypeStruct(lead + shard.shape, jnp.bfloat16) for shard in shards]
-        + [jax.ShapeDtypeStruct((8, 128), jnp.float32)],
-        in_specs=[vmem] * (count + 1),
-        out_specs=[pl.BlockSpec(memory_space=pl.ANY)] * count + [vmem],
-        scratch_shapes=[pltpu.VMEM(shard.shape, jnp.bfloat16) for shard in shards]
+        + [
+            jax.ShapeDtypeStruct((8, 128), jnp.float32),
+            jax.ShapeDtypeStruct((clips, SLOTS, PATCH), jnp.bfloat16),
+            jax.ShapeDtypeStruct((clips, SLOTS, D), jnp.float32),
+            jax.ShapeDtypeStruct((clips, NPATCH, PATCH), jnp.float32),
+        ],
+        in_specs=[far] * count + [vmem] + [far] * 6,
+        out_specs=[pl.BlockSpec(memory_space=pl.ANY)] * count + [vmem] * 4,
+        scratch_shapes=[pltpu.VMEM(lead + shard.shape, jnp.bfloat16) for shard in shards]
+        + [dma((count,))]
+        + [pltpu.VMEM(shard.shape, jnp.bfloat16) for shard in shards]
+        + [pltpu.VMEM(piece.shape, piece.dtype) for piece in (*shards, *scene)]
+        + [dma((count + 6,))]
         + [dma((count,))]
         + [dma((len(pieces), levels))] * 4
         + [pltpu.VMEM((levels + 1, 8, 128), jnp.float32)]
         + [dma((levels + 1,))] * 2,
         compiler_params=pltpu.CompilerParams(
-            collective_id=1, has_side_effects=True, vmem_limit_bytes=32 * 2**20
+            collective_id=1, has_side_effects=True, vmem_limit_bytes=60 * 2**20
         ),
         name="gather_rows",
-    )(*shards, tally)
-    return found[:count], found[count]
+    )(*shards, tally, *scene)
+    return found[:count], found[count], found[count + 1 :]
 
 
 def reduce_kernel(levels, pieces, count, owners, devices, *refs):
@@ -1141,26 +1203,25 @@
     return moved.astype(np.float32)
 
 
-def window_patches(spec):
+def window_scene(spec, keep):
     position = np.arange(NPATCH)
     row = np.empty(NPATCH, np.int32)
     row[window_place(position)] = position
-    rows = row[:, None]
-    take = (rows // GF == np.arange(GT)[None, :]).astype(np.float32)
-    column = lax.broadcasted_iota(jnp.int32, (NPATCH, PS * GF * PS), 1)
-    inside = (column // PS) % GF == jnp.asarray(rows % GF)
+    take = (row[:, None] // GF == np.arange(GT)[None, :]).astype(np.float32)
     source = np.arange(PS * GF * PS)[:, None]
     target = np.arange(PATCH)[None, :]
     fold = np.logical_and(source // (GF * PS) == target // PS, source % PS == target % PS)
-    lines = spec.reshape(spec.shape[0], GT, PS * GF * PS)
-    spread = jnp.einsum(
-        "rt,ctl->crl", jnp.asarray(take, jnp.bfloat16), lines, preferred_element_type=jnp.float32
-    )
-    spread = jnp.where(inside, spread, 0.0).astype(jnp.bfloat16)
-    found = jnp.einsum(
-        "crl,lq->crq", spread, jnp.asarray(fold, jnp.bfloat16), preferred_element_type=jnp.float32
-    )
-    return found.astype(jnp.bfloat16)
+    table = window_sinusoid(D)
+    high = table.astype(jnp.bfloat16)
+    low = (table - high.astype(np.float32)).astype(jnp.bfloat16)
+    return (
+        spec.reshape(spec.shape[0], GT, PS * GF * PS),
+        window_place(jnp.pad(keep, ((0, 0), (0, SLOTS - VIS))))[:, :, None],
+        jnp.asarray(take, jnp.bfloat16),
+        jnp.asarray(row[:, None] % GF),
+        jnp.asarray(fold, jnp.bfloat16),
+        jnp.asarray(np.concatenate([high, low], axis=1)),
+    )
 
 
 @jax.custom_vjp
@@ -1186,12 +1247,6 @@
 times.defvjp(times_keep, times_back)
 
 
-def soft_rows(scores, allowed, scaling):
-    scores = jnp.where(allowed, scores * scaling, -1e30)
-    exponent = jnp.exp(scores - jnp.max(scores, axis=-1, keepdims=True))
-    return exponent / jnp.sum(exponent, axis=-1, keepdims=True)
-
-
 def dot_rows(left, right):
     return lax.dot_general(left, right, (((1,), (1,)), ((), ())), preferred_element_type=jnp.float32)
 
@@ -1205,29 +1260,32 @@
     return jnp.where(lane // size == head, value, jnp.zeros_like(value))
 
 
+def soft_keys(queries, keys_here, allow, size):
+    rows = queries.shape[0]
+    scores = dot_rows(keys_here, queries).reshape(128 // size, rows, rows)
+    scores = jnp.where(allow, scores * size ** (-0.5), -1e30)
+    exponent = jnp.exp(scores - jnp.max(scores, axis=1, keepdims=True))
+    return exponent / jnp.sum(exponent, axis=1, keepdims=True)
+
+
+def flat_heads(value):
+    return value.astype(jnp.bfloat16).reshape(-1, value.shape[2])
+
+
 def attention_kernel(size, joined, allowed, out):
     width = out.shape[1]
-    per = 128 // size
-    allow = jnp.broadcast_to(allowed[...], (out.shape[0], allowed.shape[1])) > 0.0
+    allow = allowed[...][None] > 0.0
     for lane in range(0, width, 128):
         queries = joined[:, lane : lane + 128]
-        key_rows = joined[:, width + lane : width + lane + 128]
-        values = joined[:, 2 * width + lane : 2 * width + lane + 128]
-        total = jnp.zeros(queries.shape, jnp.float32)
-        for head in range(per):
-            scores = dot_rows(queries, head_lanes(key_rows, head, size))
-            soft = soft_rows(scores, allow, size ** (-0.5)).astype(jnp.bfloat16)
-            total = total + jnp.dot(
-                soft, head_lanes(values, head, size), preferred_element_type=jnp.float32
-            )
-        out[:, lane : lane + 128] = total.astype(jnp.bfloat16)
+        keys_here = stack_heads(joined[:, width + lane : width + lane + 128], size)
+        values_here = stack_heads(joined[:, 2 * width + lane : 2 * width + lane + 128], size)
+        soft = flat_heads(soft_keys(queries, keys_here, allow, size))
+        out[:, lane : lane + 128] = dot_columns(soft, values_here).astype(jnp.bfloat16)
 
 
 def attention_back_kernel(size, joined, allowed, grad, out, query_sum, value_sum):
-    width = grad.shape[1]
-    per = 128 // size
-    scaling = size ** (-0.5)
-    allow = jnp.broadcast_to(allowed[...], (grad.shape[0], allowed.shape[1])) > 0.0
+    width, rows = grad.shape[1], grad.shape[0]
+    allow = allowed[...][None] > 0.0
 
     @pl.when(pl.program_id(0) == 0)
     def clear():
@@ -1236,21 +1294,17 @@
 
     for lane in range(0, width, 128):
         queries = joined[:, lane : lane + 128]
-        key_rows = joined[:, width + lane : width + lane + 128]
-        values = joined[:, 2 * width + lane : 2 * width + lane + 128]
+        keys_here = stack_heads(joined[:, width + lane : width + lane + 128], size)
+        values_here = stack_heads(joined[:, 2 * width + lane : 2 * width + lane + 128], size)
         pull = grad[:, lane : lane + 128]
-        query_grad = jnp.zeros(queries.shape, jnp.float32)
-        key_grad = jnp.zeros(queries.shape, jnp.float32)
-        value_grad = jnp.zeros(queries.shape, jnp.float32)
-        for head in range(per):
-            keys_here = head_lanes(key_rows, head, size)
-            soft = soft_rows(dot_rows(queries, keys_here), allow, scaling)
-            soft_grad = dot_rows(pull, head_lanes(values, head, size))
-            score_grad = soft * (soft_grad - jnp.sum(soft * soft_grad, axis=-1, keepdims=True))
-            score_grad = (score_grad * scaling).astype(jnp.bfloat16)
-            query_grad = query_grad + jnp.dot(score_grad, keys_here, preferred_element_type=jnp.float32)
-            key_grad = key_grad + dot_columns(score_grad, head_lanes(queries, head, size))
-            value_grad = value_grad + dot_columns(soft.astype(jnp.bfloat16), head_lanes(pull, head, size))
+        soft = soft_keys(queries, keys_here, allow, size)
+        soft_grad = dot_rows(values_here, pull).reshape(128 // size, rows, rows)
+        score_grad = soft * (soft_grad - jnp.sum(soft * soft_grad, axis=1, keepdims=True))
+        score_grad = flat_heads(score_grad * size ** (-0.5))
+        soft = flat_heads(soft)
+        query_grad = dot_columns(score_grad, keys_here)
+        key_grad = unstack_heads(jnp.dot(score_grad, queries, preferred_element_type=jnp.float32), size)
+        value_grad = unstack_heads(jnp.dot(soft, pull, preferred_element_type=jnp.float32), size)
         out[:, lane : lane + 128] = query_grad.astype(jnp.bfloat16)
         out[:, width + lane : width + lane + 128] = key_grad.astype(jnp.bfloat16)
         out[:, 2 * width + lane : 2 * width + lane + 128] = value_grad.astype(jnp.bfloat16)
@@ -1286,9 +1340,9 @@
 
 
 def unstack_heads(value, size):
-    rows = value.shape[1]
-    per = value.shape[0] // rows
-    lane = lax.broadcasted_iota(jnp.int32, (rows, rows), 1) // size
+    per = value.shape[1] // size
+    rows = value.shape[0] // per
+    lane = lax.broadcasted_iota(jnp.int32, (rows, value.shape[1]), 1) // size
     found = value[:rows]
     for head in range(1, per):
         found = jnp.where(lane == head, value[head * rows : (head + 1) * rows], found)
@@ -1418,6 +1472,70 @@
 decoder_attention = attention_block(window_kernel, window_back_kernel, 8 * WIN * WIN, DHEAD)
 
 
+def gelu_keep(value):
+    portion = 0.5 + 0.5 * lax.erf(value * math.sqrt(0.5))
+    slope = portion + value * jnp.exp(-0.5 * value * value) * (1.0 / math.sqrt(2.0 * math.pi))
+    return value * portion, slope
+
+
+def hidden_back_kernel(normed, inner, slope, grad, up, down, normed_grad, up_grad, down_grad, bias_grad):
+    @pl.when(pl.program_id(0) == 0)
+    def clear():
+        normed_grad[...] = jnp.zeros_like(normed_grad)
+
+    inner_grad = dot_rows(grad[...], down[...]) * slope[...]
+    bias_grad[0:1, :] = jnp.sum(inner_grad, axis=0, keepdims=True)
+    short = inner_grad.astype(jnp.bfloat16)
+    down_grad[...] = dot_columns(inner[...], grad[...]).astype(jnp.bfloat16)
+    up_grad[...] = dot_columns(normed[...], short).astype(jnp.bfloat16)
+    normed_grad[...] += dot_rows(short, up[...])
+
+
+def hidden_backward(normed, inner, slope, grad, up, down):
+    (tokens, width), units = normed.shape, inner.shape[1]
+    tile = 512
+    whole = pl.BlockSpec((tokens, width), lambda step: (0, 0))
+    columns = pl.BlockSpec((tokens, tile), lambda step: (0, step))
+    up_tile = pl.BlockSpec((width, tile), lambda step: (0, step))
+    down_tile = pl.BlockSpec((tile, width), lambda step: (step, 0))
+    return pl.pallas_call(
+        hidden_back_kernel,
+        grid=(units // tile,),
+        out_shape=[
+            jax.ShapeDtypeStruct((tokens, width), jnp.float32),
+            jax.ShapeDtypeStruct((width, units), jnp.bfloat16),
+            jax.ShapeDtypeStruct((units, width), jnp.bfloat16),
+            jax.ShapeDtypeStruct((8, units), jnp.float32),
+        ],
+        in_specs=[whole, columns, columns, whole, up_tile, down_tile],
+        out_specs=[whole, up_tile, down_tile, pl.BlockSpec((8, tile), lambda step: (0, step))],
+        compiler_params=pltpu.CompilerParams(vmem_limit_bytes=40 * 2**20),
+        name="hidden_backward",
+    )(normed, inner, slope, grad, up, down)
+
+
+@jax.custom_vjp
+def hidden_layer(normed, up, bias, down):
+    return hidden_keep(normed, up, bias, down)[0]
+
+
+def hidden_keep(normed, up, bias, down):
+    short = normed.astype(jnp.bfloat16)
+    value, slope = gelu_keep(jnp.dot(short, up, preferred_element_type=jnp.float32) + bias)
+    inner = value.astype(jnp.bfloat16)
+    return jnp.dot(inner, down, preferred_element_type=jnp.float32), (short, inner, slope, up, down)
+
+
+def hidden_back(kept, grad):
+    short, inner, slope, up, down = kept
+    found = hidden_backward(short, inner, slope, grad.astype(jnp.bfloat16), up, down)
+    normed_grad, up_grad, down_grad, bias_grad = found
+    return normed_grad, up_grad, bias_grad[0], down_grad
+
+
+hidden_layer.defvjp(hidden_keep, hidden_back)
+
+
 def window_allowed():
     position = np.arange(NPATCH)
     window, inner = position // (WIN * WIN), position % (WIN * WIN)
@@ -1430,41 +1548,20 @@
     return same.transpose(0, 2, 1, 3).reshape(-1, WIN * WIN, 8 * WIN * WIN).astype(np.float32)
 
 
-@jax.custom_vjp
-def gelu(value):
-    return value * (0.5 + 0.5 * lax.erf(value * math.sqrt(0.5)))
-
-
-def gelu_keep(value):
-    portion = 0.5 + 0.5 * lax.erf(value * math.sqrt(0.5))
-    slope = portion + value * jnp.exp(-0.5 * value * value) * (1.0 / math.sqrt(2.0 * math.pi))
-    return value * portion, slope
-
-
-def gelu_back(slope, grad):
-    return (grad * slope,)
-
-
-gelu.defvjp(gelu_keep, gelu_back)
-
-
-def local_loss(weights, patches, keep, counts):
-    clips = patches.shape[0]
+def local_loss(weights, picked, where, target, keep, counts):
+    clips = picked.shape[0]
     pieces = unpack(weights[10])
-    keep = jnp.pad(keep, ((0, 0), (0, SLOTS - VIS)))
-    spot = window_place(keep)
-    chosen = (spot[:, :, None] == jnp.arange(NPATCH)[None, None, :]).astype(jnp.float32)
-    shown = chosen * (jnp.arange(SLOTS)[None, :] < counts[:, None])[:, :, None]
-    picked = jnp.einsum("cjp,cpv->cjv", chosen.astype(jnp.bfloat16), patches, preferred_element_type=jnp.float32)
-    where = jnp.einsum("cjp,pd->cjd", chosen, window_sinusoid(D), precision=HIGH)
+    spot = window_place(jnp.pad(keep, ((0, 0), (0, SLOTS - VIS))))
+    shown = (spot[:, :, None] == jnp.arange(NPATCH)[None, None, :]).astype(jnp.float32)
+    shown = shown * (jnp.arange(SLOTS)[None, :] < counts[:, None])[:, :, None]
     hidden = times(picked.reshape(-1, PATCH), weights[8][:, :D]) + pieces[11] + where.reshape(-1, D)
     normed = layer_norm(hidden, pieces[0], pieces[1])
-    visible = (jnp.arange(SLOTS)[None, :] < counts[:, None]).astype(jnp.float32)[:, None, :]
+    visible = (jnp.arange(SLOTS)[None, :] < counts[:, None]).astype(jnp.float32)
+    visible = jnp.broadcast_to(visible[:, :, None], (clips, SLOTS, SLOTS))
     attended = encoder_attention(normed, weights[0], pieces[2], pieces[3], visible)
     hidden = hidden + times(attended, weights[1]) + pieces[4]
     normed = layer_norm(hidden, pieces[5], pieces[6])
-    inner = gelu(times(normed, weights[2]) + pieces[7])
-    hidden = hidden + times(inner, weights[3]) + pieces[8]
+    hidden = hidden + hidden_layer(normed, weights[2], pieces[7], weights[3]) + pieces[8]
     latent = layer_norm(hidden, pieces[9], pieces[10])
 
     pieces = pieces[12:]
@@ -1477,14 +1574,10 @@
     attended = decoder_attention(normed, weights[4], pieces[4], pieces[5], jnp.asarray(window_allowed()))
     hidden = hidden + times(attended, weights[5]) + pieces[6]
     normed = layer_norm(hidden, pieces[7], pieces[8])
-    inner = gelu(times(normed, weights[6]) + pieces[9])
-    hidden = hidden + times(inner, weights[7]) + pieces[10]
+    hidden = hidden + hidden_layer(normed, weights[6], pieces[9], weights[7]) + pieces[10]
     normed = layer_norm(hidden, pieces[11], pieces[12])
     predicted = times(normed, weights[8][:, D:].T) + pieces[13]
-    patches = patches.astype(jnp.float32).reshape(-1, PATCH)
-    centred = patches - jnp.mean(patches, axis=-1, keepdims=True)
-    target = centred * lax.rsqrt(jnp.mean(centred * centred, axis=-1, keepdims=True) + 1e-06)
-    deviation = predicted - target
+    deviation = predicted - target.reshape(-1, PATCH)
     patch_error = jnp.mean(deviation * deviation, axis=-1)
     return jnp.sum((1.0 - cells.reshape(-1)) * patch_error)
 
@@ -1504,14 +1597,14 @@
     column = lax.broadcasted_iota(jnp.int32, (8, 128), 1)
     first = jnp.logical_and(row == 0, column == 0)
     count_part = jnp.sum(NPATCH - counts).astype(jnp.float32)
-    gathered, tally = gather_rows(own, jnp.where(first, count_part, 0.0), devices)
+    scene = window_scene(spectrogram, keep)
+    gathered, tally, made = gather_rows(own, jnp.where(first, count_part, 0.0), scene, devices)
     mask_count = tally[0, 0]
     weights = [piece.reshape(-1, piece.shape[-1]) for piece in gathered[:10]]
     weights[4] = weights[4].astype(jnp.float32)
     vectors = gathered[10].reshape(devices, spare)[:, :vector_rows].reshape(-1).astype(jnp.float32)
-    patches = window_patches(spectrogram)
     loss_part, pull = jax.vjp(
-        lambda *params: local_loss(params, patches, keep, counts), *weights, vectors
+        lambda *params: local_loss(params, *made, keep, counts), *weights, vectors
     )
     grads = list(pull(1.0 / mask_count))
     grads[10] = jnp.pad(grads[10].reshape(devices, vector_rows), ((0, 0), (0, spare - vector_rows)))

time: 513 us -> 500 us (0.975)
  matrix products: 93.1 us -> 52.7 us
  Pallas kernels: 360 us -> 389 us
    dot_general x11 -> x4, matrix products: 43.5 us -> 15.4 us  [the longest x2 11.2 us: hidden_keep(): jnp.dot(short, up, preferred_element_type=jnp.float32) + bias]
    pallas_call x0 -> x2, Pallas kernels: none -> 24.3 us  [the longest x1 12.4 us: local_loss(): hidden_layer(normed, weights[2], pieces[7], weights[3])]
    dot_general x9 -> x5, matrix products: 19 us -> 4.46 us  [times_keep(): jnp.dot(short, matrix.astype(jnp.bfloat16), preferred_element_type=jnp.fl...]
    pallas_call x1, Pallas kernels: 92.4 us -> 100 us  [gather_rows(): pl.pallas_call(functools.partial(gather_kernel, levels, pieces, count), o...]
    unnamed x226 -> x104, local copies, waits for them, and re-layouts: 15.5 us -> 12.2 us
where the time goes in v4:
time: 500 us; the launch traced here: 491 us
  Pallas kernels  389 us (78%)
  matrix products  52.7 us (11%)
  other arithmetic  22.4 us (4%)
  local copies, waits for them, and re-layouts  21.5 us (4%)
  between operations  5.2 us (1%)
    pallas_call x1, Pallas kernels, reduce_rows(): pl.pallas_call(functools.partial(reduce_kernel, levels, pieces, count, ow...  148 us
    pallas_call x1, Pallas kernels, gather_rows(): pl.pallas_call(functools.partial(gather_kernel, levels, pieces, count), o...  100 us
    pallas_call x1, Pallas kernels, orthogonalize(): pl.pallas_call(functools.partial(muon_kernel, owners, shapes), out_shape=...  44.2 us
    pallas_call x1, Pallas kernels, return_rows(): pl.pallas_call(functools.partial(return_kernel, owners, count, devices),...  38.1 us
    pallas_call x1, Pallas kernels, local_loss(): decoder_attention(normed, weights[4], pieces[4], pieces[5], jnp.asarray(w...  13.5 us
    pallas_call x1, Pallas kernels, local_loss(): hidden_layer(normed, weights[2], pieces[7], weights[3])  12.4 us
    unnamed x104, local copies, waits for them, and re-layouts  12.2 us
    pallas_call x1, Pallas kernels, local_loss(): hidden_layer(normed, weights[6], pieces[9], weights[7])  11.8 us

profile of v4, /device:TPU:15, one launch (start us, length us, event | category | flops | bytes accessed | tf_op | source)
XLA Modules:
  0.0 491.1 jit_solution(1537409807038437174)
XLA Ops:
  7.9 2.1 reshape.520.refs_12_
  10.0 100.0 %gather_rows.1 = (bf16[2,2,2,2,48,2304]{5,4,3,2,1,0:T(8,128)(2,1)}, bf16[2,2,2,2,48,768]{5,4,3,2,1,0:T(8,128)(2,1)}, bf16[2,2,2,2,48,3072]{5,4,3,2,1,0:T(8,128)(...) custom-call(f32[48,2304]{1,0:T(8,128)} %refs_8_.3, ...), custom_call_target="tpu_custom_call" | custom-call | tf_op jit(solution)/shard_map/gather_rows/pallas_call | solution.py:550
  113.1 1.9 fusion.70
  116.9 3.4 jvp_attention_forward_.2
  121.5 3.7 fusion.8
  125.3 1.8 fusion.72
  128.7 2.4 fusion.73
  135.1 7.2 %jvp_attention_forward_.3 = bf16[1024,512]{1,0:T(8,128)(2,1)S(1)} custom-call(bf16[1024,1536]{1,0:T(8,128)(2,1)S(1)} %add_convert_fusion.joined, f32[4,16,128]{2,1,0:T(8,128)S(1)} %copy-done.9), custom_call_target="tpu_custom_call" | custom-call | tf_op jit(solution)/shard_map/jvp(attention_forward)/pallas_call | solution.py:1410
  145.5 7.5 %fusion.3 = (f32[1024,2048]{1,0:T(8,128)}, bf16[1024,2048]{1,0:T(8,128)(2,1)S(1)}) fusion(f32[2048]{0:T(1024)S(1)} %slice.179, bf16[1024,512]{1,0:T(8,128)(2,1)S(1)} %add_convert_fusion.3.normed, bf16[512,2048]{1,0:T(8,128)(2,1)S(1)} %bitcast.124), kind=kOutput, calls=%fused_computation.4 | convolution fusion | flops 2170552320 | bytes 15736832 | tf_op jit(solution)/shard_map/jvp()/dot_general | solution.py:1524
  153.0 2.4 fusion.75
  165.1 11.8 %transpose_jvp_hidden_backward__.2 = (f32[1024,512]{1,0:T(8,128)S(1)}, bf16[512,2048]{1,0:T(8,128)(2,1)S(1)}, bf16[2048,512]{1,0:T(8,128)(2,1)S(1)}, f32[8,2048]{1,0:T(8,128)S(1)}) custom-call(bf16[1024,512]{1,0:T(8,128)(2,1)S(1)} %add_convert_fusion.3.normed, bf16[1024,2048]{1,0:T(8,128)(2,1)} %copy-done.27, f32[1024,2048]{1,0:T(8,128)} %get-tuple-element.242.slope, ...), custom_call_target="tpu_custom_call" | custom-call | tf_op jit(solution)/shard_map/transpose(jvp(hidden_backward))/pallas_call | solution.py:1577
  177.0 3.9 multiply_reduce_fusion.2
  185.3 13.5 %transpose_jvp_attention_backward__.2 = (bf16[1024,1536]{1,0:T(8,128)(2,1)S(1)}, f32[8,512]{1,0:T(8,128)S(1)}, f32[8,512]{1,0:T(8,128)S(1)}) custom-call(bf16[1024,1536]{1,0:T(8,128)(2,1)S(1)} %add_convert_fusion.joined, f32[4,16,128]{2,1,0:T(8,128)S(1)} %copy-done.9, bf16[1024,512]{1,0:T(8,128)(2,1)S(1)} %convolution_convert_fusion.2.grad), custom_call_target="tpu_custom_call" | custom-call | tf_op jit(solution)/shard_map/transpose(jvp(attention_backward))/pallas_call | solution.py:1574
  198.8 5.7 %multiply_reduce_fusion.1 = (f32[512]{0:T(512)S(1)}, f32[1024]{0:T(1024)S(1)}, f32[512]{0:T(512)S(1)}, bf16[1024,512]{1,0:T(8,128)(2,1)}, f32[1024,512]{1,0:T(8,128)S(1)}) fusion(f32[2,512,512]{2,1,0:T(8,128)S(1)} %copy-done.15, f32[1024]{0:T(1024)S(1)} %bitcast.190, f32[1024]{0:T(1024)S(1)} %rsqrt.69, f32[512]{0:T(512)S(1)} %get-tuple-element.262, ...), kind=kOutput, calls=%fused_computation.28 | convolution fusion | flops 1616377856 | bytes 9981952 | tf_op jit(solution)/shard_map/transpose(jvp())/dot_general | solution.py:1574
  210.3 12.4 %transpose_jvp_hidden_backward__.3 = (f32[320,768]{1,0:T(8,128)S(1)}, bf16[768,3072]{1,0:T(8,128)(2,1)S(1)}, bf16[3072,768]{1,0:T(8,128)(2,1)}, f32[8,3072]{1,0:T(8,128)S(1)}) custom-call(bf16[320,768]{1,0:T(8,128)(2,1)S(1)} %add_convert_fusion.7.normed, bf16[320,3072]{1,0:T(8,128)(2,1)S(1)} %copy-done.8, f32[320,3072]{1,0:T(8,128)S(1)} %get-tuple-element.244.slope, ...), custom_call_target="tpu_custom_call" | custom-call | tf_op jit(solution)/shard_map/transpose(jvp(hidden_backward))/pallas_call | solution.py:1564
  226.8 6.3 %transpose_jvp_attention_backward__.3 = (bf16[320,2304]{1,0:T(8,128)(2,1)S(1)}, f32[8,768]{1,0:T(8,128)S(1)}, f32[8,768]{1,0:T(8,128)S(1)}) custom-call(bf16[320,2304]{1,0:T(8,128)(2,1)S(1)} %fusion.4.joined, f32[2,160,160]{2,1,0:T(8,128)S(1)} %broadcast_in_dim.52.allowed, bf16[320,768]{1,0:T(8,128)(2,1)S(1)} %convolution_convert_fusion.5.grad), custom_call_target="tpu_custom_call" | custom-call | tf_op jit(solution)/shard_map/transpose(jvp(attention_backward))/pallas_call | solution.py:1561
  236.2 1.8 convolution_convert_fusion.1
  239.9 2.3 copy.64
  242.2 4.9 fusion.9.refs_4_
  247.1 4.1 convolution_convert_fusion
  251.2 148.5 %reduce_rows.1 = (f32[48,2304]{1,0:T(8,128)}, f32[48,768]{1,0:T(8,128)}, f32[48,3072]{1,0:T(8,128)}, f32[192,768]{1,0:T(8,128)}, f32[32,1536]{1,0:T(8,128)}, /*i...) custom-call(bf16[2,2,2,2,48,2304]{5,4,3,2,1,0:T(8,128)(2,1)} %bitcas, ...), custom_call_target="tpu_custom_call" | custom-call | tf_op jit(solution)/shard_map/reduce_rows/pallas_call | solution.py:817
  402.9 44.2 %orthogonalize.1 = (bf16[768,2304]{1,0:T(8,128)(2,1)}, bf16[768,768]{1,0:T(8,128)(2,1)}, bf16[768,3072]{1,0:T(8,128)(2,1)}, bf16[3072,768]{1,0:T(8,128)(2,1)}, b...) custom-call(bf16[768,2304]{1,0:T(8,128)(2,1)} %bitcast.148, ...), custom_call_target="tpu_custom_call" | custom-call | tf_op jit(solution)/shard_map/orthogonalize/pallas_call | solution.py:1157
  447.1 38.1 %return_rows.1 = (bf16[48,2304]{1,0:T(8,128)(2,1)}, bf16[48,768]{1,0:T(8,128)(2,1)}, bf16[48,3072]{1,0:T(8,128)(2,1)}, bf16[192,768]{1,0:T(8,128)(2,1)}, bf16[32...) custom-call(bf16[16,48,2304]{2,1,0:T(8,128)(2,1)} %bitcast.147, ...), custom_call_target="tpu_custom_call" | custom-call | tf_op jit(solution)/shard_map/return_rows/pallas_call | solution.py:923
  486.0 3.8 finish.1
  (211 shorter events, 52.0 us)
Async XLA Ops:
  115.0 5.3 %copy-start.22 = (f32[320,768]{1,0:T(8,128)}, f32[320,768]{1,0:T(8,128)S(1)}, u32[]{:S(2)}) copy-start(f32[320,768]{1,0:T(8,128)S(1)} %get-tuple-element.284) | copy-start | bytes 2949124
  115.0 6.5 %slice-start = ((s8[4718592]{0:T(1024)(128)(4,1)}), s8[4194304]{0:T(1024)(128)(4,1)S(1)}, s32[]{:S(2)}) async-start(s8[4718592]{0:T(1024)(128)(4,1)} %bitcast.135), calls=%async_computation | async-start | bytes 8388608
  115.5 6.0 %slice-start.1 = ((s8[4718592]{0:T(1024)(128)(4,1)}), s8[524288]{0:T(1024)(128)(4,1)S(1)}, s32[]{:S(2)}) async-start(s8[4718592]{0:T(1024)(128)(4,1)} %bitcast.135), calls=%async_computation.1 | async-start | bytes 1048576
  121.0 4.2 copy-start.18
  121.3 4.0 slice-start.2
  127.1 4.0 copy-start.28
  131.1 11.2 %copy-start.14 = (f32[2,512,512]{2,1,0:T(8,128)}, f32[2,512,512]{2,1,0:T(8,128)S(1)}, u32[]{:S(2)}) copy-start(f32[2,512,512]{2,1,0:T(8,128)S(1)} %get-tuple-element.290) | copy-start | bytes 6291460
  135.1 7.3 %copy-start.30 = (bf16[2,2,2,2,32,512]{5,4,3,2,1,0:T(8,128)(2,1)S(1)}, bf16[2,2,2,2,32,512]{5,4,3,2,1,0:T(8,128)(2,1)}, u32[]{:S(2)}) copy-start(bf16[2,2,2,2,32,512]{5,4,3,2,1,0:T(8,128)(2,1)} %get-tuple-element.125) | copy-start | bytes 1572868
  143.1 9.9 %copy-start.16 = (f32[1024,512]{1,0:T(8,128)}, f32[1024,512]{1,0:T(8,128)S(1)}, u32[]{:S(2)}) copy-start(f32[1024,512]{1,0:T(8,128)S(1)} %get-tuple-element.292) | copy-start | bytes 6291460
  145.5 7.5 %copy-start.3 = (bf16[2,2,2,2,128,512]{5,4,3,2,1,0:T(8,128)(2,1)S(1)}, bf16[2,2,2,2,128,512]{5,4,3,2,1,0:T(8,128)(2,1)}, u32[]{:S(2)}) copy-start(bf16[2,2,2,2,128,512]{5,4,3,2,1,0:T(8,128)(2,1)} %get-tuple-element.127) | copy-start | bytes 6291460
  177.0 4.0 copy-start.5
  177.0 4.0 copy-start.17
  185.3 13.5 %copy-start.15 = (f32[2,512,512]{2,1,0:T(8,128)S(1)}, f32[2,512,512]{2,1,0:T(8,128)}, u32[]{:S(2)}) copy-start(f32[2,512,512]{2,1,0:T(8,128)} %copy-done.14) | copy-start | bytes 6291460
  198.8 5.8 %copy-start.10 = (bf16[1024,1536]{1,0:T(8,128)(2,1)}, bf16[1024,1536]{1,0:T(8,128)(2,1)S(1)}, u32[]{:S(2)}) copy-start(bf16[1024,1536]{1,0:T(8,128)(2,1)S(1)} %get-tuple-element.131) | copy-start | bytes 9437188
  210.3 12.5 %copy-start.19 = (f32[320,768]{1,0:T(8,128)S(1)}, f32[320,768]{1,0:T(8,128)}, u32[]{:S(2)}) copy-start(f32[320,768]{1,0:T(8,128)} %copy-done.18) | copy-start | bytes 2949124
  226.2 7.0 %copy-start.23 = (f32[320,768]{1,0:T(8,128)S(1)}, f32[320,768]{1,0:T(8,128)}, u32[]{:S(2)}) copy-start(f32[320,768]{1,0:T(8,128)} %copy-done.22) | copy-start | bytes 2949124
  226.2 7.0 %copy-start.40 = (bf16[2,2,2,2,48,2304]{5,4,3,2,1,0:T(8,128)(2,1)S(1)}, bf16[2,2,2,2,48,2304]{5,4,3,2,1,0:T(8,128)(2,1)}, u32[]{:S(2)}) copy-start(bf16[2,2,2,2,48,2304]{5,4,3,2,1,0:T(8,128)(2,1)} %get-tuple-element.119) | copy-start | bytes 10616836
  238.1 4.2 copy-start.11
  242.2 4.9 copy-start.13
  242.2 4.9 copy-start.24
  447.1 38.2 %copy-start.36 = (f32[16,256]{1,0:T(8,128)S(1)}, f32[16,256]{1,0:T(8,128)}, u32[]{:S(2)}) copy-start(f32[16,256]{1,0:T(8,128)} %get-tuple-element.201) | copy-start | bytes 49156
  447.1 38.2 %copy-start.35 = (f32[1248]{0:T(1024)S(1)}, f32[1248]{0:T(1024)}, u32[]{:S(2)}) copy-start(f32[1248]{0:T(1024)} %param.59) | copy-start | bytes 14980
  447.1 38.2 %copy-start.37 = (f32[1248]{0:T(1024)S(1)}, f32[1248]{0:T(1024)}, u32[]{:S(2)}) copy-start(f32[1248]{0:T(1024)} %param.60) | copy-start | bytes 14980
  447.1 38.2 %copy-start.38 = (f32[1248]{0:T(1024)S(1)}, f32[1248]{0:T(1024)}, u32[]{:S(2)}) copy-start(f32[1248]{0:T(1024)} %param.61) | copy-start | bytes 14980
  (25 other events, 49.6 us)

commit v5 on v4

--- a/solution.py
+++ b/solution.py
@@ -298,6 +298,7 @@
 REDUCE_STEPS = ((21, 17, 12, 9, 19, 15, 18, 4, 20, 3, 11, 10, 1, 0, 7, 14, 16, 5, 8, 13, 6, 2), (21, 17, 19, 15, 9, 12, 10, 14, 1, 20, 0, 18, 4, 8, 3, 7, 11, 13, 2, 16, 6, 5), (21, 17, 19, 20, 15, 18, 9, 14, 0, 10, 12, 8, 7, 16, 1, 6, 4, 5, 3, 11, 13, 2), (21, 17, 20, 15, 9, 19, 10, 18, 14, 0, 12, 8, 1, 16, 7, 6, 4, 5, 3, 2, 13, 11))
 OWNERS = (4, 11, 5, 10, 6, 9, 7, 8)
 SLOTS = 160
+GROUPS = 4
 
 
 def bit_count(devices):
@@ -409,13 +410,10 @@
             patches = patches + jnp.dot(
                 spread, fold[start : start + part, :], preferred_element_type=jnp.float32
             )
-        slot = lax.broadcasted_iota(jnp.int32, (SLOTS, NPATCH), 1)
-        chosen = jnp.where(slot == spots[clip], 1.0, 0.0).astype(jnp.bfloat16)
-        picked = jnp.dot(chosen, patches.astype(jnp.bfloat16), preferred_element_type=jnp.float32)
-        picked_out[clip] = picked.astype(jnp.bfloat16)
-        where_out[clip] = jnp.dot(chosen, table[:, :D], preferred_element_type=jnp.float32) + jnp.dot(
-            chosen, table[:, D:], preferred_element_type=jnp.float32
-        )
+        slot = lax.broadcasted_iota(jnp.int32, (NPATCH, SLOTS), 0)
+        chosen = jnp.where(slot == spots[clip : clip + 1, :], 1.0, 0.0).astype(jnp.bfloat16)
+        picked_out[clip] = dot_columns(chosen, patches.astype(jnp.bfloat16)).astype(jnp.bfloat16)
+        where_out[clip] = dot_columns(chosen, table[:, :D]) + dot_columns(chosen, table[:, D:])
         centred = patches - jnp.mean(patches, axis=-1, keepdims=True)
         spread = jnp.mean(centred * centred, axis=-1, keepdims=True)
         target_out[clip] = centred * lax.rsqrt(spread + 1e-06)
@@ -484,7 +482,11 @@
             short[number][...] = shards[number][...].astype(jnp.bfloat16)
             keep(number).start()
         hop(piece, 0, False).start()
-    tally_out[...] = tally[...]
+    masked = jnp.int32(0)
+    for clip in range(tally.shape[0]):
+        masked = masked + (NPATCH - tally[clip])
+    corner = lax.broadcasted_iota(jnp.int32, (8, 128), 0) + lax.broadcasted_iota(jnp.int32, (8, 128), 1) == 0
+    tally_out[...] = jnp.where(corner, masked.astype(jnp.float32), 0.0)
 
     def swap(stage):
         if stage < levels:
@@ -556,7 +558,7 @@
             jax.ShapeDtypeStruct((clips, SLOTS, D), jnp.float32),
             jax.ShapeDtypeStruct((clips, NPATCH, PATCH), jnp.float32),
         ],
-        in_specs=[far] * count + [vmem] + [far] * 6,
+        in_specs=[far] * count + [pl.BlockSpec(memory_space=pltpu.SMEM)] + [far] * 6,
         out_specs=[pl.BlockSpec(memory_space=pl.ANY)] * count + [vmem] * 4,
         scratch_shapes=[pltpu.VMEM(lead + shard.shape, jnp.bfloat16) for shard in shards]
         + [dma((count,))]
@@ -1216,7 +1218,7 @@
     low = (table - high.astype(np.float32)).astype(jnp.bfloat16)
     return (
         spec.reshape(spec.shape[0], GT, PS * GF * PS),
-        window_place(jnp.pad(keep, ((0, 0), (0, SLOTS - VIS))))[:, :, None],
+        window_place(jnp.pad(keep, ((0, 0), (0, SLOTS - VIS)))),
         jnp.asarray(take, jnp.bfloat16),
         jnp.asarray(row[:, None] % GF),
         jnp.asarray(fold, jnp.bfloat16),
@@ -1357,6 +1359,12 @@
 
 
 def window_kernel(size, joined, allowed, out):
+    for group in range(allowed.shape[0]):
+        rows = pl.ds(group * 128, 128)
+        window_group(size, joined.at[rows], allowed.at[group], out.at[rows])
+
+
+def window_group(size, joined, allowed, out):
     width = out.shape[1]
     allow = allowed[...][None] > 0.0
     for lane in range(0, width, 128):
@@ -1368,14 +1376,21 @@
 
 
 def window_back_kernel(size, joined, allowed, grad, out, query_sum, value_sum):
-    width = grad.shape[1]
-    allow = allowed[...][None] > 0.0
-
     @pl.when(pl.program_id(0) == 0)
     def clear():
         query_sum[...] = jnp.zeros_like(query_sum)
         value_sum[...] = jnp.zeros_like(value_sum)
 
+    for group in range(allowed.shape[0]):
+        rows = pl.ds(group * 128, 128)
+        window_back_group(
+            size, joined.at[rows], allowed.at[group], grad.at[rows], out.at[rows], query_sum, value_sum
+        )
+
+
+def window_back_group(size, joined, allowed, grad, out, query_sum, value_sum):
+    width = grad.shape[1]
+    allow = allowed[...][None] > 0.0
     for lane in range(0, width, 128):
         queries = joined[:, lane : lane + 128]
         keys_here = stack_heads(joined[:, width + lane : width + lane + 128], size)
@@ -1400,7 +1415,8 @@
     steps = joined.shape[0] // rows
     period = allowed.shape[0]
     wide = pl.BlockSpec((rows, joined.shape[1]), lambda step: (step, 0))
-    mask = pl.BlockSpec((None,) + allowed.shape[1:], lambda step: (lax.rem(step, period), 0, 0))
+    rest = (0,) * (allowed.ndim - 1)
+    mask = pl.BlockSpec((None,) + allowed.shape[1:], lambda step: (lax.rem(step, period),) + rest)
     narrow_rows = pl.BlockSpec((rows, joined.shape[1] // 3), lambda step: (step, 0))
     return steps, wide, mask, narrow_rows
 
@@ -1437,6 +1453,27 @@
     )(joined, allowed, grad)
 
 
+def weight_grad_kernel(rows, grad, out):
+    out[...] = dot_columns(rows[...], grad[...]).astype(out.dtype)
+
+
+def weight_grad(rows, grad, kind):
+    (tokens, height), width = rows.shape, grad.shape[1]
+    tile = width // 3
+    return pl.pallas_call(
+        weight_grad_kernel,
+        grid=(3,),
+        out_shape=jax.ShapeDtypeStruct((height, width), kind),
+        in_specs=[
+            pl.BlockSpec((tokens, height), lambda step: (0, 0)),
+            pl.BlockSpec((tokens, tile), lambda step: (0, step)),
+        ],
+        out_specs=pl.BlockSpec((height, tile), lambda step: (0, step)),
+        compiler_params=pltpu.CompilerParams(vmem_limit_bytes=40 * 2**20),
+        name="weight_grad",
+    )(rows, grad)
+
+
 def attention_block(forward, backward, rows, size):
     def join(normed, matrix, query_bias, value_bias):
         width = matrix.shape[1] // 3
@@ -1461,7 +1498,7 @@
             backward, joined, allowed, grad.astype(jnp.bfloat16), rows, size
         )
         normed_grad = dot_rows(pulled, matrix.astype(jnp.bfloat16))
-        matrix_grad = dot_columns(short, pulled).astype(matrix.dtype)
+        matrix_grad = weight_grad(short, pulled, matrix.dtype)
         return normed_grad, matrix_grad, query_sum[0], value_sum[0], jnp.zeros_like(allowed)
 
     apply.defvjp(keep, back)
@@ -1469,7 +1506,7 @@
 
 
 encoder_attention = attention_block(attention_kernel, attention_back_kernel, SLOTS, HEAD)
-decoder_attention = attention_block(window_kernel, window_back_kernel, 8 * WIN * WIN, DHEAD)
+decoder_attention = attention_block(window_kernel, window_back_kernel, GROUPS * 8 * WIN * WIN, DHEAD)
 
 
 def gelu_keep(value):
@@ -1493,7 +1530,7 @@
 
 def hidden_backward(normed, inner, slope, grad, up, down):
     (tokens, width), units = normed.shape, inner.shape[1]
-    tile = 512
+    tile = 1024
     whole = pl.BlockSpec((tokens, width), lambda step: (0, 0))
     columns = pl.BlockSpec((tokens, tile), lambda step: (0, step))
     up_tile = pl.BlockSpec((width, tile), lambda step: (0, step))
@@ -1545,7 +1582,8 @@
     region = region * 3 + (freq_col >= GF - WIN) + (freq_col >= GF - SHIFT)
     region = region.reshape(-1, 8, 1, WIN * WIN)
     same = region == region.transpose(0, 1, 3, 2)
-    return same.transpose(0, 2, 1, 3).reshape(-1, WIN * WIN, 8 * WIN * WIN).astype(np.float32)
+    same = same.transpose(0, 2, 1, 3).reshape(-1, GROUPS, WIN * WIN, 8 * WIN * WIN)
+    return same.astype(np.float32)
 
 
 def local_loss(weights, picked, where, target, keep, counts):
@@ -1595,10 +1633,8 @@
     own[10] = jnp.pad(own[10], (0, spare - vector_rows)).reshape(VEC_ROWS, VEC_COLS)
     row = lax.broadcasted_iota(jnp.int32, (8, 128), 0)
     column = lax.broadcasted_iota(jnp.int32, (8, 128), 1)
-    first = jnp.logical_and(row == 0, column == 0)
-    count_part = jnp.sum(NPATCH - counts).astype(jnp.float32)
     scene = window_scene(spectrogram, keep)
-    gathered, tally, made = gather_rows(own, jnp.where(first, count_part, 0.0), scene, devices)
+    gathered, tally, made = gather_rows(own, counts, scene, devices)
     mask_count = tally[0, 0]
     weights = [piece.reshape(-1, piece.shape[-1]) for piece in gathered[:10]]
     weights[4] = weights[4].astype(jnp.float32)

time: 500 us -> 486 us (0.972)
  matrix products: 52.7 us -> 40.1 us
    dot_general x2 -> x1, matrix products: 10.6 us -> 2.3 us  [local_loss(): decoder_attention(normed, weights[4], pieces[4], pieces[5], jnp.asarray(w...]
    unnamed x104 -> x102, local copies, waits for them, and re-layouts: 12.2 us -> 14.7 us
    pallas_call x1 -> x2, Pallas kernels: 13.5 us -> 14.7 us  [local_loss(): decoder_attention(normed, weights[4], pieces[4], pieces[5], jnp.asarray(w...]
where the time goes in v5:
time: 486 us; the launch traced here: 478 us
  Pallas kernels  392 us (81%)
  matrix products  40.1 us (8%)
  local copies, waits for them, and re-layouts  20.9 us (4%)
  other arithmetic  19.8 us (4%)
    pallas_call x1, Pallas kernels, reduce_rows(): pl.pallas_call(functools.partial(reduce_kernel, levels, pieces, count, ow...  148 us
    pallas_call x1, Pallas kernels, gather_rows(): pl.pallas_call(functools.partial(gather_kernel, levels, pieces, count), o...  99.9 us
    pallas_call x1, Pallas kernels, orthogonalize(): pl.pallas_call(functools.partial(muon_kernel, owners, shapes), out_shape=...  44.4 us
    pallas_call x1, Pallas kernels, return_rows(): pl.pallas_call(functools.partial(return_kernel, owners, count, devices),...  39.9 us
    pallas_call x2, Pallas kernels, local_loss(): decoder_attention(normed, weights[4], pieces[4], pieces[5], jnp.asarray(w...  14.7 us
    unnamed x102, local copies, waits for them, and re-layouts  14.7 us
    pallas_call x1, Pallas kernels, local_loss(): hidden_layer(normed, weights[2], pieces[7], weights[3])  12.8 us
    pallas_call x1, Pallas kernels, local_loss(): hidden_layer(normed, weights[6], pieces[9], weights[7])  12.2 us

profile of v5, /device:TPU:15, one launch (start us, length us, event | category | flops | bytes accessed | tf_op | source)
XLA Modules:
  0.0 477.6 jit_solution(11280639173637463335)
XLA Ops:
  3.8 2.1 reshape.521.refs_12_
  5.8 99.9 %gather_rows.1 = (bf16[2,2,2,2,48,2304]{5,4,3,2,1,0:T(8,128)(2,1)}, bf16[2,2,2,2,48,768]{5,4,3,2,1,0:T(8,128)(2,1)}, bf16[2,2,2,2,48,3072]{5,4,3,2,1,0:T(8,128)(...) custom-call(f32[48,2304]{1,0:T(8,128)} %refs_8_.3, ...), custom_call_target="tpu_custom_call" | custom-call | tf_op jit(solution)/shard_map/gather_rows/pallas_call | solution.py:552
  108.8 1.9 fusion.68
  112.7 3.4 jvp_attention_forward_.2
  117.3 3.9 fusion.8
  121.3 1.8 fusion.70
  124.7 2.4 fusion.71
  129.2 1.8 add_convert_fusion.joined
  131.1 3.5 jvp_attention_forward_.3
  137.7 7.4 %fusion.3 = (f32[1024,2048]{1,0:T(8,128)}, bf16[1024,2048]{1,0:T(8,128)(2,1)S(1)}) fusion(f32[2048]{0:T(1024)S(1)} %slice.179, bf16[1024,512]{1,0:T(8,128)(2,1)S(1)} %add_convert_fusion.3.normed, bf16[512,2048]{1,0:T(8,128)(2,1)S(1)} %bitcast.117), kind=kOutput, calls=%fused_computation.4 | convolution fusion | flops 2170552320 | bytes 15736832 | tf_op jit(solution)/shard_map/jvp()/dot_general | solution.py:1561
  145.2 2.4 fusion.73
  157.1 12.2 %transpose_jvp_hidden_backward__.2 = (f32[1024,512]{1,0:T(8,128)S(1)}, bf16[512,2048]{1,0:T(8,128)(2,1)S(1)}, bf16[2048,512]{1,0:T(8,128)(2,1)S(1)}, f32[8,2048]{1,0:T(8,128)S(1)}) custom-call(bf16[1024,512]{1,0:T(8,128)(2,1)S(1)} %add_convert_fusion.3.normed, bf16[1024,2048]{1,0:T(8,128)(2,1)} %copy-done.24, f32[1024,2048]{1,0:T(8,128)} %get-tuple-element.242.slope, ...), custom_call_target="tpu_custom_call" | custom-call | tf_op jit(solution)/shard_map/transpose(jvp(hidden_backward))/pallas_call | solution.py:1615
  169.4 3.9 multiply_reduce_fusion.2
  177.7 12.1 %transpose_jvp_attention_backward__.2 = (bf16[1024,1536]{1,0:T(8,128)(2,1)S(1)}, f32[8,512]{1,0:T(8,128)S(1)}, f32[8,512]{1,0:T(8,128)S(1)}) custom-call(bf16[1024,1536]{1,0:T(8,128)(2,1)S(1)} %add_convert_fusion.joined, f32[1,4,16,128]{3,2,1,0:T(8,128)S(1)} %copy-done.11, bf16[1024,512]{1,0:T(8,128)(2,1)S(1)} %convolution_convert_fusion.1.grad), custom_call_target="tpu_custom_call" | custom-call | tf_op jit(solution)/shard_map/transpose(jvp(attention_backward))/pallas_call | solution.py:1612
  189.8 2.3 multiply_reduce_fusion.1
  192.1 2.6 transpose_jvp_weight_grad__.3
  201.4 12.8 %transpose_jvp_hidden_backward__.3 = (f32[320,768]{1,0:T(8,128)S(1)}, bf16[768,3072]{1,0:T(8,128)(2,1)S(1)}, bf16[3072,768]{1,0:T(8,128)(2,1)}, f32[8,3072]{1,0:T(8,128)S(1)}) custom-call(bf16[320,768]{1,0:T(8,128)(2,1)S(1)} %add_convert_fusion.7.normed, bf16[320,3072]{1,0:T(8,128)(2,1)S(1)} %copy-done.10, f32[320,3072]{1,0:T(8,128)S(1)} %get-tuple-element.244.slope, ...), custom_call_target="tpu_custom_call" | custom-call | tf_op jit(solution)/shard_map/transpose(jvp(hidden_backward))/pallas_call | solution.py:1602
  218.2 6.1 %transpose_jvp_attention_backward__.3 = (bf16[320,2304]{1,0:T(8,128)(2,1)S(1)}, f32[8,768]{1,0:T(8,128)S(1)}, f32[8,768]{1,0:T(8,128)S(1)}) custom-call(bf16[320,2304]{1,0:T(8,128)(2,1)S(1)} %fusion.4.joined, f32[2,160,160]{2,1,0:T(8,128)S(1)} %broadcast_in_dim.41.allowed, bf16[320,768]{1,0:T(8,128)(2,1)S(1)} %convolution_convert_fusion.4.grad), custom_call_target="tpu_custom_call" | custom-call | tf_op jit(solution)/shard_map/transpose(jvp(attention_backward))/pallas_call | solution.py:1599
  227.2 1.9 convolution_convert_fusion
  231.0 2.8 transpose_jvp_weight_grad__.2
  235.5 148.5 %reduce_rows.1 = (f32[48,2304]{1,0:T(8,128)}, f32[48,768]{1,0:T(8,128)}, f32[48,3072]{1,0:T(8,128)}, f32[192,768]{1,0:T(8,128)}, f32[32,1536]{1,0:T(8,128)}, /*i...) custom-call(bf16[2,2,2,2,48,2304]{5,4,3,2,1,0:T(8,128)(2,1)} %bitcas, ...), custom_call_target="tpu_custom_call" | custom-call | tf_op jit(solution)/shard_map/reduce_rows/pallas_call | solution.py:819
  387.2 44.4 %orthogonalize.1 = (bf16[768,2304]{1,0:T(8,128)(2,1)}, bf16[768,768]{1,0:T(8,128)(2,1)}, bf16[768,3072]{1,0:T(8,128)(2,1)}, bf16[3072,768]{1,0:T(8,128)(2,1)}, b...) custom-call(bf16[768,2304]{1,0:T(8,128)(2,1)} %bitcast.141, ...), custom_call_target="tpu_custom_call" | custom-call | tf_op jit(solution)/shard_map/orthogonalize/pallas_call | solution.py:1159
  431.6 39.9 %return_rows.1 = (bf16[48,2304]{1,0:T(8,128)(2,1)}, bf16[48,768]{1,0:T(8,128)(2,1)}, bf16[48,3072]{1,0:T(8,128)(2,1)}, bf16[192,768]{1,0:T(8,128)(2,1)}, bf16[32...) custom-call(bf16[16,48,2304]{2,1,0:T(8,128)(2,1)} %bitcast.140, ...), custom_call_target="tpu_custom_call" | custom-call | tf_op jit(solution)/shard_map/return_rows/pallas_call | solution.py:925
  472.2 3.8 finish.1
  (204 shorter events, 49.0 us)
Async XLA Ops:
  1.4 4.4 copy-start.31
  110.7 5.3 %copy-start.18 = (f32[320,768]{1,0:T(8,128)}, f32[320,768]{1,0:T(8,128)S(1)}, u32[]{:S(2)}) copy-start(f32[320,768]{1,0:T(8,128)S(1)} %get-tuple-element.284) | copy-start | bytes 2949124
  111.1 6.2 %slice-start = ((s8[4718592]{0:T(1024)(128)(4,1)}), s8[4194304]{0:T(1024)(128)(4,1)S(1)}, s32[]{:S(2)}) async-start(s8[4718592]{0:T(1024)(128)(4,1)} %bitcast.128), calls=%async_computation | async-start | bytes 8388608
  111.3 5.9 %slice-start.1 = ((s8[4718592]{0:T(1024)(128)(4,1)}), s8[524288]{0:T(1024)(128)(4,1)S(1)}, s32[]{:S(2)}) async-start(s8[4718592]{0:T(1024)(128)(4,1)} %bitcast.128), calls=%async_computation.1 | async-start | bytes 1048576
  116.7 4.5 copy-start.16
  117.0 4.2 slice-start.2
  117.3 4.0 slice-start.3
  123.1 4.0 copy-start.25
  127.1 7.5 %copy-start.12 = (f32[2,512,512]{2,1,0:T(8,128)}, f32[2,512,512]{2,1,0:T(8,128)S(1)}, u32[]{:S(2)}) copy-start(f32[2,512,512]{2,1,0:T(8,128)S(1)} %get-tuple-element.290) | copy-start | bytes 6291460
  131.1 3.5 copy-start.27
  135.4 9.8 %copy-start.14 = (f32[1024,512]{1,0:T(8,128)}, f32[1024,512]{1,0:T(8,128)S(1)}, u32[]{:S(2)}) copy-start(f32[1024,512]{1,0:T(8,128)S(1)} %get-tuple-element.292) | copy-start | bytes 6291460
  137.7 7.5 %copy-start.5 = (bf16[2,2,2,2,128,512]{5,4,3,2,1,0:T(8,128)(2,1)S(1)}, bf16[2,2,2,2,128,512]{5,4,3,2,1,0:T(8,128)(2,1)}, u32[]{:S(2)}) copy-start(bf16[2,2,2,2,128,512]{5,4,3,2,1,0:T(8,128)(2,1)} %get-tuple-element.127) | copy-start | bytes 6291460
  169.3 4.0 copy-start.7
  169.4 4.0 copy-start.8
  169.4 4.0 copy-start.15
  177.7 12.1 %copy-start.13 = (f32[2,512,512]{2,1,0:T(8,128)S(1)}, f32[2,512,512]{2,1,0:T(8,128)}, u32[]{:S(2)}) copy-start(f32[2,512,512]{2,1,0:T(8,128)} %copy-done.12) | copy-start | bytes 6291460
  177.7 12.1 %copy-start.40 = (bf16[2,2,2,2,32,1536]{5,4,3,2,1,0:T(8,128)(2,1)S(1)}, bf16[2,2,2,2,32,1536]{5,4,3,2,1,0:T(8,128)(2,1)}, u32[]{:S(2)}) copy-start(bf16[2,2,2,2,32,1536]{5,4,3,2,1,0:T(8,128)(2,1)} %get-tuple-element.124) | copy-start | bytes 4718596
  201.4 12.8 %copy-start.17 = (f32[320,768]{1,0:T(8,128)S(1)}, f32[320,768]{1,0:T(8,128)}, u32[]{:S(2)}) copy-start(f32[320,768]{1,0:T(8,128)} %copy-done.16) | copy-start | bytes 2949124
  217.6 6.7 %copy-start.19 = (f32[320,768]{1,0:T(8,128)S(1)}, f32[320,768]{1,0:T(8,128)}, u32[]{:S(2)}) copy-start(f32[320,768]{1,0:T(8,128)} %copy-done.18) | copy-start | bytes 2949124
  217.6 6.7 %copy-start.38 = (bf16[2,2,2,2,48,2304]{5,4,3,2,1,0:T(8,128)(2,1)S(1)}, bf16[2,2,2,2,48,2304]{5,4,3,2,1,0:T(8,128)(2,1)}, u32[]{:S(2)}) copy-start(bf16[2,2,2,2,48,2304]{5,4,3,2,1,0:T(8,128)(2,1)} %get-tuple-element.119) | copy-start | bytes 10616836
  431.5 40.0 %copy-start.34 = (f32[16,256]{1,0:T(8,128)S(1)}, f32[16,256]{1,0:T(8,128)}, u32[]{:S(2)}) copy-start(f32[16,256]{1,0:T(8,128)} %get-tuple-element.201) | copy-start | bytes 49156
  431.5 40.0 %copy-start.33 = (f32[1248]{0:T(1024)S(1)}, f32[1248]{0:T(1024)}, u32[]{:S(2)}) copy-start(f32[1248]{0:T(1024)} %param.59) | copy-start | bytes 14980
  431.5 40.0 %copy-start.35 = (f32[1248]{0:T(1024)S(1)}, f32[1248]{0:T(1024)}, u32[]{:S(2)}) copy-start(f32[1248]{0:T(1024)} %param.60) | copy-start | bytes 14980
  431.6 40.0 %copy-start.36 = (f32[1248]{0:T(1024)S(1)}, f32[1248]{0:T(1024)}, u32[]{:S(2)}) copy-start(f32[1248]{0:T(1024)} %param.61) | copy-start | bytes 14980
  (24 other events, 43.6 us)

commit v6 on v5

--- a/solution.py
+++ b/solution.py
@@ -421,7 +421,8 @@
 
 def gather_kernel(levels, pieces, count, *refs):
     sources, tally, rest = refs[:count] + refs[count + 1 : count + 7], refs[count], refs[count + 7 :]
-    outs, tally_out, made, rest = rest[:count], rest[count], rest[count + 1 : count + 4], rest[count + 4 :]
+    outs, count_out, made, rest = rest[:count], rest[count], rest[count + 1 : count + 4], rest[count + 4 :]
+    tally_out, rest = rest[0], rest[1:]
     wholes, save_sem, rest = rest[:count], rest[count], rest[count + 1 :]
     short, held, load_sem, rest = rest[:count], rest[count : 2 * count + 6], rest[2 * count + 6], rest[2 * count + 7 :]
     shards, scene = held[:count], held[count:]
@@ -538,6 +539,7 @@
         for stage in range(levels):
             hop(piece, stage, False).wait_send()
             cross(piece, stage, core).wait_send()
+    count_out[...] = tally_out[0:1, 0:1]
     for number in range(count):
         save(number).wait()
 
@@ -553,14 +555,15 @@
         functools.partial(gather_kernel, levels, pieces, count),
         out_shape=[jax.ShapeDtypeStruct(lead + shard.shape, jnp.bfloat16) for shard in shards]
         + [
-            jax.ShapeDtypeStruct((8, 128), jnp.float32),
+            jax.ShapeDtypeStruct((1, 1), jnp.float32),
             jax.ShapeDtypeStruct((clips, SLOTS, PATCH), jnp.bfloat16),
             jax.ShapeDtypeStruct((clips, SLOTS, D), jnp.float32),
             jax.ShapeDtypeStruct((clips, NPATCH, PATCH), jnp.float32),
         ],
         in_specs=[far] * count + [pl.BlockSpec(memory_space=pltpu.SMEM)] + [far] * 6,
         out_specs=[pl.BlockSpec(memory_space=pl.ANY)] * count + [vmem] * 4,
-        scratch_shapes=[pltpu.VMEM(lead + shard.shape, jnp.bfloat16) for shard in shards]
+        scratch_shapes=[pltpu.VMEM((8, 128), jnp.float32)]
+        + [pltpu.VMEM(lead + shard.shape, jnp.bfloat16) for shard in shards]
         + [dma((count,))]
         + [pltpu.VMEM(shard.shape, jnp.bfloat16) for shard in shards]
         + [pltpu.VMEM(piece.shape, piece.dtype) for piece in (*shards, *scene)]
@@ -747,7 +750,8 @@
     for number in range(blocks, count):
         share(number, core).start()
     row = lax.broadcasted_iota(jnp.int32, (8, 128), 0)
-    stats_out[...] = jnp.where(row == 0, jnp.sum(squares, axis=0, keepdims=True), stats_in[...])
+    others = jnp.where(row == 1, stats_in[...], 0.0)
+    stats_out[...] = jnp.where(row == 0, jnp.sum(squares, axis=0, keepdims=True), others)
     add_up(me, core, devices, stats_out, stats_land, stats_send, stats_recv, own_sem)
     norm = jnp.sqrt(jnp.sum(stats_out[0:1, :], axis=1, keepdims=True))
     factor = jnp.minimum(1.0, CLIP_MAX / (norm + 1e-06))
@@ -963,6 +967,7 @@
     mats, moved, stats, adam_in = refs[:count], refs[count : 2 * count], refs[2 * count], refs[2 * count + 1 :][:8]
     rest = refs[2 * count + 9 :]
     outs, moved_out, adam_out, rest = rest[:count], rest[count : 2 * count], rest[2 * count :][:6], rest[2 * count + 6 :]
+    norm_out, loss_out, rest = rest[0], rest[1], rest[2:]
     exact, wide, wide_low, tall, wide_out, tall_out, gram = rest[:7]
     base, poly, other, chain, sem, in_sem, out_sem = rest[7:14]
     held_rows = rest[14:]
@@ -977,6 +982,8 @@
         move_in(number).start()
     norm = jnp.sqrt(jnp.sum(stats[0:1, :], axis=1, keepdims=True))
     factor = jnp.minimum(1.0, CLIP_MAX / (norm + 1e-06))
+    norm_out[...] = norm
+    loss_out[...] = stats[1:2, 0:1]
     for group in range(2):
         weight, first, second, grad = [ref[...] for ref in adam_in[4 * group : 4 * group + 4]]
         made = adam_update(weight, first, second, grad * factor, DECAY)
@@ -1160,9 +1167,10 @@
         functools.partial(muon_kernel, owners, shapes),
         out_shape=[jax.ShapeDtypeStruct(shape, jnp.bfloat16) for shape in shapes]
         + [jax.ShapeDtypeStruct(piece.shape, piece.dtype) for piece in moved]
-        + [jax.ShapeDtypeStruct(piece.shape, piece.dtype) for piece in renewed],
+        + [jax.ShapeDtypeStruct(piece.shape, piece.dtype) for piece in renewed]
+        + [jax.ShapeDtypeStruct((1, 1), jnp.float32)] * 2,
         in_specs=[anywhere] * (2 * count) + [vmem] * 9,
-        out_specs=[anywhere] * (2 * count) + [vmem] * 6,
+        out_specs=[anywhere] * (2 * count) + [vmem] * 8,
         scratch_shapes=[
             pltpu.VMEM(fine, jnp.float32),
             pltpu.VMEM((side, longest), jnp.bfloat16),
@@ -1183,7 +1191,7 @@
         compiler_params=pltpu.CompilerParams(vmem_limit_bytes=60 * 2**20),
         name="orthogonalize",
     )(*mats, *moved, stats, *adam)
-    return found[:count], found[count : 2 * count], found[2 * count : 2 * count + 3], found[2 * count + 3 :]
+    return found[:count], found[count : 2 * count], found[2 * count :]
 
 
 def window_place(position):
@@ -1631,11 +1639,9 @@
     vector_rows = own[10].shape[0]
     spare = VEC_ROWS * VEC_COLS
     own[10] = jnp.pad(own[10], (0, spare - vector_rows)).reshape(VEC_ROWS, VEC_COLS)
-    row = lax.broadcasted_iota(jnp.int32, (8, 128), 0)
-    column = lax.broadcasted_iota(jnp.int32, (8, 128), 1)
     scene = window_scene(spectrogram, keep)
     gathered, tally, made = gather_rows(own, counts, scene, devices)
-    mask_count = tally[0, 0]
+    mask_count = tally.reshape(())
     weights = [piece.reshape(-1, piece.shape[-1]) for piece in gathered[:10]]
     weights[4] = weights[4].astype(jnp.float32)
     vectors = gathered[10].reshape(devices, spare)[:, :vector_rows].reshape(-1).astype(jnp.float32)
@@ -1649,16 +1655,15 @@
         grad = grads[number]
         grads[number] = grad.reshape(lead + (grad.shape[0] // devices, grad.shape[1]))
     renewed, others, stats, collected = reduce_rows(
-        grads, jnp.where(jnp.logical_and(row == 1, column == 0), loss_part, 0.0), moments, OWNERS, devices
-    )
-    loss_sum = stats[1, 0]
-    grad_norm = jnp.sqrt(jnp.sum(stats[0]))
-    factor = jnp.minimum(1.0, CLIP_MAX / (grad_norm + 1e-06))
+        grads, loss_part.reshape(1, 1), moments, OWNERS, devices
+    )
     adam = (*rest[16:19], others[0], *rest[19:22], others[1])
     flat = [piece.reshape(-1, piece.shape[2]) for piece in collected]
-    made, renewed, patch_new, embed_new = orthogonalize(flat, renewed, stats, adam, OWNERS)
+    made, renewed, more = orthogonalize(flat, renewed, stats, adam, OWNERS)
+    patch_new, embed_new, grad_norm, loss_sum = more[:3], more[3:6], more[6].reshape(()), more[7].reshape(())
     made = [piece.reshape(devices, -1, piece.shape[1]) for piece in made]
     new_weights = finish(return_rows(made, OWNERS, devices), masters[:8], devices)
+    factor = jnp.minimum(1.0, CLIP_MAX / (grad_norm + 1e-06))
     vector_grad = others[2].reshape(-1)[:vector_rows] * factor
     vector_new = adam_update(*rest[22:25], vector_grad, 0.0)
     return (loss_sum, mask_count, grad_norm, *new_weights, *renewed, *patch_new, *embed_new, *vector_new)

time: 486 us -> 490 us (level)
    unnamed x102 -> x232, local copies, waits for them, and re-layouts: 14.7 us -> 15.8 us
where the time goes in v6:
time: 490 us; the launch traced here: 482 us
  Pallas kernels  392 us (80%)
  matrix products  42.6 us (9%)
  local copies, waits for them, and re-layouts  22.1 us (5%)
  other arithmetic  18.9 us (4%)
  between operations  5.9 us (1%)
    pallas_call x1, Pallas kernels, reduce_rows(): pl.pallas_call(functools.partial(reduce_kernel, levels, pieces, count, ow...  149 us
    pallas_call x1, Pallas kernels, gather_rows(): pl.pallas_call(functools.partial(gather_kernel, levels, pieces, count), o...  99.9 us
    pallas_call x1, Pallas kernels, orthogonalize(): pl.pallas_call(functools.partial(muon_kernel, owners, shapes), out_shape=...  44.5 us
    pallas_call x1, Pallas kernels, return_rows(): pl.pallas_call(functools.partial(return_kernel, owners, count, devices),...  40 us
    unnamed x232, local copies, waits for them, and re-layouts  15.8 us
    pallas_call x2, Pallas kernels, local_loss(): decoder_attention(normed, weights[4], pieces[4], pieces[5], jnp.asarray(w...  14.7 us
    pallas_call x1, Pallas kernels, local_loss(): hidden_layer(normed, weights[2], pieces[7], weights[3])  12.7 us
    pallas_call x1, Pallas kernels, local_loss(): hidden_layer(normed, weights[6], pieces[9], weights[7])  12.2 us

profile of v6, /device:TPU:15, one launch (start us, length us, event | category | flops | bytes accessed | tf_op | source)
XLA Modules:
  0.0 481.6 jit_solution(12837784713655649227)
XLA Ops:
  4.9 2.1 reshape.533.refs_12_
  7.0 99.9 %gather_rows.1 = (bf16[2,2,2,2,48,2304]{5,4,3,2,1,0:T(8,128)(2,1)}, bf16[2,2,2,2,48,768]{5,4,3,2,1,0:T(8,128)(2,1)}, bf16[2,2,2,2,48,3072]{5,4,3,2,1,0:T(8,128)(...) custom-call(f32[48,2304]{1,0:T(8,128)} %refs_8_.3, ...), custom_call_target="tpu_custom_call" | custom-call | tf_op jit(solution)/shard_map/gather_rows/pallas_call | solution.py:554
  108.7 1.9 fusion.68
  112.7 3.4 jvp_attention_forward_.2
  117.9 3.7 fusion.8
  121.7 1.8 fusion.70
  125.1 2.4 fusion.71
  131.9 3.5 jvp_attention_forward_.3
  138.6 7.7 %fusion.3 = (f32[1024,2048]{1,0:T(8,128)}, bf16[1024,2048]{1,0:T(8,128)(2,1)S(1)}) fusion(f32[2048]{0:T(1024)S(1)} %slice.167, bf16[1024,512]{1,0:T(8,128)(2,1)S(1)} %add_convert_fusion.3.normed, bf16[512,2048]{1,0:T(8,128)(2,1)S(1)} %bitcast.121), kind=kOutput, calls=%fused_computation.4 | convolution fusion | flops 2170552320 | bytes 15736832 | tf_op jit(solution)/shard_map/jvp()/dot_general | solution.py:1569
  146.3 2.4 fusion.73
  159.1 12.2 %transpose_jvp_hidden_backward__.2 = (f32[1024,512]{1,0:T(8,128)S(1)}, bf16[512,2048]{1,0:T(8,128)(2,1)S(1)}, bf16[2048,512]{1,0:T(8,128)(2,1)S(1)}, f32[8,2048]{1,0:T(8,128)S(1)}) custom-call(bf16[1024,512]{1,0:T(8,128)(2,1)S(1)} %add_convert_fusion.3.normed, bf16[1024,2048]{1,0:T(8,128)(2,1)} %copy-done.24, f32[1024,2048]{1,0:T(8,128)} %get-tuple-element.246.slope, ...), custom_call_target="tpu_custom_call" | custom-call | tf_op jit(solution)/shard_map/transpose(jvp(hidden_backward))/pallas_call | solution.py:1623
  172.1 3.8 multiply_reduce_fusion.2
  180.8 12.0 %transpose_jvp_attention_backward__.2 = (bf16[1024,1536]{1,0:T(8,128)(2,1)S(1)}, f32[8,512]{1,0:T(8,128)S(1)}, f32[8,512]{1,0:T(8,128)S(1)}) custom-call(bf16[1024,1536]{1,0:T(8,128)(2,1)S(1)} %add_convert_fusion.joined, f32[1,4,16,128]{3,2,1,0:T(8,128)S(1)} %copy-done.11, bf16[1024,512]{1,0:T(8,128)(2,1)S(1)} %convolution_convert_fusion.1.grad), custom_call_target="tpu_custom_call" | custom-call | tf_op jit(solution)/shard_map/transpose(jvp(attention_backward))/pallas_call | solution.py:1620
  194.1 2.8 multiply_reduce_fusion.1
  196.9 2.6 transpose_jvp_weight_grad__.3
  206.6 12.7 %transpose_jvp_hidden_backward__.3 = (f32[320,768]{1,0:T(8,128)S(1)}, bf16[768,3072]{1,0:T(8,128)(2,1)S(1)}, bf16[3072,768]{1,0:T(8,128)(2,1)}, f32[8,3072]{1,0:T(8,128)S(1)}) custom-call(bf16[320,768]{1,0:T(8,128)(2,1)S(1)} %add_convert_fusion.7.normed, bf16[320,3072]{1,0:T(8,128)(2,1)S(1)} %copy-done.10, f32[320,3072]{1,0:T(8,128)S(1)} %get-tuple-element.248.slope, ...), custom_call_target="tpu_custom_call" | custom-call | tf_op jit(solution)/shard_map/transpose(jvp(hidden_backward))/pallas_call | solution.py:1610
  223.3 6.1 %transpose_jvp_attention_backward__.3 = (bf16[320,2304]{1,0:T(8,128)(2,1)S(1)}, f32[8,768]{1,0:T(8,128)S(1)}, f32[8,768]{1,0:T(8,128)S(1)}) custom-call(bf16[320,2304]{1,0:T(8,128)(2,1)S(1)} %fusion.4.joined, f32[2,160,160]{2,1,0:T(8,128)S(1)} %broadcast_in_dim.35.allowed, bf16[320,768]{1,0:T(8,128)(2,1)S(1)} %convolution_convert_fusion.4.grad), custom_call_target="tpu_custom_call" | custom-call | tf_op jit(solution)/shard_map/transpose(jvp(attention_backward))/pallas_call | solution.py:1607
  232.6 1.8 convolution_convert_fusion
  236.4 2.8 transpose_jvp_weight_grad__.2
  239.2 1.9 copy-done
  241.0 148.7 %reduce_rows.1 = (f32[48,2304]{1,0:T(8,128)}, f32[48,768]{1,0:T(8,128)}, f32[48,3072]{1,0:T(8,128)}, f32[192,768]{1,0:T(8,128)}, f32[32,1536]{1,0:T(8,128)}, /*i...) custom-call(bf16[2,2,2,2,48,2304]{5,4,3,2,1,0:T(8,128)(2,1)} %bitcas, ...), custom_call_target="tpu_custom_call" | custom-call | tf_op jit(solution)/shard_map/reduce_rows/pallas_call | solution.py:823
  389.7 44.5 %orthogonalize.1 = (bf16[768,2304]{1,0:T(8,128)(2,1)}, bf16[768,768]{1,0:T(8,128)(2,1)}, bf16[768,3072]{1,0:T(8,128)(2,1)}, bf16[3072,768]{1,0:T(8,128)(2,1)}, b...) custom-call(bf16[768,2304]{1,0:T(8,128)(2,1)} %bitcast.143, ...), custom_call_target="tpu_custom_call" | custom-call | tf_op jit(solution)/shard_map/orthogonalize/pallas_call | solution.py:1166
  435.0 40.0 %return_rows.1 = (bf16[48,2304]{1,0:T(8,128)(2,1)}, bf16[48,768]{1,0:T(8,128)(2,1)}, bf16[48,3072]{1,0:T(8,128)(2,1)}, bf16[192,768]{1,0:T(8,128)(2,1)}, bf16[32...) custom-call(bf16[16,48,2304]{2,1,0:T(8,128)(2,1)} %bitcast.142, ...), custom_call_target="tpu_custom_call" | custom-call | tf_op jit(solution)/shard_map/return_rows/pallas_call | solution.py:929
  475.6 3.8 finish.1
  (328 shorter events, 51.2 us)
Async XLA Ops:
  2.1 104.7 %copy-start.43 = (f32[2,160]{1,0:T(2,128)}, f32[2,160]{1,0:T(2,128)S(1)}, u32[]{:S(2)}) copy-start(f32[2,160]{1,0:T(2,128)S(1)} %compare_convert_fusion) | copy-start | bytes 3844
  108.6 20.7 %copy-start.65 = (f32[512]{0:T(512)}, f32[512]{0:T(512)S(1)}, u32[]{:S(2)}) copy-start(f32[512]{0:T(512)S(1)} %get-tuple-element.266) | copy-start | bytes 6148
  108.6 20.7 %copy-start.88 = (f32[512]{0:T(512)}, f32[512]{0:T(512)S(1)}, u32[]{:S(2)}) copy-start(f32[512]{0:T(512)S(1)} %get-tuple-element.265) | copy-start | bytes 6148
  108.6 28.1 %copy-start.57 = (f32[512]{0:T(512)}, f32[512]{0:T(512)S(1)}, u32[]{:S(2)}) copy-start(f32[512]{0:T(512)S(1)} %get-tuple-element.261) | copy-start | bytes 6148
  108.7 15.2 %copy-start.77 = (f32[768]{0:T(1024)}, f32[768]{0:T(1024)S(1)}, u32[]{:S(2)}) copy-start(f32[768]{0:T(1024)S(1)} %get-tuple-element.269) | copy-start | bytes 9220
  108.7 15.2 %copy-start.97 = (f32[768]{0:T(1024)}, f32[768]{0:T(1024)S(1)}, u32[]{:S(2)}) copy-start(f32[768]{0:T(1024)S(1)} %get-tuple-element.270) | copy-start | bytes 9220
  159.1 12.9 %copy-start.34 = (f32[1024]{0:T(1024)S(1)}, f32[1024]{0:T(1024)}, u32[]{:S(2)}) copy-start(f32[1024]{0:T(1024)} %copy-done.33) | copy-start | bytes 12292
  159.1 12.9 %copy-start.40 = (f32[1024]{0:T(1024)S(1)}, f32[1024]{0:T(1024)}, u32[]{:S(2)}) copy-start(f32[1024]{0:T(1024)} %copy-done.39) | copy-start | bytes 12292
  159.1 12.9 %copy-start.58 = (f32[512]{0:T(512)S(1)}, f32[512]{0:T(512)}, u32[]{:S(2)}) copy-start(f32[512]{0:T(512)} %copy-done.57) | copy-start | bytes 6148
  180.7 13.3 %copy-start.13 = (f32[2,512,512]{2,1,0:T(8,128)S(1)}, f32[2,512,512]{2,1,0:T(8,128)}, u32[]{:S(2)}) copy-start(f32[2,512,512]{2,1,0:T(8,128)} %copy-done.12) | copy-start | bytes 6291460
  180.7 13.3 %copy-start.66 = (f32[512]{0:T(512)S(1)}, f32[512]{0:T(512)}, u32[]{:S(2)}) copy-start(f32[512]{0:T(512)} %copy-done.65) | copy-start | bytes 6148
  180.8 13.3 %copy-start.81 = (f32[1,4,2,128]{3,1,2,0:T(4,128)S(1)}, f32[1,4,2,128]{3,1,2,0:T(4,128)}, u32[]{:S(2)}) copy-start(f32[1,4,2,128]{3,1,2,0:T(4,128)} %copy.65) | copy-start | bytes 12292
  180.8 13.3 %copy-start.82 = (f32[1024]{0:T(1024)S(1)}, f32[1024]{0:T(1024)}, u32[]{:S(2)}) copy-start(f32[1024]{0:T(1024)} %rsqrt.69) | copy-start | bytes 12292
  180.8 13.3 %copy-start.89 = (f32[512]{0:T(512)S(1)}, f32[512]{0:T(512)}, u32[]{:S(2)}) copy-start(f32[512]{0:T(512)} %copy-done.88) | copy-start | bytes 6148
  180.8 13.2 %copy-start.105 = (bf16[2,2,2,2,32,1536]{5,4,3,2,1,0:T(8,128)(2,1)S(1)}, bf16[2,2,2,2,32,1536]{5,4,3,2,1,0:T(8,128)(2,1)}, u32[]{:S(2)}) copy-start(bf16[2,2,2,2,32,1536]{5,4,3,2,1,0:T(8,128)(2,1)} %get-tuple-element.126) | copy-start | bytes 4718596
  206.6 12.8 %copy-start.17 = (f32[320,768]{1,0:T(8,128)S(1)}, f32[320,768]{1,0:T(8,128)}, u32[]{:S(2)}) copy-start(f32[320,768]{1,0:T(8,128)} %copy-done.16) | copy-start | bytes 2949124
  206.6 12.8 %copy-start.36 = (f32[768]{0:T(1024)S(1)}, f32[768]{0:T(1024)}, u32[]{:S(2)}) copy-start(f32[768]{0:T(1024)} %copy-done.35) | copy-start | bytes 9220
  206.6 12.8 %copy-start.42 = (f32[320]{0:T(512)S(1)}, f32[320]{0:T(512)}, u32[]{:S(2)}) copy-start(f32[320]{0:T(512)} %copy-done.41) | copy-start | bytes 3844
  206.6 12.8 %copy-start.64 = (f32[320]{0:T(512)S(1)}, f32[320]{0:T(512)}, u32[]{:S(2)}) copy-start(f32[320]{0:T(512)} %copy-done.63) | copy-start | bytes 3844
  206.6 13.2 %copy-start.70 = (f32[320]{0:T(512)S(1)}, f32[320]{0:T(512)}, u32[]{:S(2)}) copy-start(f32[320]{0:T(512)} %copy-done.69) | copy-start | bytes 3844
  434.9 40.0 %copy-start.79 = (f32[16,256]{1,0:T(8,128)S(1)}, f32[16,256]{1,0:T(8,128)}, u32[]{:S(2)}) copy-start(f32[16,256]{1,0:T(8,128)} %get-tuple-element.205) | copy-start | bytes 49156
  434.9 40.1 %copy-start.59 = (f32[1248]{0:T(1024)S(1)}, f32[1248]{0:T(1024)}, u32[]{:S(2)}) copy-start(f32[1248]{0:T(1024)} %param.59) | copy-start | bytes 14980
  434.9 40.1 %copy-start.92 = (f32[1248]{0:T(1024)S(1)}, f32[1248]{0:T(1024)}, u32[]{:S(2)}) copy-start(f32[1248]{0:T(1024)} %param.60) | copy-start | bytes 14980
  434.9 40.0 %copy-start.93 = (f32[1248]{0:T(1024)S(1)}, f32[1248]{0:T(1024)}, u32[]{:S(2)}) copy-start(f32[1248]{0:T(1024)} %param.61) | copy-start | bytes 14980
  (89 other events, 284.6 us)

commit v7 on v5

--- a/solution.py
+++ b/solution.py
@@ -1530,7 +1530,7 @@
 
 def hidden_backward(normed, inner, slope, grad, up, down):
     (tokens, width), units = normed.shape, inner.shape[1]
-    tile = 1024
+    tile = 512
     whole = pl.BlockSpec((tokens, width), lambda step: (0, 0))
     columns = pl.BlockSpec((tokens, tile), lambda step: (0, step))
     up_tile = pl.BlockSpec((width, tile), lambda step: (0, step))

time: 486 us -> 485 us (level)
  no operation moved by 1% of the time
where the time goes in v7:
time: 485 us; the launch traced here: 475 us
  Pallas kernels  390 us (80%)
  matrix products  40.1 us (8%)
  local copies, waits for them, and re-layouts  20.9 us (4%)
  other arithmetic  19.8 us (4%)
    pallas_call x1, Pallas kernels, reduce_rows(): pl.pallas_call(functools.partial(reduce_kernel, levels, pieces, count, ow...  149 us
    pallas_call x1, Pallas kernels, gather_rows(): pl.pallas_call(functools.partial(gather_kernel, levels, pieces, count), o...  99.9 us
    pallas_call x1, Pallas kernels, orthogonalize(): pl.pallas_call(functools.partial(muon_kernel, owners, shapes), out_shape=...  44.2 us
    pallas_call x1, Pallas kernels, return_rows(): pl.pallas_call(functools.partial(return_kernel, owners, count, devices),...  38.5 us
    unnamed x102, local copies, waits for them, and re-layouts  14.7 us
    pallas_call x2, Pallas kernels, local_loss(): decoder_attention(normed, weights[4], pieces[4], pieces[5], jnp.asarray(w...  14.7 us
    pallas_call x1, Pallas kernels, local_loss(): hidden_layer(normed, weights[2], pieces[7], weights[3])  12.6 us
    pallas_call x1, Pallas kernels, local_loss(): hidden_layer(normed, weights[6], pieces[9], weights[7])  11.8 us

profile of v7, /device:TPU:15, one launch (start us, length us, event | category | flops | bytes accessed | tf_op | source)
XLA Modules:
  0.0 475.5 jit_solution(11252787870549875464)
XLA Ops:
  3.8 2.1 reshape.521.refs_12_
  5.8 99.9 %gather_rows.1 = (bf16[2,2,2,2,48,2304]{5,4,3,2,1,0:T(8,128)(2,1)}, bf16[2,2,2,2,48,768]{5,4,3,2,1,0:T(8,128)(2,1)}, bf16[2,2,2,2,48,3072]{5,4,3,2,1,0:T(8,128)(...) custom-call(f32[48,2304]{1,0:T(8,128)} %refs_8_.3, ...), custom_call_target="tpu_custom_call" | custom-call | tf_op jit(solution)/shard_map/gather_rows/pallas_call | solution.py:552
  108.8 1.9 fusion.68
  112.7 3.4 jvp_attention_forward_.2
  117.3 3.7 fusion.8
  121.0 1.8 fusion.70
  124.4 2.4 fusion.71
  129.0 1.8 add_convert_fusion.joined
  130.8 3.5 jvp_attention_forward_.3
  137.4 7.7 %fusion.3 = (f32[1024,2048]{1,0:T(8,128)}, bf16[1024,2048]{1,0:T(8,128)(2,1)S(1)}) fusion(f32[2048]{0:T(1024)S(1)} %slice.179, bf16[1024,512]{1,0:T(8,128)(2,1)S(1)} %add_convert_fusion.3.normed, bf16[512,2048]{1,0:T(8,128)(2,1)S(1)} %bitcast.117), kind=kOutput, calls=%fused_computation.4 | convolution fusion | flops 2170552320 | bytes 15736832 | tf_op jit(solution)/shard_map/jvp()/dot_general | solution.py:1561
  145.1 2.4 fusion.73
  157.1 11.8 %transpose_jvp_hidden_backward__.2 = (f32[1024,512]{1,0:T(8,128)S(1)}, bf16[512,2048]{1,0:T(8,128)(2,1)S(1)}, bf16[2048,512]{1,0:T(8,128)(2,1)S(1)}, f32[8,2048]{1,0:T(8,128)S(1)}) custom-call(bf16[1024,512]{1,0:T(8,128)(2,1)S(1)} %add_convert_fusion.3.normed, bf16[1024,2048]{1,0:T(8,128)(2,1)} %copy-done.24, f32[1024,2048]{1,0:T(8,128)} %get-tuple-element.242.slope, ...), custom_call_target="tpu_custom_call" | custom-call | tf_op jit(solution)/shard_map/transpose(jvp(hidden_backward))/pallas_call | solution.py:1615
  169.0 3.9 multiply_reduce_fusion.2
  177.3 12.0 %transpose_jvp_attention_backward__.2 = (bf16[1024,1536]{1,0:T(8,128)(2,1)S(1)}, f32[8,512]{1,0:T(8,128)S(1)}, f32[8,512]{1,0:T(8,128)S(1)}) custom-call(bf16[1024,1536]{1,0:T(8,128)(2,1)S(1)} %add_convert_fusion.joined, f32[1,4,16,128]{3,2,1,0:T(8,128)S(1)} %copy-done.11, bf16[1024,512]{1,0:T(8,128)(2,1)S(1)} %convolution_convert_fusion.1.grad), custom_call_target="tpu_custom_call" | custom-call | tf_op jit(solution)/shard_map/transpose(jvp(attention_backward))/pallas_call | solution.py:1612
  189.3 2.3 multiply_reduce_fusion.1
  191.6 2.6 transpose_jvp_weight_grad__.3
  201.0 12.6 %transpose_jvp_hidden_backward__.3 = (f32[320,768]{1,0:T(8,128)S(1)}, bf16[768,3072]{1,0:T(8,128)(2,1)S(1)}, bf16[3072,768]{1,0:T(8,128)(2,1)}, f32[8,3072]{1,0:T(8,128)S(1)}) custom-call(bf16[320,768]{1,0:T(8,128)(2,1)S(1)} %add_convert_fusion.7.normed, bf16[320,3072]{1,0:T(8,128)(2,1)S(1)} %copy-done.10, f32[320,3072]{1,0:T(8,128)S(1)} %get-tuple-element.244.slope, ...), custom_call_target="tpu_custom_call" | custom-call | tf_op jit(solution)/shard_map/transpose(jvp(hidden_backward))/pallas_call | solution.py:1602
  217.6 6.1 %transpose_jvp_attention_backward__.3 = (bf16[320,2304]{1,0:T(8,128)(2,1)S(1)}, f32[8,768]{1,0:T(8,128)S(1)}, f32[8,768]{1,0:T(8,128)S(1)}) custom-call(bf16[320,2304]{1,0:T(8,128)(2,1)S(1)} %fusion.4.joined, f32[2,160,160]{2,1,0:T(8,128)S(1)} %broadcast_in_dim.41.allowed, bf16[320,768]{1,0:T(8,128)(2,1)S(1)} %convolution_convert_fusion.4.grad), custom_call_target="tpu_custom_call" | custom-call | tf_op jit(solution)/shard_map/transpose(jvp(attention_backward))/pallas_call | solution.py:1599
  226.6 1.9 convolution_convert_fusion
  230.4 2.8 transpose_jvp_weight_grad__.2
  234.9 148.8 %reduce_rows.1 = (f32[48,2304]{1,0:T(8,128)}, f32[48,768]{1,0:T(8,128)}, f32[48,3072]{1,0:T(8,128)}, f32[192,768]{1,0:T(8,128)}, f32[32,1536]{1,0:T(8,128)}, /*i...) custom-call(bf16[2,2,2,2,48,2304]{5,4,3,2,1,0:T(8,128)(2,1)} %bitcas, ...), custom_call_target="tpu_custom_call" | custom-call | tf_op jit(solution)/shard_map/reduce_rows/pallas_call | solution.py:819
  386.9 44.2 %orthogonalize.1 = (bf16[768,2304]{1,0:T(8,128)(2,1)}, bf16[768,768]{1,0:T(8,128)(2,1)}, bf16[768,3072]{1,0:T(8,128)(2,1)}, bf16[3072,768]{1,0:T(8,128)(2,1)}, b...) custom-call(bf16[768,2304]{1,0:T(8,128)(2,1)} %bitcast.141, ...), custom_call_target="tpu_custom_call" | custom-call | tf_op jit(solution)/shard_map/orthogonalize/pallas_call | solution.py:1159
  431.1 38.5 %return_rows.1 = (bf16[48,2304]{1,0:T(8,128)(2,1)}, bf16[48,768]{1,0:T(8,128)(2,1)}, bf16[48,3072]{1,0:T(8,128)(2,1)}, bf16[192,768]{1,0:T(8,128)(2,1)}, bf16[32...) custom-call(bf16[16,48,2304]{2,1,0:T(8,128)(2,1)} %bitcast.140, ...), custom_call_target="tpu_custom_call" | custom-call | tf_op jit(solution)/shard_map/return_rows/pallas_call | solution.py:925
  470.3 3.8 finish.1
  (204 shorter events, 49.0 us)
Async XLA Ops:
  1.4 4.4 copy-start.31
  110.7 5.3 %copy-start.18 = (f32[320,768]{1,0:T(8,128)}, f32[320,768]{1,0:T(8,128)S(1)}, u32[]{:S(2)}) copy-start(f32[320,768]{1,0:T(8,128)S(1)} %get-tuple-element.284) | copy-start | bytes 2949124
  111.1 6.2 %slice-start = ((s8[4718592]{0:T(1024)(128)(4,1)}), s8[4194304]{0:T(1024)(128)(4,1)S(1)}, s32[]{:S(2)}) async-start(s8[4718592]{0:T(1024)(128)(4,1)} %bitcast.128), calls=%async_computation | async-start | bytes 8388608
  111.3 5.9 %slice-start.1 = ((s8[4718592]{0:T(1024)(128)(4,1)}), s8[524288]{0:T(1024)(128)(4,1)S(1)}, s32[]{:S(2)}) async-start(s8[4718592]{0:T(1024)(128)(4,1)} %bitcast.128), calls=%async_computation.1 | async-start | bytes 1048576
  116.7 4.2 copy-start.16
  117.0 4.0 slice-start.2
  117.3 3.7 slice-start.3
  122.8 4.0 copy-start.25
  126.8 7.5 %copy-start.12 = (f32[2,512,512]{2,1,0:T(8,128)}, f32[2,512,512]{2,1,0:T(8,128)S(1)}, u32[]{:S(2)}) copy-start(f32[2,512,512]{2,1,0:T(8,128)S(1)} %get-tuple-element.290) | copy-start | bytes 6291460
  130.8 3.5 copy-start.27
  135.1 10.0 %copy-start.14 = (f32[1024,512]{1,0:T(8,128)}, f32[1024,512]{1,0:T(8,128)S(1)}, u32[]{:S(2)}) copy-start(f32[1024,512]{1,0:T(8,128)S(1)} %get-tuple-element.292) | copy-start | bytes 6291460
  137.4 7.7 %copy-start.5 = (bf16[2,2,2,2,128,512]{5,4,3,2,1,0:T(8,128)(2,1)S(1)}, bf16[2,2,2,2,128,512]{5,4,3,2,1,0:T(8,128)(2,1)}, u32[]{:S(2)}) copy-start(bf16[2,2,2,2,128,512]{5,4,3,2,1,0:T(8,128)(2,1)} %get-tuple-element.127) | copy-start | bytes 6291460
  168.9 4.0 copy-start.7
  168.9 4.0 copy-start.8
  169.0 4.0 copy-start.15
  177.2 12.1 %copy-start.13 = (f32[2,512,512]{2,1,0:T(8,128)S(1)}, f32[2,512,512]{2,1,0:T(8,128)}, u32[]{:S(2)}) copy-start(f32[2,512,512]{2,1,0:T(8,128)} %copy-done.12) | copy-start | bytes 6291460
  177.3 12.1 %copy-start.40 = (bf16[2,2,2,2,32,1536]{5,4,3,2,1,0:T(8,128)(2,1)S(1)}, bf16[2,2,2,2,32,1536]{5,4,3,2,1,0:T(8,128)(2,1)}, u32[]{:S(2)}) copy-start(bf16[2,2,2,2,32,1536]{5,4,3,2,1,0:T(8,128)(2,1)} %get-tuple-element.124) | copy-start | bytes 4718596
  200.9 12.6 %copy-start.17 = (f32[320,768]{1,0:T(8,128)S(1)}, f32[320,768]{1,0:T(8,128)}, u32[]{:S(2)}) copy-start(f32[320,768]{1,0:T(8,128)} %copy-done.16) | copy-start | bytes 2949124
  217.0 6.7 %copy-start.19 = (f32[320,768]{1,0:T(8,128)S(1)}, f32[320,768]{1,0:T(8,128)}, u32[]{:S(2)}) copy-start(f32[320,768]{1,0:T(8,128)} %copy-done.18) | copy-start | bytes 2949124
  217.0 6.7 %copy-start.38 = (bf16[2,2,2,2,48,2304]{5,4,3,2,1,0:T(8,128)(2,1)S(1)}, bf16[2,2,2,2,48,2304]{5,4,3,2,1,0:T(8,128)(2,1)}, u32[]{:S(2)}) copy-start(bf16[2,2,2,2,48,2304]{5,4,3,2,1,0:T(8,128)(2,1)} %get-tuple-element.119) | copy-start | bytes 10616836
  431.1 38.5 %copy-start.34 = (f32[16,256]{1,0:T(8,128)S(1)}, f32[16,256]{1,0:T(8,128)}, u32[]{:S(2)}) copy-start(f32[16,256]{1,0:T(8,128)} %get-tuple-element.201) | copy-start | bytes 49156
  431.1 38.6 %copy-start.33 = (f32[1248]{0:T(1024)S(1)}, f32[1248]{0:T(1024)}, u32[]{:S(2)}) copy-start(f32[1248]{0:T(1024)} %param.59) | copy-start | bytes 14980
  431.1 38.6 %copy-start.35 = (f32[1248]{0:T(1024)S(1)}, f32[1248]{0:T(1024)}, u32[]{:S(2)}) copy-start(f32[1248]{0:T(1024)} %param.60) | copy-start | bytes 14980
  431.1 38.5 %copy-start.36 = (f32[1248]{0:T(1024)S(1)}, f32[1248]{0:T(1024)}, u32[]{:S(2)}) copy-start(f32[1248]{0:T(1024)} %param.61) | copy-start | bytes 14980
  (24 other events, 43.6 us)
